TPU v7x, 32 devices: a whole 2x2x4 slice. The times are simulated.
32 devices in a mesh: group: 2 (over y), dm: 4 (over z), tm: 2 (over x), beam: 2 (over core).
Axes of the slice: x: 2, y: 2, z: 4, core: 2. Of those that a mesh axis runs over, the one named last changes fastest.
Arguments:
- raw: bfloat16 [16, 4194304], P(('group', 'dm', 'beam'), 'tm'), parts along dimension 0
- proto: float32 [4, 16384], replicated, may hold values from -4 to 4
- delays: int32 [8, 4, 64], replicated, may hold values from 0 to 3, as said below
- widths: int32 [8], replicated, may hold values from 1 to 8, as said below
- owners: int32 [8, 1], replicated, may hold values from 0 to 3; in each aligned block of 8 rows (0 to 7, 8 to 15, ...) at most 4 rows name the same one
Outputs:
- detect: bfloat16 [16, 8, 2, 4, 8, 256], P('dm', 'group', 'beam', None, None, 'tm'), parts along dimension 1
There are 2 independent parts, one for each index of `group`. A program takes and returns all parts, laid end to end along the dimension named above; an argument that names none is the same for every part. Nothing has to cross between parts.
Inputs may be any that keep to these rules, and one draw needn't show every extreme that they name: `delays`: 3 occurs in every draw. `widths`: 8 occurs in every draw. `owners`: each owner holds at most 4 DM blocks, and some owner holds exactly 4.
All inputs are finite; a program needn't handle non-finite values.
Results may differ from a plain program's by a relative error of at most 0.014.
Values may be sent and summed in bfloat16 or wider, within the bound.
No kernel may reach another device: no remote copies, remote signals or barrier semaphores. Data moves between devices by JAX's collectives and lax.ppermute only.
A program may use at most 128 MiB of HBM per device.

v0:
```python
import math

import jax
import jax.numpy as jnp
from jax import lax
from jax.sharding import PartitionSpec as P

DFT_A = 128
NBLK = 64
PFB_BLK = 16
FD = 4
TT = 8
MAXT = 3
WMAX = 8


def shifted(value, axis, steps):
    count = lax.axis_size(axis)
    first, last = (max(0, -steps), min(count, count - steps))
    return lax.ppermute(value, axis, [(source, source + steps) for source in range(first, last)])


def dft_tables(size):
    index = jnp.arange(size, dtype=jnp.int32)
    product = index[:, None] * index[None, :] % size
    angle = product.astype(jnp.float32) * (2.0 * math.pi / size)
    return (jnp.cos(angle).astype(jnp.bfloat16), jnp.sin(angle).astype(jnp.bfloat16))


def twiddle_tables(rows, cols, total):
    first = jnp.arange(rows, dtype=jnp.int32)
    second = jnp.arange(cols, dtype=jnp.int32)
    product = first[:, None] * second[None, :] % total
    angle = product.astype(jnp.float32) * (2.0 * math.pi / total)
    return (jnp.cos(angle), jnp.sin(angle))


def spectra_power(window_frames, proto):
    taps, channels = proto.shape
    beams_here = window_frames.shape[0]
    count = window_frames.shape[1] - taps + 1
    side_b = channels // DFT_A
    acc = window_frames[:, 0:count].astype(jnp.float32) * proto[0]
    for tap in range(1, taps):
        acc = acc + window_frames[:, tap : tap + count].astype(jnp.float32) * proto[tap]
    frames_bf = acc.astype(jnp.bfloat16).reshape(beams_here * count, DFT_A, side_b)
    cos_a, sin_a = dft_tables(DFT_A)
    cos_b, sin_b = dft_tables(side_b)
    tw_cos, tw_sin = twiddle_tables(side_b, DFT_A, channels)
    a_re = jnp.einsum("kab,fa->kbf", frames_bf, cos_a, preferred_element_type=jnp.float32)
    a_im = -jnp.einsum("kab,fa->kbf", frames_bf, sin_a, preferred_element_type=jnp.float32)
    t_re = (a_re * tw_cos + a_im * tw_sin).astype(jnp.bfloat16)
    t_im = (a_im * tw_cos - a_re * tw_sin).astype(jnp.bfloat16)
    c_re = jnp.einsum("kbf,gb->kgf", t_re, cos_b, preferred_element_type=jnp.float32) + jnp.einsum(
        "kbf,gb->kgf", t_im, sin_b, preferred_element_type=jnp.float32
    )
    c_im = jnp.einsum("kbf,gb->kgf", t_im, cos_b, preferred_element_type=jnp.float32) - jnp.einsum(
        "kbf,gb->kgf", t_re, sin_b, preferred_element_type=jnp.float32
    )
    power = (c_re * c_re + c_im * c_im) * (1.0 / (taps * channels))
    return power.reshape(beams_here, count, channels)


def blocked_power(extended, proto, first, count):
    taps = proto.shape[0]

    def block_power(index):
        start = first + index * PFB_BLK
        window = lax.dynamic_slice_in_dim(extended, start, PFB_BLK + taps - 1, 1)
        return spectra_power(window, proto)

    blocks = lax.map(block_power, jnp.arange(count // PFB_BLK, dtype=jnp.int32))
    beams_here = extended.shape[0]
    return jnp.moveaxis(blocks, 0, 1).reshape(beams_here, count, extended.shape[2])


def fine_masks(groups, width):
    block = jnp.arange(groups, dtype=jnp.int32)[:, None]
    inner = jnp.arange(width, dtype=jnp.int32)[None, :]
    fine = block * FD * (width - 1 - inner) // (groups * (width - 1))
    return jnp.stack([(fine == step).astype(jnp.bfloat16) for step in range(FD)])


def subband_sums(flat_ext, groups, count):
    beams_here, length, channels = flat_ext.shape
    width = channels // NBLK
    view = flat_ext.reshape(beams_here, length, NBLK, width)
    masks = fine_masks(groups, width)
    total = jnp.zeros((beams_here, groups, NBLK, count), jnp.float32)
    for step in range(FD):
        part = view[:, FD - 1 - step : FD - 1 - step + count]
        total = total + jnp.einsum(
            "bkci,gi->bgck", part, masks[step], preferred_element_type=jnp.float32
        )
    return (total * (1.0 / math.sqrt(width))).astype(jnp.bfloat16)


def dedisperse(extended, delays, count):
    length = count + WMAX - 1
    total = 0.0
    for value in range(MAXT + 1):
        start = (MAXT - value) * TT
        window = extended[..., start : start + length]
        mask = (delays == value).astype(jnp.bfloat16)
        total = total + jnp.einsum(
            "rgck,gjc->rgjk", window, mask, preferred_element_type=jnp.float32
        )
    return total * (1.0 / math.sqrt(NBLK))


def boxcar(series, widths, count):
    lags = jnp.arange(WMAX, dtype=jnp.int32)
    weights = (lags[None, :] < widths[:, None]).astype(jnp.float32) / jnp.sqrt(
        widths.astype(jnp.float32)
    )[:, None]
    stacked = jnp.stack(
        [series[..., WMAX - 1 - lag : WMAX - 1 - lag + count] for lag in range(WMAX)], -2
    )
    return jnp.einsum("rgjik,wi->rgjwk", stacked, weights)


def slot_table(owners, owner_count, capacity):
    owner = owners[:, 0]
    groups = owner.shape[0]
    index = jnp.arange(groups, dtype=jnp.int32)
    same = owner[:, None] == owner[None, :]
    earlier = index[None, :] < index[:, None]
    rank = jnp.sum((same & earlier).astype(jnp.int32), 1)
    hit_owner = owner[None, None, :] == jnp.arange(owner_count, dtype=jnp.int32)[:, None, None]
    hit_slot = rank[None, None, :] == jnp.arange(capacity, dtype=jnp.int32)[None, :, None]
    return (hit_owner & hit_slot).astype(jnp.int32)


def shards(raw, proto, delays, widths, owners):
    taps, channels = proto.shape
    beams_here = raw.shape[0]
    spec = raw.shape[1] // channels
    groups = delays.shape[0]
    owner_count = lax.axis_size("dm")
    capacity = 2 * (groups // owner_count)
    halo = MAXT * TT + WMAX - 1
    frames = raw.reshape(beams_here, spec, channels)
    total_spectra = spec * lax.axis_size("tm")
    history = taps - 1 + FD - 1
    before = shifted(frames[:, spec - history :], "tm", 1)
    extended = jnp.concatenate([before, frames], 1)
    early_power = spectra_power(extended[:, 0 : FD - 1 + taps - 1], proto)
    main_power = blocked_power(extended, proto, FD - 1, spec)
    band = lax.psum(jnp.sum(main_power, 1), "tm") / total_spectra
    ratio = jnp.concatenate([early_power, main_power], 1) / (band[:, None, :] + 1e-06)
    flat_ext = (ratio - jnp.mean(ratio, 2, keepdims=True)).astype(jnp.bfloat16)
    sub = subband_sums(flat_ext, groups, spec)
    table = slot_table(owners, owner_count, capacity)
    table_bf = table.astype(jnp.bfloat16)
    packed = jnp.einsum(
        "osg,bgck->obsck", table_bf, sub, preferred_element_type=jnp.float32
    ).astype(jnp.bfloat16)
    received = lax.all_to_all(packed, "dm", split_axis=0, concat_axis=1, tiled=True)[0]
    earlier_sub = shifted(received[..., spec - halo :], "tm", 1)
    owned = jnp.concatenate([earlier_sub, received], -1)
    mine = lax.dynamic_index_in_dim(table, lax.axis_index("dm"), 0, keepdims=False)
    slot_delays = jnp.sum(mine[:, :, None, None] * delays[None], 1)
    series = dedisperse(owned, slot_delays, spec)
    box = boxcar(series, widths, spec).astype(jnp.bfloat16)
    result = jnp.transpose(box, (1, 0, 2, 3, 4))
    return result.reshape(capacity, owner_count, beams_here, result.shape[2], result.shape[3], spec)


def solution(mesh):
    return jax.shard_map(
        shards,
        mesh=mesh,
        in_specs=(P(("group", "dm", "beam"), "tm"), P(), P(), P(), P()),
        out_specs=P("dm", "group", "beam", None, None, "tm"),
        check_vma=False,
    )
```

profile of v0, /device:TPU:0, one launch (start us, length us, event | category | flops | bytes accessed | tf_op | source)
XLA Modules:
  0.0 273.6 jit_solution(5279019373399987779)
XLA Ops:
  6.5 90.0 %reduce.3 = bf16[2097152]{0:T(1024)(128)(2,1)} reduce(bf16[1,2097152]{1,0:T(2,128)(2,1)} %param.7, bf16[]{:T(256)} %constant.179), dimensions={0}, to_apply=%param.7.reduce_sub_computation | reduce | bytes 8388610 | tf_op args[0]
  96.5 7.3 %reshape.370 = bf16[1,128,16384]{2,1,0:T(8,128)(2,1)} reshape(bf16[2097152]{0:T(1024)(128)(2,1)} %reduce.3) | data formatting | bytes 8388608 | tf_op jit(solution)/shard_map/reshape | solution.py:142
  103.9 1.0 slice.160
  104.9 5.0 %collective-permute-start = (bf16[1,6,16384]{2,1,0:T(8,128)(2,1)S(1)}, bf16[1,6,16384]{2,1,0:T(8,128)(2,1)S(1)}, u32[]{:S(2)}, u32[]{:S(2)}) collective-permute-start(bf16[1,6,16384]{2,1,0:T(8,128)(2,1)S(1)} %slice.160), channel_id=1, source_target_pairs={{0,2},{1,3},{4,6},{5,7},{8,10},{9,11},{12,14},{13,15},{16,18},{17,... | collective-permute-start | bytes 589832 | tf_op jit(solution)/shard_map/ppermute | solution.py:20
  110.6 4.6 %collective-permute-done = bf16[1,6,16384]{2,1,0:T(8,128)(2,1)S(1)} collective-permute-done((bf16[1,6,16384]{2,1,0:T(8,128)(2,1)S(1)}, bf16[1,6,16384]{2,1,0:T(8,128)(2,1)S(1)}, u32[]{:S(2)}, u32[]{:S(2)}) %collective-permute-start) | collective-permute-done | bytes 196640 | tf_op jit(solution)/shard_map/ppermute | solution.py:20
  117.6 5.4 %pad_maximum_fusion = bf16[1,134,16384]{2,1,0:T(8,128)(2,1)} fusion(bf16[1,128,16384]{2,1,0:T(8,128)(2,1)} %reshape.370, bf16[1,6,16384]{2,1,0:T(8,128)(2,1)S(1)} %collective-permute-done), kind=kLoop, calls=%fused_computation.68 | loop fusion | flops 8781824 | bytes 8781824 | tf_op jit(solution)/shard_map/concatenate | solution.py:146
  122.9 75.4 %while.13 = (s32[]{:T(128)}, f32[8,1,16,16384]{3,2,1,0:T(8,128)}, s32[8]{0:T(128)S(1)}, bf16[1,134,16384]{2,1,0:T(8,128)(2,1)}, f32[4,16384]{1,0:T(4,128)S(1)}, ...) while((s32[]{:T(128)}, f32[8,1,16,16384]{3,2,1,0:T(8,128)}, ...), condition=%wide.region_3.4_spmd, body=%wide.region_2.3_spmd.sunk | while | flops 411435008 | bytes 22545144 | solution.py:72
  124.4 3.3 %fusion.264 = bf16[2,8,128,128]{3,1,2,0:T(8,128)(2,1)S(1)} fusion(bf16[1,134,16384]{2,1,0:T(8,128)(2,1)} %get-tuple-element.202, s32[]{:T(128)S(6)} %add.420, s32[]{:T(128)S(6)} %add.421, s32[]{:T(128)S(6)} %add.422, s32[]{:T(128)S(6)} %select_n.191, f32[16384]{0:T(1024)S(1)} %bitcast.245, f32[16384]{0:T(1024)S(1)} %bitcast.246, ...), kind=kLoop, calls=%fused_computation.11.clone.1 | loop fusion | flops 3145728 | bytes 2883600 | tf_op jit(solution)/shard_map/while
  128.6 0.7 subtract_convert_fusion.3
  131.5 1.1 constant_dynamic-update-slice_fusion.2
  134.1 3.2 %fusion.264 = bf16[2,8,128,128]{3,1,2,0:T(8,128)(2,1)S(1)} fusion(bf16[1,134,16384]{2,1,0:T(8,128)(2,1)} %get-tuple-element.202, s32[]{:T(128)S(6)} %add.420, s32[]{:T(128)S(6)} %add.421, s32[]{:T(128)S(6)} %add.422, s32[]{:T(128)S(6)} %select_n.191, f32[16384]{0:T(1024)S(1)} %bitcast.245, f32[16384]{0:T(1024)S(1)} %bitcast.246, ...), kind=kLoop, calls=%fused_computation.11.clone.1 | loop fusion | flops 3145728 | bytes 2883600 | tf_op jit(solution)/shard_map/while
  138.2 0.7 subtract_convert_fusion.3
  141.1 1.1 constant_dynamic-update-slice_fusion.2
  143.7 3.0 %fusion.264 = bf16[2,8,128,128]{3,1,2,0:T(8,128)(2,1)S(1)} fusion(bf16[1,134,16384]{2,1,0:T(8,128)(2,1)} %get-tuple-element.202, s32[]{:T(128)S(6)} %add.420, s32[]{:T(128)S(6)} %add.421, s32[]{:T(128)S(6)} %add.422, s32[]{:T(128)S(6)} %select_n.191, f32[16384]{0:T(1024)S(1)} %bitcast.245, f32[16384]{0:T(1024)S(1)} %bitcast.246, ...), kind=kLoop, calls=%fused_computation.11.clone.1 | loop fusion | flops 3145728 | bytes 2883600 | tf_op jit(solution)/shard_map/while
  147.6 0.7 subtract_convert_fusion.3
  150.5 1.1 constant_dynamic-update-slice_fusion.2
  153.1 3.0 %fusion.264 = bf16[2,8,128,128]{3,1,2,0:T(8,128)(2,1)S(1)} fusion(bf16[1,134,16384]{2,1,0:T(8,128)(2,1)} %get-tuple-element.202, s32[]{:T(128)S(6)} %add.420, s32[]{:T(128)S(6)} %add.421, s32[]{:T(128)S(6)} %add.422, s32[]{:T(128)S(6)} %select_n.191, f32[16384]{0:T(1024)S(1)} %bitcast.245, f32[16384]{0:T(1024)S(1)} %bitcast.246, ...), kind=kLoop, calls=%fused_computation.11.clone.1 | loop fusion | flops 3145728 | bytes 2883600 | tf_op jit(solution)/shard_map/while
  157.0 0.7 subtract_convert_fusion.3
  159.9 1.1 constant_dynamic-update-slice_fusion.2
  162.5 2.9 %fusion.264 = bf16[2,8,128,128]{3,1,2,0:T(8,128)(2,1)S(1)} fusion(bf16[1,134,16384]{2,1,0:T(8,128)(2,1)} %get-tuple-element.202, s32[]{:T(128)S(6)} %add.420, s32[]{:T(128)S(6)} %add.421, s32[]{:T(128)S(6)} %add.422, s32[]{:T(128)S(6)} %select_n.191, f32[16384]{0:T(1024)S(1)} %bitcast.245, f32[16384]{0:T(1024)S(1)} %bitcast.246, ...), kind=kLoop, calls=%fused_computation.11.clone.1 | loop fusion | flops 3145728 | bytes 2883600 | tf_op jit(solution)/shard_map/while
  166.3 0.7 subtract_convert_fusion.3
  169.2 1.0 constant_dynamic-update-slice_fusion.2
  171.8 3.0 %fusion.264 = bf16[2,8,128,128]{3,1,2,0:T(8,128)(2,1)S(1)} fusion(bf16[1,134,16384]{2,1,0:T(8,128)(2,1)} %get-tuple-element.202, s32[]{:T(128)S(6)} %add.420, s32[]{:T(128)S(6)} %add.421, s32[]{:T(128)S(6)} %add.422, s32[]{:T(128)S(6)} %select_n.191, f32[16384]{0:T(1024)S(1)} %bitcast.245, f32[16384]{0:T(1024)S(1)} %bitcast.246, ...), kind=kLoop, calls=%fused_computation.11.clone.1 | loop fusion | flops 3145728 | bytes 2883600 | tf_op jit(solution)/shard_map/while
  175.7 0.7 subtract_convert_fusion.3
  178.6 1.1 constant_dynamic-update-slice_fusion.2
  181.2 2.9 %fusion.264 = bf16[2,8,128,128]{3,1,2,0:T(8,128)(2,1)S(1)} fusion(bf16[1,134,16384]{2,1,0:T(8,128)(2,1)} %get-tuple-element.202, s32[]{:T(128)S(6)} %add.420, s32[]{:T(128)S(6)} %add.421, s32[]{:T(128)S(6)} %add.422, s32[]{:T(128)S(6)} %select_n.191, f32[16384]{0:T(1024)S(1)} %bitcast.245, f32[16384]{0:T(1024)S(1)} %bitcast.246, ...), kind=kLoop, calls=%fused_computation.11.clone.1 | loop fusion | flops 3145728 | bytes 2883600 | tf_op jit(solution)/shard_map/while
  185.0 0.7 subtract_convert_fusion.3
  188.0 1.1 constant_dynamic-update-slice_fusion.2
  190.5 2.9 %fusion.264 = bf16[2,8,128,128]{3,1,2,0:T(8,128)(2,1)S(1)} fusion(bf16[1,134,16384]{2,1,0:T(8,128)(2,1)} %get-tuple-element.202, s32[]{:T(128)S(6)} %add.420, s32[]{:T(128)S(6)} %add.421, s32[]{:T(128)S(6)} %add.422, s32[]{:T(128)S(6)} %select_n.191, f32[16384]{0:T(1024)S(1)} %bitcast.245, f32[16384]{0:T(1024)S(1)} %bitcast.246, ...), kind=kLoop, calls=%fused_computation.11.clone.1 | loop fusion | flops 3145728 | bytes 2883600 | tf_op jit(solution)/shard_map/while
  194.3 0.7 subtract_convert_fusion.3
  197.2 1.1 constant_dynamic-update-slice_fusion.2
  198.3 4.5 %reduce_sum.40 = f32[16384]{0:T(1024)} reduce(f32[8,1,16,16384]{3,2,1,0:T(8,128)} %get-tuple-element.95, f32[]{:T(128)} %constant.170.clone.1), dimensions={0,1,2}, to_apply=%region_4.5 | reduce | flops 2080768 | bytes 8454148 | tf_op jit(solution)/shard_map/reduce_sum | solution.py:149
  203.5 6.0 %copy.62 = f32[16,8,64,256]{3,2,1,0:T(8,128)S(1)} copy(f32[16,8,64,256]{3,1,2,0:T(8,128)} %bitcast.241) | data formatting | bytes 16777216
  209.5 8.1 %copy.45 = f32[1,128,64,256]{3,1,2,0:T(8,128)} copy(f32[1,128,64,256]{3,2,1,0:T(8,128)S(1)} %bitcast.243) | data formatting | bytes 16777216 | tf_op jit(solution)/shard_map/concatenate | solution.py:150
  217.6 8.4 %all-reduce.2.cloned.1.call-done = f32[1,16384]{1,0:T(1,128)} async-done(((f32[1,16384]{1,0:T(1,128)}), f32[1,16384]{1,0:T(1,128)}) %all-reduce.2.cloned.1.call-update) | async-done | bytes 65552 | tf_op jit(solution)/shard_map/psum | solution.py:149
  226.0 1.1 fusion.221
  227.0 4.2 %fusion.56 = f32[131]{0:T(256)S(1)} fusion(f32[1,128,16384]{2,1,0:T(8,128)} %bitcast.242, f32[1,3,16384]{2,1,0:T(4,128)S(1)} %concatenate.39, f32[16384]{0:T(1024)S(1)} %bitcast.253), kind=kLoop, calls=%fused_computation.67 | loop fusion | flops 6438781 | bytes 8651276 | tf_op jit(solution)/shard_map/reduce_sum | solution.py:151
  231.3 4.8 %fusion.55 = bf16[1,131,64,256]{3,1,2,0:T(8,128)(2,1)S(1)} fusion(f32[1,128,64,256]{3,1,2,0:T(8,128)} %copy.45, f32[1,3,64,256]{3,1,2,0:T(4,128)S(1)} %copy.44, f32[131]{0:T(256)S(1)} %broadcast_multiply_fusion, f32[64,256]{1,0:T(8,128)S(1)} %add.239), kind=kLoop, calls=%fused_computation.65 | loop fusion | flops 8585216 | bytes 12943884 | tf_op jit(solution)/shard_map/convert_element_type | solution.py:151
  236.1 1.2 fusion.59
  237.3 1.2 fusion.65
  238.5 1.2 fusion.64
  239.7 3.6 %fusion.61 = bf16[4,1,4,64,128]{4,2,0,3,1:T(4,128)(2,1)S(1)} fusion(f32[8,128,64]{1,0,2:T(8,128)S(1)} %fusion.64, bf16[1,131,64,256]{3,1,2,0:T(8,128)(2,1)} %copy-done, s32[256]{0:T(256)S(1)} %iota_subtract_fusion, s32[8]{0:T(128)S(1)} %iota_multiply_fusion.2, pred[4,8]{1,0:T(4,128)(4,1)S(1)} %get-tuple-element.124, pred[4,8]{1,0:T(4,128)(4,1)S(1)} %get-tuple-element.125), kind=kOutput, calls=%fused_computation.78 | convolution fusion | flops 36000128 | bytes 4719712 | tf_op jit(solution)/shard_map/osg,bgck->obsck/dot_general | solution.py:155
  243.3 0.8 copy.46
  244.1 4.6 %all-to-all-start = ((bf16[4,1,4,64,128]{4,2,3,1,0:T(4,128)(2,1)}), bf16[4,1,4,64,128]{4,2,3,1,0:T(4,128)(2,1)S(1)}, u32[]{:S(2)}, u32[]{:S(2)}) async-start(bf16[4,1,4,64,128]{4,2,3,1,0:T(4,128)(2,1)} %copy.46), calls=%async_computation | async-start | bytes 524288 | tf_op jit(solution)/shard_map/all_to_all | solution.py:158
  248.8 8.4 %all-to-all-done = bf16[4,1,4,64,128]{4,2,3,1,0:T(4,128)(2,1)S(1)} async-done(((bf16[4,1,4,64,128]{4,2,3,1,0:T(4,128)(2,1)}), bf16[4,1,4,64,128]{4,2,3,1,0:T(4,128)(2,1)S(1)}, u32[]{:S(2)}, u32[]{:S(2)}) %all-to-all-start) | async-done | bytes 262176 | tf_op jit(solution)/shard_map/all_to_all | solution.py:158
  257.4 2.5 collective-permute-start.1
  259.9 3.8 %collective-permute-done.1 = bf16[4,4,64,31]{3,2,0,1:T(8,128)(2,1)S(1)} collective-permute-done((bf16[4,4,64,31]{3,2,0,1:T(8,128)(2,1)S(1)}, bf16[4,4,64,31]{3,2,0,1:T(8,128)(2,1)S(1)}, u32[]{:S(2)}, u32[]{:S(2)}) %collective-permute-start.1) | collective-permute-done | bytes 63520 | tf_op jit(solution)/shard_map/ppermute | solution.py:20
  266.1 0.7 copy.49
  (132 shorter events, 37.9 us)
Async XLA Ops:
  6.5 103.7 %copy-start.1 = (f32[4,16384]{1,0:T(4,128)S(1)}, f32[4,16384]{1,0:T(4,128)}, u32[]{:S(2)}) copy-start(f32[4,16384]{1,0:T(4,128)} %param.8) | copy-start | bytes 786436
  6.5 103.9 %copy-start.4 = (s32[8,1]{0,1:T(1,128)S(1)}, s32[8,1]{0,1:T(1,128)}, u32[]{:S(2)}) copy-start(s32[8,1]{0,1:T(1,128)} %param.11) | copy-start | bytes 100
  6.5 219.4 %all-reduce.2.cloned.1.call-start = ((), (), s32[]{:S(2)}) async-start(), calls=%async_computation.1 | async-start | bytes 131072 | tf_op jit(solution)/shard_map/psum | solution.py:149
  104.9 10.4 %collective-permute-start = (bf16[1,6,16384]{2,1,0:T(8,128)(2,1)S(1)}, bf16[1,6,16384]{2,1,0:T(8,128)(2,1)S(1)}, u32[]{:S(2)}, u32[]{:S(2)}) collective-permute-start(bf16[1,6,16384]{2,1,0:T(8,128)(2,1)S(1)} %slice.160), channel_id=1, source_target_pairs={{0,2},{1,3},{4,6},{5,7},{8,10},{9,11},{12,14},{13,15},{16,18},{17,... | collective-permute-start | bytes 589832 | tf_op jit(solution)/shard_map/ppermute | solution.py:20
  236.1 2.4 copy-start
  238.5 10.2 %copy-start.2 = (s32[8,4,64]{2,1,0:T(4,128)S(1)}, s32[8,4,64]{2,1,0:T(4,128)}, u32[]{:S(2)}) copy-start(s32[8,4,64]{2,1,0:T(4,128)} %param.9) | copy-start | bytes 24580
  238.5 10.2 %copy-start.3 = (s32[8]{0:T(128)S(1)}, s32[8]{0:T(128)}, u32[]{:S(2)}) copy-start(s32[8]{0:T(128)} %param.10) | copy-start | bytes 100
  244.1 13.0 %all-to-all-start = ((bf16[4,1,4,64,128]{4,2,3,1,0:T(4,128)(2,1)}), bf16[4,1,4,64,128]{4,2,3,1,0:T(4,128)(2,1)S(1)}, u32[]{:S(2)}, u32[]{:S(2)}) async-start(bf16[4,1,4,64,128]{4,2,3,1,0:T(4,128)(2,1)} %copy.46), calls=%async_computation | async-start | bytes 524288 | tf_op jit(solution)/shard_map/all_to_all | solution.py:158
  257.4 6.3 %collective-permute-start.1 = (bf16[4,4,64,31]{3,2,0,1:T(8,128)(2,1)S(1)}, bf16[4,4,64,31]{3,2,0,1:T(8,128)(2,1)S(1)}, u32[]{:S(2)}, u32[]{:S(2)}) collective-permute-start(bf16[4,4,64,31]{3,2,0,1:T(8,128)(2,1)S(1)} %slice.169), channel_id=1, source_target_pairs={{0,2},{1,3},{4,6},{5,7},{8,10},{9,11},{12,14},{13,15},{16,18},{17,... | collective-permute-start | bytes 190472 | tf_op jit(solution)/shard_map/ppermute | solution.py:20
Sparse Core Ops, SparseCore 0:
  202.9 22.9 all-reduce.1
where the time goes:
time: 274 us
  other arithmetic  137 us (50%)
  local copies, waits for them, and re-layouts  42.6 us (16%)
  matrix products  37.3 us (14%)
  waiting for transfers between devices  25.2 us (9%)
  between operations  13.6 us (5%)
  starting transfers between devices  12.1 us (4%)
  loops' own time  5.67 us (2%)
    unnamed x2, other arithmetic  90.3 us
    while x8, other arithmetic  24.1 us
    dynamic_update_slice x8, local copies, waits for them, and re-layouts, blocked_power(): blocks = lax.map(block_power, jnp.arange(count // PFB_BLK, dtype=jnp.int32))  8.56 us
    psum x1, waiting for transfers between devices, shards(): band = lax.psum(jnp.sum(main_power, 1), 'tm') / total_spectra  8.4 us
    ppermute x2, waiting for transfers between devices, shifted(): lax.ppermute(value, axis, [(source, source + steps) for source in range(f...  8.39 us
    all_to_all x1, waiting for transfers between devices, shards(): lax.all_to_all(packed, 'dm', split_axis=0, concat_axis=1, tiled=True)[0]  8.38 us
    concatenate x4, local copies, waits for them, and re-layouts, shards(): jnp.concatenate([early_power, main_power], 1) / (band[:, None, :] + 1e-06)  8.35 us
    ppermute x2, starting transfers between devices, shifted(): lax.ppermute(value, axis, [(source, source + steps) for source in range(f...  7.52 us
  transfers between devices with their start and end apart: 4, of which 4 were waited for; matrix products, arithmetic and copies ran while one was open for 6% of the time, Pallas kernels for 0%

commit v1 on v0

v1 whole, which is shorter than its diff:
```python
import functools
import math

import jax
import jax.numpy as jnp
import numpy as np
from jax import lax
from jax.experimental import pallas as pl
from jax.experimental.pallas import tpu as pltpu
from jax.sharding import PartitionSpec as P

DFT_A = 128
NBLK = 64
FD = 4
TT = 8
MAXT = 3
WMAX = 8
LANES = 128
CHUNK = 16
LIMIT = 56 * 1024 * 1024


def ceil_to(value, unit):
    return -(-value // unit) * unit


def angle_tables(rows, cols, total):
    product = np.arange(rows)[:, None] * np.arange(cols)[None, :] % total
    angle = product.astype(np.float64) * (2.0 * math.pi / total)
    return np.cos(angle), np.sin(angle)


class Sizes:
    def __init__(self, taps, channels, spec, groups, n_dm, n_tm):
        self.taps, self.channels, self.spec, self.groups = taps, channels, spec, groups
        self.n_dm, self.n_tm = n_dm, n_tm
        self.side = channels // DFT_A
        self.half = DFT_A // 2 + 1
        self.rows = ceil_to(self.half, 8)
        self.rows16 = ceil_to(self.half, 16)
        self.hist = taps - 1
        self.raw_rows = self.hist * DFT_A
        self.bounds = n_tm - 1
        self.msg_rows = self.bounds * self.raw_rows + 2 * self.rows
        self.capacity = 2 * (groups // n_dm)


def dft_constants(z):
    cos_a, sin_a = angle_tables(DFT_A, DFT_A, DFT_A)
    first = np.zeros((2 * z.rows, DFT_A))
    first[: z.half] = cos_a[: z.half]
    first[z.rows : z.rows + z.half] = -sin_a[: z.half]
    tw_cos, tw_sin = np.zeros((2, z.rows, z.side))
    tw_cos[: z.half], tw_sin[: z.half] = angle_tables(z.half, z.side, z.channels)
    cos_b, sin_b = angle_tables(z.side, z.side, z.side)
    second = np.block([[cos_b, -sin_b], [sin_b, cos_b]])
    return (
        jnp.asarray(first, jnp.bfloat16),
        jnp.asarray(np.stack([tw_cos, tw_sin]), jnp.float32),
        jnp.asarray(second, jnp.bfloat16),
    )


def mask_constants(z):
    width = z.channels // NBLK
    fine = np.arange(z.groups)[:, None] * FD * (width - 1 - np.arange(width))[None, :] // (z.groups * (width - 1))
    parities = width // DFT_A
    masks = np.zeros((2, FD, parities, z.groups, z.rows16))
    for step in range(FD):
        for parity in range(parities):
            hit = fine[:, parity * DFT_A : (parity + 1) * DFT_A] == step
            masks[0, step, parity, :, : z.half] = hit[:, : z.half]
            masks[1, step, parity, :, 1 : z.half - 1] = hit[:, : z.half - 1 : -1]
    weight = np.zeros((z.rows, LANES))
    weight[: z.half] = 2.0 / z.channels
    weight[0] = weight[z.half - 1] = 1.0 / z.channels
    expand = np.zeros((NBLK, 2 * z.side))
    lane = np.arange(z.side)
    expand[lane // parities, lane] = 1
    expand[(z.side - 1 - lane) // parities, z.side + lane] = 1
    return (
        jnp.asarray(masks.reshape(-1, z.rows16), jnp.bfloat16),
        jnp.asarray(weight, jnp.float32),
        jnp.asarray(expand, jnp.bfloat16),
    )


def fill_frames(z, load, pr_ref, y_ref, count):
    for block in range(DFT_A // 16):
        rows = pl.ds(block * 16, 16)
        taps = [pr_ref[tap, rows, :] for tap in range(z.taps)]
        window = [load(k, block) for k in range(z.hist)]
        for k in range(count):
            window.append(load(k + z.hist, block))
            acc = window[0] * taps[0]
            for tap in range(1, z.taps):
                acc = acc + window[tap] * taps[tap]
            y_ref[rows, k * LANES : (k + 1) * LANES] = acc.astype(jnp.bfloat16)
            window.pop(0)


def transform(z, y_ref, first_ref, twiddle_ref, second_ref, a_ref, t_ref, count):
    a_ref[...] = jnp.dot(first_ref[...], y_ref[...], preferred_element_type=jnp.float32)
    pad = jnp.zeros((z.rows16 - z.rows, LANES), jnp.float32)
    for k in range(count):
        lanes = slice(k * LANES, (k + 1) * LANES)
        re, im = a_ref[: z.rows, lanes], a_ref[z.rows :, lanes]
        cos, sin = twiddle_ref[0], twiddle_ref[1]
        t_re = re * cos + im * sin
        t_im = im * cos - re * sin
        rows = slice(k * z.rows16, (k + 1) * z.rows16)
        t_ref[rows, :LANES] = jnp.concatenate([t_re, pad]).astype(jnp.bfloat16)
        t_ref[rows, LANES:] = jnp.concatenate([t_im, pad]).astype(jnp.bfloat16)
    c = jnp.dot(t_ref[...], second_ref[...], preferred_element_type=jnp.float32)
    out = []
    for k in range(count):
        part = c[k * z.rows16 : k * z.rows16 + z.rows]
        re, im = part[:, :LANES], part[:, LANES:]
        out.append(re * re + im * im)
    return out


def channelize(z, raw_ref, proto_ref, first_ref, twiddle_ref, second_ref,
               power_ref, pr_ref, band_ref, msg_ref, buf, y_ref, a_ref, t_ref, sems):
    chunks = z.spec // CHUNK
    span = CHUNK * z.channels
    front = z.hist * z.channels
    copies = [
        pltpu.make_async_copy(
            raw_ref.at[:, pl.ds(i * span, span)], buf.at[:, pl.ds(front + i * span, span)], sems.at[i]
        )
        for i in range(chunks)
    ]
    for copy in copies:
        copy.start()
    buf[:, :front] = jnp.zeros((1, front), jnp.bfloat16)
    for tap in range(z.taps):
        pr_ref[tap] = proto_ref[tap : tap + 1, :].reshape(DFT_A, LANES)
    early = lax.axis_index("tm") > 0
    band_ref[...] = jnp.zeros_like(band_ref)

    def step(i, carry):
        pltpu.make_async_copy(
            raw_ref.at[:, pl.ds(0, span)], buf.at[:, pl.ds(front, span)], sems.at[i]
        ).wait()
        base = i * span

        def load(k, block):
            start = pl.multiple_of(base + k * z.channels + block * 16 * LANES, 16 * LANES)
            return buf[:, pl.ds(start, 16 * LANES)].astype(jnp.float32).reshape(16, LANES)

        fill_frames(z, load, pr_ref, y_ref, CHUNK)
        power = transform(z, y_ref, first_ref, twiddle_ref, second_ref, a_ref, t_ref, CHUNK)
        late = power[z.hist]
        for k in range(z.hist + 1, CHUNK):
            late = late + power[k]
        head = power[0]
        for k in range(1, z.hist):
            head = head + power[k]
        skip = jnp.logical_and(i == 0, early)
        band_ref[...] = band_ref[...] + late + jnp.where(skip, 0.0, head)
        for k in range(CHUNK):
            power_ref[i * CHUNK + k] = power[k]
        return carry

    lax.fori_loop(0, chunks, step, 0)

    def spectrum(start):
        start = pl.multiple_of(start, z.channels)
        return buf[:, pl.ds(start, z.channels)].astype(jnp.float32).reshape(DFT_A, LANES).astype(jnp.bfloat16)

    row = 0
    if z.n_tm == 2:
        starts = [jnp.where(early, z.hist, z.spec) * z.channels]
    else:
        starts = [z.spec * z.channels, z.hist * z.channels]
    for start in starts:
        for k in range(z.hist):
            msg_ref[row : row + DFT_A] = spectrum(start + k * z.channels)
            row += DFT_A
    high = band_ref[...].astype(jnp.bfloat16)
    msg_ref[row : row + z.rows] = high
    msg_ref[row + z.rows : row + 2 * z.rows] = (band_ref[...] - high.astype(jnp.float32)).astype(jnp.bfloat16)


def search(z, power_ref, pr_ref, band_ref, own_ref, other_ref, first_ref, twiddle_ref, second_ref,
           masks_ref, weight_ref, expand_ref, delays_ref, owners_ref,
           out_ref, y_ref, a_ref, t_ref, bound_ref, inv_ref, sums_ref, mean_ref, f_ref, g_ref, sub_ref, del_ref):
    me = lax.axis_index("tm")
    groups, spec = z.groups, z.spec
    total = band_ref[...]
    lo = z.bounds * z.raw_rows
    total = total + (
        other_ref[lo : lo + z.rows].astype(jnp.float32) + other_ref[lo + z.rows : lo + 2 * z.rows].astype(jnp.float32)
    )
    swap = jnp.logical_and(me > 0, z.n_tm == 2)
    y_ref[:, z.hist * LANES :] = jnp.zeros((DFT_A, LANES), jnp.bfloat16)
    for b in range(z.bounds):

        def load(k, block, b=b):
            start = b * z.raw_rows + (k % z.hist) * DFT_A + block * 16
            own = own_ref[start : start + 16].astype(jnp.float32)
            other = other_ref[start : start + 16].astype(jnp.float32)
            return jnp.where(swap, other, own) if k < z.hist else jnp.where(swap, own, other)

        fill_frames(z, load, pr_ref, y_ref, z.hist)
        power = transform(z, y_ref, first_ref, twiddle_ref, second_ref, a_ref, t_ref, z.hist)
        for k in range(z.hist):
            total = total + power[k]
            bound_ref[b * z.hist + k] = power[k]
    scale = float(z.taps * z.channels)
    inv_ref[...] = 1.0 / (total * (1.0 / (z.spec * z.n_tm)) + 1e-6 * scale)
    mine = jnp.maximum(me - 1, 0) * z.hist

    def head_power(k):
        return jnp.where(me > 0, bound_ref[mine + k], power_ref[k])

    weighted = weight_ref[...] * inv_ref[...]

    def fold(value):
        value = value * weighted
        return jnp.sum(value.reshape(z.rows // 8, 8, LANES), 0)

    def sum_step(i, carry):
        for k in range(CHUNK):
            at = pl.multiple_of((i * CHUNK + k) * 8, 8)
            sums_ref[pl.ds(at, 8)] = fold(power_ref[i * CHUNK + k])
        return carry

    lax.fori_loop(0, spec // CHUNK, sum_step, 0)
    for k in range(z.hist):
        sums_ref[k * 8 : k * 8 + 8] = fold(head_power(k))
    acc = sums_ref[pl.ds(0, spec, stride=8)]
    for j in range(1, 8):
        acc = acc + sums_ref[pl.ds(j, spec, stride=8)]
    mean_ref[...] = jnp.broadcast_to(jnp.sum(acc, 1, keepdims=True), (spec, LANES))
    gap = (FD - 1) * LANES
    g_ref[:, :gap] = jnp.zeros((g_ref.shape[0], gap), jnp.float32)
    g_ref[:, gap + spec * LANES :] = jnp.zeros((g_ref.shape[0], gap), jnp.float32)
    f_ref[z.rows :] = jnp.zeros((z.rows16 - z.rows, CHUNK * LANES), jnp.float32)

    def flat_step(i, carry):
        for k in range(CHUNK):
            at = i * CHUNK + k
            power = power_ref[at]
            if k < z.hist:
                power = jnp.where(jnp.logical_and(me > 0, i == 0), bound_ref[mine + k], power)
            f_ref[: z.rows, k * LANES : (k + 1) * LANES] = power * inv_ref[...] - mean_ref[pl.ds(at, 1)]
        lanes = pl.ds(pl.multiple_of(gap + i * CHUNK * LANES, LANES), CHUNK * LANES)
        g_ref[:, lanes] = jnp.dot(masks_ref[...], f_ref[...].astype(jnp.bfloat16), preferred_element_type=jnp.float32)
        return carry

    lax.fori_loop(0, spec // CHUNK, flat_step, 0)
    parities = z.channels // NBLK // DFT_A
    lane = lax.broadcasted_iota(jnp.int32, (groups, LANES), 1)
    block = parities * groups

    def sub_step(k, carry):
        for m in range(2):
            acc = None
            for step in range(FD):
                lanes = pl.ds(pl.multiple_of((k + FD - 1 - step) * LANES, LANES), LANES)
                row = (m * FD + step) * block
                part = g_ref[row : row + groups, lanes]
                for parity in range(1, parities):
                    hit = (lane if m == 0 else LANES - 1 - lane) % parities == parity
                    part = jnp.where(hit, g_ref[row + parity * groups : row + (parity + 1) * groups, lanes], part)
                acc = part if acc is None else acc + part
            sub_ref[m, pl.ds(pl.multiple_of(k * groups, 8), groups)] = acc
        return carry

    length = spec + FD - 1
    lax.fori_loop(0, length, sub_step, 0)
    stop = ceil_to(length, 16)
    sub_ref[:, length * groups :] = jnp.zeros((2, (stop - length) * groups, LANES), jnp.float32)
    trials = delays_ref.shape[1]
    out_ref[...] = jnp.zeros_like(out_ref)
    wide = 2 * LANES
    del_ref[...] = jnp.zeros_like(del_ref)
    empty = jnp.zeros((wide - stop, wide), jnp.bfloat16)
    unit = 1.0 / (math.sqrt(z.channels // NBLK) * math.sqrt(NBLK))
    for g in range(groups):
        del_ref[:trials, :NBLK] = delays_ref[g].astype(jnp.float32)
        spread = jnp.dot(del_ref[:, :NBLK].astype(jnp.bfloat16), expand_ref[...], preferred_element_type=jnp.float32)
        hits = jnp.concatenate([jnp.where(spread == value, unit, 0.0) for value in range(MAXT + 1)])
        both = [sub_ref[m, pl.ds(g, stop, stride=groups)].astype(jnp.bfloat16) for m in range(2)]
        series = jnp.concatenate([jnp.concatenate(both, 1), empty])
        found = lax.dot_general(
            hits.astype(jnp.bfloat16), series, (((1,), (1,)), ((), ())), preferred_element_type=jnp.float32
        )
        dd = found[:8]
        for value in range(1, MAXT + 1):
            dd = dd + pltpu.roll(found[value * 8 : value * 8 + 8], value * TT, 1)
        owner = owners_ref[g, 0]
        rank = jnp.int32(0)
        for earlier in range(g):
            rank = rank + jnp.where(owners_ref[earlier, 0] == owner, 1, 0)
        out_ref[owner * z.n_tm + me, rank] = dd[:trials, :LANES]
        late = pltpu.roll(dd, wide - (spec - WMAX + 1), 1)

        @pl.when(me + 1 < z.n_tm)
        def _(late=late, owner=owner, rank=rank):
            out_ref[owner * z.n_tm + me + 1, rank] = late[:trials, :LANES]


def boxes(z, recv_ref, widths_ref, out_ref, d_ref):
    me = lax.axis_index("tm")
    trials = recv_ref.shape[2]
    rank = lax.broadcasted_iota(jnp.int32, (8, LANES), 0)
    count = widths_ref.shape[0]
    width = jnp.zeros((8, LANES), jnp.int32)
    for w in range(count):
        width = jnp.where(rank == w, widths_ref[w], width)
    norm = 1.0 / jnp.sqrt(width.astype(jnp.float32))
    weights = [jnp.where(width > lag, norm, 0.0) for lag in range(WMAX)]
    prior = WMAX - 1
    zero = jnp.zeros((8, LANES), jnp.float32)
    before = jnp.maximum(me - 1, 0)
    rows = z.capacity * trials
    for d in range(z.n_dm):
        own = recv_ref[d * z.n_tm + me].reshape(rows, LANES)
        past = recv_ref[d * z.n_tm + before].reshape(rows, LANES)
        past = jnp.where(me > 0, past, 0.0)
        wide = jnp.concatenate([own, jnp.zeros_like(own)], 1)
        wide = pltpu.roll(wide, prior, 1) + jnp.concatenate([past, jnp.zeros_like(past)], 1)
        for lag in range(WMAX):
            shift = prior - lag
            d_ref[lag] = (pltpu.roll(wide, 2 * LANES - shift, 1) if shift else wide)[:, :LANES]
        for s in range(z.capacity):
            for j in range(trials):
                acc = None
                for lag in range(WMAX):
                    part = d_ref[lag, s * trials + j : s * trials + j + 1, :] * weights[lag]
                    acc = part if acc is None else acc + part
                out_ref[s, d, 0, j] = acc[:count].astype(jnp.bfloat16)


def vmem_spec():
    return pl.BlockSpec(memory_space=pltpu.VMEM)


def smem_spec():
    return pl.BlockSpec(memory_space=pltpu.SMEM)


def shards(n_dm, n_tm, raw, proto, delays, widths, owners):
    taps, channels = proto.shape
    groups, trials, _ = delays.shape
    z = Sizes(taps, channels, raw.shape[1] // channels, groups, n_dm, n_tm)
    first, twiddle, second = dft_constants(z)
    masks, weight, expand = mask_constants(z)
    params = pltpu.CompilerParams(vmem_limit_bytes=LIMIT)
    own_rows = z.raw_rows * (1 if n_tm == 2 else 2) + 2 * z.rows
    f32, bf16 = jnp.float32, jnp.bfloat16
    power, pr, band, msg = pl.pallas_call(
        functools.partial(channelize, z),
        out_shape=(
            jax.ShapeDtypeStruct((z.spec, z.rows, LANES), f32),
            jax.ShapeDtypeStruct((taps, DFT_A, LANES), f32),
            jax.ShapeDtypeStruct((z.rows, LANES), f32),
            jax.ShapeDtypeStruct((own_rows, LANES), bf16),
        ),
        in_specs=[pl.BlockSpec(memory_space=pl.ANY)] + [vmem_spec()] * 4,
        out_specs=[vmem_spec()] * 4,
        scratch_shapes=[
            pltpu.VMEM((1, (z.spec + z.hist) * channels), bf16),
            pltpu.VMEM((DFT_A, CHUNK * LANES), bf16),
            pltpu.VMEM((2 * z.rows, CHUNK * LANES), f32),
            pltpu.VMEM((CHUNK * z.rows16, 2 * LANES), bf16),
            pltpu.SemaphoreType.DMA((z.spec // CHUNK,)),
        ],
        compiler_params=params,
        name="channelize",
    )(raw, proto, first, twiddle, second)
    if n_tm == 2:
        own, other = msg, lax.ppermute(msg, "tm", [(0, 1), (1, 0)])
    else:
        every = lax.all_gather(msg, "tm")
        lasts = every[:-1, : z.raw_rows].reshape(-1, LANES)
        firsts = every[1:, z.raw_rows : 2 * z.raw_rows].reshape(-1, LANES)
        parts = every[:, 2 * z.raw_rows :].astype(f32).reshape(n_tm, 2, z.rows, LANES)
        rest = jnp.sum(parts, (0, 1)) - band
        high = rest.astype(bf16)
        pair = jnp.concatenate([high, (rest - high.astype(f32)).astype(bf16)])
        own, other = jnp.concatenate([lasts, pair]), jnp.concatenate([firsts, pair])
    length = ceil_to(z.spec + FD - 1, 16)
    out = pl.pallas_call(
        functools.partial(search, z),
        out_shape=jax.ShapeDtypeStruct((n_dm * n_tm, z.capacity, trials, LANES), f32),
        in_specs=[vmem_spec()] * 12 + [smem_spec()],
        out_specs=vmem_spec(),
        scratch_shapes=[
            pltpu.VMEM((DFT_A, (z.hist + 1) * LANES), bf16),
            pltpu.VMEM((2 * z.rows, (z.hist + 1) * LANES), f32),
            pltpu.VMEM((z.hist * z.rows16, 2 * LANES), bf16),
            pltpu.VMEM((z.bounds * z.hist, z.rows, LANES), f32),
            pltpu.VMEM((z.rows, LANES), f32),
            pltpu.VMEM((z.spec * 8, LANES), f32),
            pltpu.VMEM((z.spec, LANES), f32),
            pltpu.VMEM((z.rows16, CHUNK * LANES), f32),
            pltpu.VMEM((masks.shape[0], (z.spec + 2 * (FD - 1)) * LANES), f32),
            pltpu.VMEM((2, length * groups, LANES), f32),
            pltpu.VMEM((8, LANES), f32),
        ],
        compiler_params=params,
        name="search",
    )(power, pr, band, own, other, first, twiddle, second, masks, weight, expand, delays, owners)
    recv = lax.all_to_all(out, ("dm", "tm"), split_axis=0, concat_axis=0, tiled=True)
    return pl.pallas_call(
        functools.partial(boxes, z),
        out_shape=jax.ShapeDtypeStruct((z.capacity, n_dm, 1, trials, widths.shape[0], z.spec), bf16),
        in_specs=[vmem_spec(), smem_spec()],
        out_specs=vmem_spec(),
        scratch_shapes=[pltpu.VMEM((WMAX, z.capacity * trials, LANES), f32)],
        compiler_params=params,
        name="boxes",
    )(recv, widths)


def solution(mesh):
    sizes = dict(mesh.shape)
    return jax.shard_map(
        functools.partial(shards, sizes["dm"], sizes["tm"]),
        mesh=mesh,
        in_specs=(P(("group", "dm", "beam"), "tm"), P(), P(), P(), P()),
        out_specs=P("dm", "group", "beam", None, None, "tm"),
        check_vma=False,
    )
```

time: 274 us -> 46.8 us (0.17)
  other arithmetic: 137 us -> 0 us
  local copies, waits for them, and re-layouts: 42.6 us -> 1.36 us
  matrix products: 37.3 us -> 0 us
  Pallas kernels: 0 us -> 26 us
  waiting for transfers between devices: 25.2 us -> 3.11 us
  between operations: 13.6 us -> 0.01 us
  blocking collectives: 0 us -> 13.1 us
  starting transfers between devices: 12.1 us -> 3.01 us
  loops' own time: 5.67 us -> 0 us
    unnamed x2 -> x0, other arithmetic: 90.3 us -> none
    dot_general x63 -> x0, matrix products: 37.3 us -> none  [the longest x9 5.91 us: spectra_power(): jnp.einsum('kab,fa->kbf', frames_bf, cos_a, preferred_element_type=jnp.fl...]
    pallas_call x0 -> x3, Pallas kernels: none -> 26 us  [the longest x1 12.9 us: shards(): pl.pallas_call(functools.partial(channelize, z), out_shape=(jax.ShapeDtyp...]
    while x8 -> x0, other arithmetic: 24.1 us -> none
    all_to_all x0 -> x1, blocking collectives: none -> 13.1 us  [shards(): lax.all_to_all(out, ('dm', 'tm'), split_axis=0, concat_axis=0, tiled=True)]
    reduce_sum x4 -> x0, other arithmetic: 9 us -> none  [the longest x1 4.48 us: shards(): band = lax.psum(jnp.sum(main_power, 1), 'tm') / total_spectra]
    dynamic_update_slice x8 -> x0, local copies, waits for them, and re-layouts: 8.56 us -> none  [blocked_power(): blocks = lax.map(block_power, jnp.arange(count // PFB_BLK, dtype=jnp.int32))]
    psum x1 -> x0, waiting for transfers between devices: 8.4 us -> none  [shards(): band = lax.psum(jnp.sum(main_power, 1), 'tm') / total_spectra]
  transfers between devices with their start and end apart: 4 -> 1, of which waited for: 4 -> 1; matrix products, arithmetic and copies ran while one was open for 6% -> 1% of each run, Pallas kernels for 0% -> 0%
where the time goes in v1:
time: 46.8 us; the launch traced here: 46.5 us
  Pallas kernels  26 us (56%)
  blocking collectives  13.1 us (28%)
  waiting for transfers between devices  3.11 us (7%)
  starting transfers between devices  3.01 us (6%)
  local copies, waits for them, and re-layouts  1.36 us (3%)
    all_to_all x1, blocking collectives, shards(): lax.all_to_all(out, ('dm', 'tm'), split_axis=0, concat_axis=0, tiled=True)  13.1 us
    pallas_call x1, Pallas kernels, shards(): pl.pallas_call(functools.partial(channelize, z), out_shape=(jax.ShapeDtyp...  12.9 us
    pallas_call x1, Pallas kernels, shards(): pl.pallas_call(functools.partial(search, z), out_shape=jax.ShapeDtypeStru...  11.2 us
    ppermute x1, waiting for transfers between devices, shards(): own, other = (msg, lax.ppermute(msg, 'tm', [(0, 1), (1, 0)]))  3.11 us
    ppermute x1, starting transfers between devices, shards(): own, other = (msg, lax.ppermute(msg, 'tm', [(0, 1), (1, 0)]))  3.01 us
    pallas_call x1, Pallas kernels, shards(): pl.pallas_call(functools.partial(boxes, z), out_shape=jax.ShapeDtypeStruc...  1.86 us
    unnamed x5, local copies, waits for them, and re-layouts  1.36 us
  transfers between devices with their start and end apart: 1, of which 1 were waited for; matrix products, arithmetic and copies ran while one was open for 1% of the time, Pallas kernels for 0%

profile of v1, /device:TPU:0, one launch (start us, length us, event | category | flops | bytes accessed | tf_op | source)
XLA Modules:
  0.0 46.5 jit_solution(7767024491953849034)
XLA Ops:
  0.0 0.0 copy-start.1
  0.0 12.9 %channelize.1 = (f32[128,72,128]{2,1,0:T(8,128)}, f32[4,128,128]{2,1,0:T(8,128)}, f32[72,128]{1,0:T(8,128)}, bf16[528,128]{1,0:T(8,128)(2,1)}) custom-call(bf16[1,2097152]{1,0:T(2,128)(2,1)} %raw_ref.1, f32[4,16384]{1,0:T(4,128)} %proto_ref.1, bf16[144,128]{1,0:T(8,128)(2,1)} %constant.12.clone.first_ref, f32[2,72,128]{2,1,0:T(8,128)} %constant.13.clone.twiddle_ref, ...), custom_call_target="tpu_custom_call" | custom-call | tf_op jit(solution)/shard_map/channelize/pallas_call | solution.py:355
  12.9 3.0 %collective-permute-start = (bf16[528,128]{1,0:T(8,128)(2,1)}, bf16[528,128]{1,0:T(8,128)(2,1)S(1)}, u32[]{:S(2)}, u32[]{:S(2)}) collective-permute-start(bf16[528,128]{1,0:T(8,128)(2,1)} %get-tuple-element.12.own_ref), channel_id=1, source_target_pairs={{0,2},{2,0},{1,3},{3,1},{4,6},{6,4},{5,7},{7,5},{8,10},{10,8},{9,1... | collective-permute-start | bytes 405512 | tf_op jit(solution)/shard_map/ppermute | solution.py:376
  16.0 0.0 copy-done.1
  16.0 0.7 %copy.12.owners_ref = s32[8,1]{1,0:T(8,128)} copy(s32[8,1]{0,1:T(1,128)S(1)} %copy-done.1) | data formatting | bytes 64 | tf_op args[4]
  16.6 3.1 %collective-permute-done.other_ref = bf16[528,128]{1,0:T(8,128)(2,1)S(1)} collective-permute-done((bf16[528,128]{1,0:T(8,128)(2,1)}, bf16[528,128]{1,0:T(8,128)(2,1)S(1)}, u32[]{:S(2)}, u32[]{:S(2)}) %collective-permute-start) | collective-permute-done | bytes 135200 | tf_op jit(solution)/shard_map/ppermute | solution.py:376
  19.7 0.0 copy-start
  19.7 0.7 %copy-done = bf16[528,128]{1,0:T(8,128)(2,1)} copy-done((bf16[528,128]{1,0:T(8,128)(2,1)}, bf16[528,128]{1,0:T(8,128)(2,1)S(1)}, u32[]{:S(2)}) %copy-start) | copy-done | bytes 135192
  20.4 11.2 %search.1 = f32[8,4,4,128]{3,2,1,0:T(4,128)} custom-call(f32[128,72,128]{2,1,0:T(8,128)} %get-tuple-element.9.power_ref, f32[4,128,128]{2,1,0:T(8,128)} %get-tuple-element.10.pr_ref, f32[72,128]{1,0:T(8,128)} %get-tuple-element.11.band_ref, bf16[528,128]{1,0:T(8,128)(2,1)} %get-tuple-element.12.own_ref, bf16[528,128]{1,0:T(8,128)(2,1)} %copy-done, ...), custom_call_target="tpu_custom_call" | custom-call | tf_op jit(solution)/shard_map/search/pallas_call | solution.py:387
  31.6 13.1 %all_to_all.5.recv_ref = f32[8,4,4,128]{3,2,1,0:T(4,128)} all-to-all(f32[8,4,4,128]{3,2,1,0:T(4,128)} %search.1), channel_id=1, replica_groups=mesh['group'=2,'dm'=4,'tm'=2,'beam'=2] {'dm','tm'}, dimensions={0} | all-to-all | bytes 131072 | tf_op jit(solution)/shard_map/all_to_all | solution.py:408
  44.6 1.9 %boxes.1 = bf16[4,4,1,4,8,128]{5,4,3,2,1,0:T(8,128)(2,1)} custom-call(f32[8,4,4,128]{3,2,1,0:T(4,128)} %all_to_all.5.recv_ref, s32[8]{0:T(128)} %widths_ref.1), custom_call_target="tpu_custom_call" | custom-call | tf_op jit(solution)/shard_map/boxes/pallas_call | solution.py:409
Async XLA Ops:
  0.0 16.0 %copy-start.1 = (s32[8,1]{0,1:T(1,128)S(1)}, s32[8,1]{0,1:T(1,128)}, u32[]{:S(2)}) copy-start(s32[8,1]{0,1:T(1,128)} %param.15) | copy-start | bytes 100
  12.9 6.8 %collective-permute-start = (bf16[528,128]{1,0:T(8,128)(2,1)}, bf16[528,128]{1,0:T(8,128)(2,1)S(1)}, u32[]{:S(2)}, u32[]{:S(2)}) collective-permute-start(bf16[528,128]{1,0:T(8,128)(2,1)} %get-tuple-element.12.own_ref), channel_id=1, source_target_pairs={{0,2},{2,0},{1,3},{3,1},{4,6},{6,4},{5,7},{7,5},{8,10},{10,8},{9,1... | collective-permute-start | bytes 405512 | tf_op jit(solution)/shard_map/ppermute | solution.py:376
  19.7 0.7 %copy-start = (bf16[528,128]{1,0:T(8,128)(2,1)}, bf16[528,128]{1,0:T(8,128)(2,1)S(1)}, u32[]{:S(2)}) copy-start(bf16[528,128]{1,0:T(8,128)(2,1)S(1)} %collective-permute-done.other_ref) | copy-start | bytes 405508

commit v2 on v1

v2 whole, which is shorter than its diff:
```python
import functools
import math

import jax
import jax.numpy as jnp
import numpy as np
from jax import lax
from jax.experimental import pallas as pl
from jax.experimental.pallas import tpu as pltpu
from jax.sharding import PartitionSpec as P

DFT_A = 128
NBLK = 64
FD = 4
TT = 8
MAXT = 3
WMAX = 8
LANES = 128
CHUNK = 16
LIMIT = 32 * 1024 * 1024


def ceil_to(value, unit):
    return -(-value // unit) * unit


def angle_tables(rows, cols, total):
    product = np.arange(rows)[:, None] * np.arange(cols)[None, :] % total
    angle = product.astype(np.float64) * (2.0 * math.pi / total)
    return np.cos(angle), np.sin(angle)


class Sizes:
    def __init__(self, taps, channels, spec, groups, n_dm, n_tm):
        self.taps, self.channels, self.spec, self.groups = taps, channels, spec, groups
        self.n_dm, self.n_tm = n_dm, n_tm
        self.side = channels // DFT_A
        self.half = DFT_A // 2 + 1
        self.rows = ceil_to(self.half, 8)
        self.rows16 = ceil_to(self.half, 16)
        self.hist = taps - 1
        self.raw_rows = self.hist * DFT_A
        self.bounds = n_tm - 1
        self.msg_rows = self.bounds * self.raw_rows + 2 * self.rows
        self.capacity = 2 * (groups // n_dm)


def dft_constants(z):
    cos_a, sin_a = angle_tables(DFT_A, DFT_A, DFT_A)
    first = np.zeros((2 * z.rows, DFT_A))
    first[: z.half] = cos_a[: z.half]
    first[z.rows : z.rows + z.half] = -sin_a[: z.half]
    tw_cos, tw_sin = np.zeros((2, z.rows, z.side))
    tw_cos[: z.half], tw_sin[: z.half] = angle_tables(z.half, z.side, z.channels)
    cos_b, sin_b = angle_tables(z.side, z.side, z.side)
    second = np.block([[cos_b, -sin_b], [sin_b, cos_b]])
    return (
        jnp.asarray(first, jnp.bfloat16),
        jnp.asarray(np.stack([tw_cos, tw_sin]), jnp.float32),
        jnp.asarray(second, jnp.bfloat16),
    )


def mask_constants(z):
    width = z.channels // NBLK
    fine = np.arange(z.groups)[:, None] * FD * (width - 1 - np.arange(width))[None, :] // (z.groups * (width - 1))
    parities = width // DFT_A
    masks = np.zeros((2, FD, parities, z.groups, z.rows16))
    for step in range(FD):
        for parity in range(parities):
            hit = fine[:, parity * DFT_A : (parity + 1) * DFT_A] == step
            masks[0, step, parity, :, : z.half] = hit[:, : z.half]
            masks[1, step, parity, :, 1 : z.half - 1] = hit[:, : z.half - 1 : -1]
    weight = np.zeros((z.rows, LANES))
    weight[: z.half] = 2.0 / z.channels
    weight[0] = weight[z.half - 1] = 1.0 / z.channels
    expand = np.zeros((NBLK, 2 * z.side))
    lane = np.arange(z.side)
    expand[lane // parities, lane] = 1
    expand[(z.side - 1 - lane) // parities, z.side + lane] = 1
    return (
        jnp.asarray(masks.reshape(-1, z.rows16), jnp.bfloat16),
        jnp.asarray(weight, jnp.float32),
        jnp.asarray(expand, jnp.bfloat16),
    )


def fill_frames(z, history, load, pr_ref, y_ref, count, save=None):
    for block in range(DFT_A // 16):
        rows = pl.ds(block * 16, 16)
        taps = [pr_ref[tap, rows, :] for tap in range(z.taps)]
        window = [history(k, block) for k in range(z.hist)]
        for k in range(count):
            window.append(load(k, block))
            acc = window[0] * taps[0]
            for tap in range(1, z.taps):
                acc = acc + window[tap] * taps[tap]
            y_ref[rows, k * LANES : (k + 1) * LANES] = acc.astype(jnp.bfloat16)
            window.pop(0)
        if save is not None:
            for k in range(z.hist):
                save(k, block, window[k])


def transform(z, y_ref, first_ref, twiddle_ref, second_ref, t_refs, count):
    pad = jnp.zeros((z.rows16 - z.rows, LANES), jnp.float32)
    part = count // len(t_refs)
    out = []
    for index, t_ref in enumerate(t_refs):
        for at in range(0, part, 2):
            pair = min(2, part - at)
            lane = (index * part + at) * LANES
            a = jnp.dot(first_ref[...], y_ref[:, lane : lane + pair * LANES], preferred_element_type=jnp.float32)
            for k in range(pair):
                re = a[: z.rows, k * LANES : (k + 1) * LANES]
                im = a[z.rows :, k * LANES : (k + 1) * LANES]
                cos, sin = twiddle_ref[0], twiddle_ref[1]
                t_re = re * cos + im * sin
                t_im = im * cos - re * sin
                rows = slice((at + k) * z.rows16, (at + k + 1) * z.rows16)
                t_ref[rows, :LANES] = jnp.concatenate([t_re, pad]).astype(jnp.bfloat16)
                t_ref[rows, LANES:] = jnp.concatenate([t_im, pad]).astype(jnp.bfloat16)
        c = jnp.dot(t_ref[...], second_ref[...], preferred_element_type=jnp.float32)
        for k in range(part):
            rows = c[k * z.rows16 : k * z.rows16 + z.rows]
            re, im = rows[:, :LANES], rows[:, LANES:]
            out.append(re * re + im * im)
    return out


def channelize(z, raw_ref, proto_ref, first_in, twiddle_in, second_in, masks_in, weight_in, expand_ref, delays_ref, owners_in,
               power_ref, pr_ref, band_ref, msg_ref, first_ref, twiddle_ref, second_ref, masks_ref, weight_ref, hits_ref, owners_ref,
               buf, tap_ref, spread_ref, trial_ref, hist_ref, y0_ref, y1_ref, t0_ref, t1_ref, t2_ref, t3_ref, sems, sides):
    chunks = z.spec // CHUNK
    span = CHUNK * z.channels

    def raw_copy(i):
        part = pl.ds(i * span, span)
        return pltpu.make_async_copy(raw_ref.at[:, part], buf.at[:, part], sems.at[i])

    raw_copy(0).start()
    pairs = [
        (proto_ref, tap_ref), (first_in, first_ref), (twiddle_in, twiddle_ref), (second_in, second_ref),
        (delays_ref, trial_ref), (expand_ref, spread_ref), (masks_in, masks_ref), (weight_in, weight_ref),
    ]
    copies = [pltpu.make_async_copy(source, target, sides.at[i]) for i, (source, target) in enumerate(pairs)]
    copies[0].start()
    for copy in copies[1:]:
        copy.start()
    for i in range(1, chunks):
        raw_copy(i).start()
    hist_ref[...] = jnp.zeros_like(hist_ref)
    band_ref[...] = jnp.zeros_like(band_ref)
    for g in range(z.groups):
        owners_ref[g] = owners_in[g]
    early = lax.axis_index("tm") > 0
    copies[0].wait()
    for tap in range(z.taps):
        pr_ref[tap] = tap_ref[tap : tap + 1, :].reshape(DFT_A, LANES)
    for copy in copies[1:]:
        copy.wait()
    unit = 1.0 / (math.sqrt(z.channels // NBLK) * math.sqrt(NBLK))
    trials = trial_ref.shape[1]
    tall = jnp.concatenate(
        [
            jnp.concatenate([trial_ref[g].astype(jnp.float32), jnp.zeros((8 - trials, NBLK), jnp.float32)])
            for g in range(z.groups)
        ]
    )
    spread = jnp.dot(tall.astype(jnp.bfloat16), spread_ref[...], preferred_element_type=jnp.float32)
    for g in range(z.groups):
        mine = spread[g * 8 : g * 8 + 8]
        hits = jnp.concatenate([jnp.where(mine == value, unit, 0.0) for value in range(MAXT + 1)])
        hits_ref[g] = hits.astype(jnp.bfloat16)

    def frames(i, y_ref):
        base = i * span

        def load(k, block):
            start = pl.multiple_of(base + k * z.channels + block * 16 * LANES, 16 * LANES)
            return buf[:, pl.ds(start, 16 * LANES)].astype(jnp.float32).reshape(16, LANES)

        def history(k, block):
            return hist_ref[k, block * 16 : block * 16 + 16, :]

        def save(k, block, value):
            hist_ref[k, block * 16 : block * 16 + 16, :] = value

        fill_frames(z, history, load, pr_ref, y_ref, CHUNK, save)

    def powers(i, y_ref, t_refs):
        power = transform(z, y_ref, first_ref, twiddle_ref, second_ref, t_refs, CHUNK)
        late = power[z.hist]
        for k in range(z.hist + 1, CHUNK):
            late = late + power[k]
        head = power[0]
        for k in range(1, z.hist):
            head = head + power[k]
        skip = jnp.logical_and(i == 0, early)
        band_ref[...] = band_ref[...] + late + jnp.where(skip, 0.0, head)
        for k in range(CHUNK):
            power_ref[i * CHUNK + k] = power[k]

    def arrived(i):
        raw_copy(i).wait()

    arrived(0)
    frames(0, y0_ref)

    def step(j, carry):
        i = 2 * j
        arrived(i + 1)
        arrived(i + 2)
        frames(i + 1, y1_ref)
        powers(i, y0_ref, [t0_ref, t1_ref])
        frames(i + 2, y0_ref)
        powers(i + 1, y1_ref, [t2_ref, t3_ref])
        return carry

    lax.fori_loop(0, chunks // 2 - 1, step, 0)
    arrived(chunks - 1)
    frames(chunks - 1, y1_ref)
    powers(chunks - 2, y0_ref, [t0_ref, t1_ref])
    powers(chunks - 1, y1_ref, [t2_ref, t3_ref])

    def spectrum(start):
        start = pl.multiple_of(start, z.channels)
        return buf[:, pl.ds(start, z.channels)].astype(jnp.float32).reshape(DFT_A, LANES).astype(jnp.bfloat16)

    row = 0
    tail = (z.spec - z.hist) * z.channels
    starts = [jnp.where(early, 0, tail)] if z.n_tm == 2 else [tail, 0]
    for start in starts:
        for k in range(z.hist):
            msg_ref[row : row + DFT_A] = spectrum(start + k * z.channels)
            row += DFT_A
    high = band_ref[...].astype(jnp.bfloat16)
    msg_ref[row : row + z.rows] = high
    msg_ref[row + z.rows : row + 2 * z.rows] = (band_ref[...] - high.astype(jnp.float32)).astype(jnp.bfloat16)


def search(z, power_ref, pr_ref, band_ref, own_ref, other_ref, first_ref, twiddle_ref, second_ref,
           masks_ref, weight_ref, hits_ref, owners_ref,
           out_ref, y_ref, t_ref, bound_ref, inv_ref, weighted_ref, sums_ref, mean_ref, sub_ref):
    me = lax.axis_index("tm")
    groups, spec = z.groups, z.spec
    chunks = spec // CHUNK
    total = band_ref[...]
    lo = z.bounds * z.raw_rows
    total = total + (
        other_ref[lo : lo + z.rows].astype(jnp.float32) + other_ref[lo + z.rows : lo + 2 * z.rows].astype(jnp.float32)
    )
    swap = jnp.logical_and(me > 0, z.n_tm == 2)
    y_ref[:, z.hist * LANES :] = jnp.zeros((DFT_A, LANES), jnp.bfloat16)
    for b in range(z.bounds):

        def take(k, block, first, b=b):
            start = b * z.raw_rows + k * DFT_A + block * 16
            own = own_ref[start : start + 16].astype(jnp.float32)
            other = other_ref[start : start + 16].astype(jnp.float32)
            return jnp.where(swap, other, own) if first else jnp.where(swap, own, other)

        fill_frames(
            z, lambda k, block: take(k, block, True), lambda k, block: take(k, block, False), pr_ref, y_ref, z.hist
        )
        power = transform(z, y_ref, first_ref, twiddle_ref, second_ref, [t_ref], z.hist)
        for k in range(z.hist):
            total = total + power[k]
            bound_ref[b * z.hist + k] = power[k]
    scale = float(z.taps * z.channels)
    inv_ref[...] = 1.0 / (total * (1.0 / (z.spec * z.n_tm)) + 1e-6 * scale)
    weighted_ref[...] = weight_ref[...] * inv_ref[...]
    mine = jnp.maximum(me - 1, 0) * z.hist

    def power_of(i, k):
        value = power_ref[i * CHUNK + k]
        if k < z.hist:
            value = jnp.where(jnp.logical_and(me > 0, i == 0), bound_ref[mine + k], value)
        return value

    def means(i):
        for k in range(CHUNK):
            value = power_of(i, k) * weighted_ref[...]
            sums_ref[k * 8 : k * 8 + 8] = jnp.sum(value.reshape(z.rows // 8, 8, LANES), 0)
        acc = sums_ref[pl.ds(0, CHUNK, stride=8)]
        for j in range(1, 8):
            acc = acc + sums_ref[pl.ds(j, CHUNK, stride=8)]
        at = pl.multiple_of(i * CHUNK, CHUNK)
        mean_ref[pl.ds(at, CHUNK)] = jnp.broadcast_to(jnp.sum(acc, 1, keepdims=True), (CHUNK, LANES))

    parities = z.channels // NBLK // DFT_A
    lane = lax.broadcasted_iota(jnp.int32, (groups, LANES), 1)
    pad = jnp.zeros((z.rows16 - z.rows, LANES), jnp.float32)

    def picked(m, step, value):
        row = (m * FD + step) * parities * groups
        part = value[row : row + groups]
        for parity in range(1, parities):
            hit = (lane if m == 0 else LANES - 1 - lane) % parities == parity
            part = jnp.where(hit, value[row + parity * groups : row + (parity + 1) * groups], part)
        return part

    def flat_step(i, carry):
        flats = []
        open_sums = [list(carry[m]) for m in range(2)]
        for k in range(CHUNK):
            flat = power_of(i, k) * inv_ref[...] - mean_ref[pl.ds(i * CHUNK + k, 1)]
            flats.append(jnp.concatenate([flat, pad]).astype(jnp.bfloat16))
            if k % 2 == 0:
                continue
            found = jnp.dot(masks_ref[...], jnp.concatenate(flats[-2:], 1), preferred_element_type=jnp.float32)
            for half in range(2):
                value = found[:, half * LANES : (half + 1) * LANES]
                at = pl.multiple_of((i * CHUNK + k - 1 + half) * groups, 8)
                for m in range(2):
                    parts = [picked(m, step, value) for step in range(FD)]
                    sub_ref[m, pl.ds(at, groups)] = open_sums[m][0] + parts[0]
                    later = open_sums[m][1:] + [None]
                    open_sums[m] = [
                        parts[step + 1] if later[step] is None else later[step] + parts[step + 1]
                        for step in range(FD - 1)
                    ]
        means(jnp.minimum(i + 1, chunks - 1))
        return tuple(tuple(value) for value in open_sums)

    means(0)
    empty = jnp.zeros((groups, LANES), jnp.float32)
    carry = lax.fori_loop(0, chunks, flat_step, ((empty,) * (FD - 1),) * 2)
    length = spec + FD - 1
    stop = ceil_to(length, 16)
    for m in range(2):
        for step in range(FD - 1):
            sub_ref[m, (spec + step) * groups : (spec + step + 1) * groups] = carry[m][step]
    sub_ref[:, length * groups :] = jnp.zeros((2, (stop - length) * groups, LANES), jnp.float32)
    trials = out_ref.shape[2]
    out_ref[...] = jnp.zeros_like(out_ref)
    wide = 2 * LANES
    blank = jnp.zeros((wide - stop, wide), jnp.bfloat16)
    for g in range(groups):
        both = [sub_ref[m, pl.ds(g, stop, stride=groups)].astype(jnp.bfloat16) for m in range(2)]
        series = jnp.concatenate([jnp.concatenate(both, 1), blank])
        found = lax.dot_general(hits_ref[g], series, (((1,), (1,)), ((), ())), preferred_element_type=jnp.float32)
        dd = found[:8]
        for value in range(1, MAXT + 1):
            dd = dd + pltpu.roll(found[value * 8 : value * 8 + 8], value * TT, 1)
        owner = owners_ref[g]
        rank = jnp.int32(0)
        for earlier in range(g):
            rank = rank + jnp.where(owners_ref[earlier] == owner, 1, 0)
        late = pltpu.roll(dd, wide - (spec - WMAX + 1), 1)
        out_ref[owner * z.n_tm + jnp.minimum(me + 1, z.n_tm - 1), rank] = late[:trials, :LANES]
        out_ref[owner * z.n_tm + me, rank] = dd[:trials, :LANES]


def boxes(z, recv_ref, widths_ref, out_ref, d_ref):
    me = lax.axis_index("tm")
    trials = recv_ref.shape[2]
    rank = lax.broadcasted_iota(jnp.int32, (8, LANES), 0)
    count = widths_ref.shape[0]
    width = jnp.zeros((8, LANES), jnp.int32)
    for w in range(count):
        width = jnp.where(rank == w, widths_ref[w], width)
    norm = 1.0 / jnp.sqrt(width.astype(jnp.float32))
    weights = [jnp.where(width > lag, norm, 0.0) for lag in range(WMAX)]
    prior = WMAX - 1
    zero = jnp.zeros((8, LANES), jnp.float32)
    before = jnp.maximum(me - 1, 0)
    rows = z.capacity * trials
    for d in range(z.n_dm):
        own = recv_ref[d * z.n_tm + me].reshape(rows, LANES)
        past = recv_ref[d * z.n_tm + before].reshape(rows, LANES)
        past = jnp.where(me > 0, past, 0.0)
        wide = jnp.concatenate([own, jnp.zeros_like(own)], 1)
        wide = pltpu.roll(wide, prior, 1) + jnp.concatenate([past, jnp.zeros_like(past)], 1)
        for lag in range(WMAX):
            shift = prior - lag
            d_ref[lag] = (pltpu.roll(wide, 2 * LANES - shift, 1) if shift else wide)[:, :LANES]
        for s in range(z.capacity):
            for j in range(trials):
                acc = None
                for lag in range(WMAX):
                    part = d_ref[lag, s * trials + j : s * trials + j + 1, :] * weights[lag]
                    acc = part if acc is None else acc + part
                out_ref[s, d, 0, j] = acc[:count].astype(jnp.bfloat16)


def vmem_spec():
    return pl.BlockSpec(memory_space=pltpu.VMEM)


def smem_spec():
    return pl.BlockSpec(memory_space=pltpu.SMEM)


def any_spec():
    return pl.BlockSpec(memory_space=pl.ANY)


def kept(*values):
    return [pltpu.with_memory_space_constraint(value, pltpu.VMEM) for value in values]


def shards(n_dm, n_tm, raw, proto, delays, widths, owners):
    taps, channels = proto.shape
    groups, trials, _ = delays.shape
    z = Sizes(taps, channels, raw.shape[1] // channels, groups, n_dm, n_tm)
    first, twiddle, second = dft_constants(z)
    masks, weight, expand = mask_constants(z)
    params = pltpu.CompilerParams(vmem_limit_bytes=LIMIT)
    own_rows = z.raw_rows * (1 if n_tm == 2 else 2) + 2 * z.rows
    f32, bf16 = jnp.float32, jnp.bfloat16
    chunks = z.spec // CHUNK
    half = CHUNK // 2 * z.rows16
    power, pr, band, msg, first, twiddle, second, masks, weight, hits, owner = pl.pallas_call(
        functools.partial(channelize, z),
        out_shape=(
            pltpu.VMEM((z.spec, z.rows, LANES), f32),
            pltpu.VMEM((taps, DFT_A, LANES), f32),
            pltpu.VMEM((z.rows, LANES), f32),
            pltpu.VMEM((own_rows, LANES), bf16),
            pltpu.VMEM(first.shape, bf16),
            pltpu.VMEM(twiddle.shape, f32),
            pltpu.VMEM(second.shape, bf16),
            pltpu.VMEM(masks.shape, bf16),
            pltpu.VMEM(weight.shape, f32),
            pltpu.VMEM((groups, (MAXT + 1) * 8, 2 * LANES), bf16),
            pltpu.SMEM((groups,), jnp.int32),
        ),
        in_specs=[any_spec()] * 9 + [smem_spec()],
        out_specs=[vmem_spec()] * 10 + [smem_spec()],
        scratch_shapes=[
            pltpu.VMEM((1, z.spec * channels), bf16),
            pltpu.VMEM(proto.shape, f32),
            pltpu.VMEM(expand.shape, bf16),
            pltpu.VMEM(delays.shape, jnp.int32),
            pltpu.VMEM((z.hist, DFT_A, LANES), f32),
            pltpu.VMEM((DFT_A, CHUNK * LANES), bf16),
            pltpu.VMEM((DFT_A, CHUNK * LANES), bf16),
            pltpu.VMEM((half, 2 * LANES), bf16),
            pltpu.VMEM((half, 2 * LANES), bf16),
            pltpu.VMEM((half, 2 * LANES), bf16),
            pltpu.VMEM((half, 2 * LANES), bf16),
            pltpu.SemaphoreType.DMA((chunks,)),
            pltpu.SemaphoreType.DMA((8,)),
        ],
        compiler_params=params,
        name="channelize",
    )(raw, proto, first, twiddle, second, masks, weight, expand, delays, owners.reshape(groups))
    if n_tm == 2:
        own, other = msg, lax.ppermute(msg, "tm", [(0, 1), (1, 0)])
    else:
        every = lax.all_gather(msg, "tm")
        lasts = every[:-1, : z.raw_rows].reshape(-1, LANES)
        firsts = every[1:, z.raw_rows : 2 * z.raw_rows].reshape(-1, LANES)
        parts = every[:, 2 * z.raw_rows :].astype(f32).reshape(n_tm, 2, z.rows, LANES)
        rest = jnp.sum(parts, (0, 1)) - band
        high = rest.astype(bf16)
        pair = jnp.concatenate([high, (rest - high.astype(f32)).astype(bf16)])
        own, other = jnp.concatenate([lasts, pair]), jnp.concatenate([firsts, pair])
    length = ceil_to(z.spec + FD - 1, 16)
    out = pl.pallas_call(
        functools.partial(search, z),
        out_shape=pltpu.VMEM((n_dm * n_tm, z.capacity, trials, LANES), f32),
        in_specs=[vmem_spec()] * 11 + [smem_spec()],
        out_specs=vmem_spec(),
        scratch_shapes=[
            pltpu.VMEM((DFT_A, (z.hist + 1) * LANES), bf16),
            pltpu.VMEM((z.hist * z.rows16, 2 * LANES), bf16),
            pltpu.VMEM((z.bounds * z.hist, z.rows, LANES), f32),
            pltpu.VMEM((z.rows, LANES), f32),
            pltpu.VMEM((z.rows, LANES), f32),
            pltpu.VMEM((CHUNK * 8, LANES), f32),
            pltpu.VMEM((z.spec, LANES), f32),
            pltpu.VMEM((2, length * groups, LANES), f32),
        ],
        compiler_params=params,
        name="search",
    )(
        *kept(power, pr, band, own, other, first, twiddle, second, masks, weight, hits),
        pltpu.with_memory_space_constraint(owner, pltpu.SMEM),
    )
    recv = lax.all_to_all(out, ("dm", "tm"), split_axis=0, concat_axis=0, tiled=True)
    return pl.pallas_call(
        functools.partial(boxes, z),
        out_shape=jax.ShapeDtypeStruct((z.capacity, n_dm, 1, trials, widths.shape[0], z.spec), bf16),
        in_specs=[vmem_spec(), smem_spec()],
        out_specs=vmem_spec(),
        scratch_shapes=[pltpu.VMEM((WMAX, z.capacity * trials, LANES), f32)],
        compiler_params=params,
        name="boxes",
    )(*kept(recv), widths)


def solution(mesh):
    sizes = dict(mesh.shape)
    return jax.shard_map(
        functools.partial(shards, sizes["dm"], sizes["tm"]),
        mesh=mesh,
        in_specs=(P(("group", "dm", "beam"), "tm"), P(), P(), P(), P()),
        out_specs=P("dm", "group", "beam", None, None, "tm"),
        check_vma=False,
    )
```

time: 46.8 us -> 46.4 us (level)
  Pallas kernels: 26 us -> 15.8 us
  local copies, waits for them, and re-layouts: 1.36 us -> 10.6 us
    pallas_call x2, Pallas kernels: 24.1 us -> 14.3 us  [the longest x1 10.7 us: shards(): pl.pallas_call(functools.partial(channelize, z), out_shape=(pltpu.VMEM((z...]
    unnamed x5 -> x22, local copies, waits for them, and re-layouts: 1.36 us -> 10.6 us
  transfers between devices with their start and end apart: 1 -> 1, of which waited for: 1 -> 1; matrix products, arithmetic and copies ran while one was open for 1% -> 0% of each run, Pallas kernels for 0% -> 0%
where the time goes in v2:
time: 46.4 us; the launch traced here: 45.8 us
  Pallas kernels  15.8 us (34%)
  blocking collectives  12.8 us (28%)
  local copies, waits for them, and re-layouts  10.6 us (23%)
  waiting for transfers between devices  3.57 us (8%)
  starting transfers between devices  3.02 us (7%)
    all_to_all x1, blocking collectives, shards(): lax.all_to_all(out, ('dm', 'tm'), split_axis=0, concat_axis=0, tiled=True)  12.8 us
    pallas_call x1, Pallas kernels, shards(): pl.pallas_call(functools.partial(channelize, z), out_shape=(pltpu.VMEM((z...  10.7 us
    unnamed x22, local copies, waits for them, and re-layouts  10.6 us
    ppermute x1, waiting for transfers between devices, shards(): own, other = (msg, lax.ppermute(msg, 'tm', [(0, 1), (1, 0)]))  3.57 us
    pallas_call x1, Pallas kernels, shards(): pl.pallas_call(functools.partial(search, z), out_shape=pltpu.VMEM((n_dm *...  3.55 us
    ppermute x1, starting transfers between devices, shards(): own, other = (msg, lax.ppermute(msg, 'tm', [(0, 1), (1, 0)]))  3.02 us
    pallas_call x1, Pallas kernels, shards(): pl.pallas_call(functools.partial(boxes, z), out_shape=jax.ShapeDtypeStruc...  1.56 us
  transfers between devices with their start and end apart: 1, of which 1 were waited for; matrix products, arithmetic and copies ran while one was open for 0% of the time, Pallas kernels for 0%

profile of v2, /device:TPU:0, one launch (start us, length us, event | category | flops | bytes accessed | tf_op | source)
XLA Modules:
  0.0 45.8 jit_solution(2084812363522724227)
XLA Ops:
  0.0 0.0 copy-start.10
  0.0 0.0 copy-start
  0.0 3.4 %copy-done = bf16[1,2097152]{1,0:T(2,128)(2,1)S(1)} copy-done((bf16[1,2097152]{1,0:T(2,128)(2,1)S(1)}, bf16[1,2097152]{1,0:T(2,128)(2,1)}, u32[]{:S(2)}) %copy-start) | copy-done | bytes 4194328
  3.4 0.0 copy-start.1
  3.4 0.9 %copy-done.1 = f32[4,16384]{1,0:T(4,128)S(1)} copy-done((f32[4,16384]{1,0:T(4,128)S(1)}, f32[4,16384]{1,0:T(4,128)}, u32[]{:S(2)}) %copy-start.1) | copy-done | bytes 262168
  4.3 0.0 copy-start.2
  4.4 0.9 %copy-done.2 = bf16[256,256]{1,0:T(8,128)(2,1)S(1)} copy-done((bf16[256,256]{1,0:T(8,128)(2,1)S(1)}, bf16[256,256]{1,0:T(8,128)(2,1)}, u32[]{:S(2)}) %copy-start.2) | copy-done | bytes 131096
  5.3 0.0 copy-start.3
  5.3 0.9 %copy-done.3 = f32[2,72,128]{2,1,0:T(8,128)S(1)} copy-done((f32[2,72,128]{2,1,0:T(8,128)S(1)}, f32[2,72,128]{2,1,0:T(8,128)}, u32[]{:S(2)}) %copy-start.3) | copy-done | bytes 73752
  6.1 0.0 copy-start.4
  6.1 0.8 %copy-done.4 = f32[72,128]{1,0:T(8,128)S(1)} copy-done((f32[72,128]{1,0:T(8,128)S(1)}, f32[72,128]{1,0:T(8,128)}, u32[]{:S(2)}) %copy-start.4) | copy-done | bytes 36888
  6.9 0.0 copy-start.5
  6.9 0.8 %copy-done.5 = bf16[144,128]{1,0:T(8,128)(2,1)S(1)} copy-done((bf16[144,128]{1,0:T(8,128)(2,1)S(1)}, bf16[144,128]{1,0:T(8,128)(2,1)}, u32[]{:S(2)}) %copy-start.5) | copy-done | bytes 36888
  7.7 0.0 copy-start.6
  7.7 0.8 %copy-done.6 = bf16[64,256]{1,0:T(8,128)(2,1)S(1)} copy-done((bf16[64,256]{1,0:T(8,128)(2,1)S(1)}, bf16[64,256]{1,0:T(8,128)(2,1)}, u32[]{:S(2)}) %copy-start.6) | copy-done | bytes 32792
  8.4 0.0 copy-start.7
  8.4 0.8 %copy-done.7 = bf16[128,80]{1,0:T(8,128)(2,1)S(1)} copy-done((bf16[128,80]{1,0:T(8,128)(2,1)S(1)}, bf16[128,80]{1,0:T(8,128)(2,1)}, u32[]{:S(2)}) %copy-start.7) | copy-done | bytes 20504
  9.2 0.0 copy-start.8
  9.2 0.7 %copy-done.8 = s32[8,4,64]{2,1,0:T(4,128)S(1)} copy-done((s32[8,4,64]{2,1,0:T(4,128)S(1)}, s32[8,4,64]{2,1,0:T(4,128)}, u32[]{:S(2)}) %copy-start.8) | copy-done | bytes 8216
  9.9 0.0 copy-start.9
  9.9 0.7 %copy-done.9 = s32[8,1]{0,1:T(1,128)S(1)} copy-done((s32[8,1]{0,1:T(1,128)S(1)}, s32[8,1]{0,1:T(1,128)}, u32[]{:S(2)}) %copy-start.9) | copy-done | bytes 56
  10.6 10.7 %channelize.1 = (f32[128,72,128]{2,1,0:T(8,128)S(1)}, f32[4,128,128]{2,1,0:T(8,128)S(1)}, f32[72,128]{1,0:T(8,128)S(1)}, bf16[528,128]{1,0:T(8,128)(2,1)S(1)}, b...) custom-call(bf16[1,2097152]{1,0:T(2,128)(2,1)S(1)} %copy-done, ...), custom_call_target="tpu_custom_call" | custom-call | tf_op jit(solution)/shard_map/channelize/pallas_call | solution.py:414
  21.3 3.0 %collective-permute-start = (bf16[528,128]{1,0:T(8,128)(2,1)S(1)}, bf16[528,128]{1,0:T(8,128)(2,1)S(1)}, u32[]{:S(2)}, u32[]{:S(2)}) collective-permute-start(bf16[528,128]{1,0:T(8,128)(2,1)S(1)} %get-tuple-element.19.own_ref), channel_id=1, source_target_pairs={{0,2},{2,0},{1,3},{3,1},{4,6},{6,4},{5,7},{7,5},{8,10},{10,8},{9,1... | collective-permute-start | bytes 405512 | tf_op jit(solution)/shard_map/ppermute | solution.py:450
  24.3 3.6 %collective-permute-done.other_ref = bf16[528,128]{1,0:T(8,128)(2,1)S(1)} collective-permute-done((bf16[528,128]{1,0:T(8,128)(2,1)S(1)}, bf16[528,128]{1,0:T(8,128)(2,1)S(1)}, u32[]{:S(2)}, u32[]{:S(2)}) %collective-permute-start) | collective-permute-done | bytes 135200 | tf_op jit(solution)/shard_map/ppermute | solution.py:450
  27.9 3.5 %search.1 = f32[8,4,4,128]{3,2,1,0:T(4,128)S(1)} custom-call(f32[128,72,128]{2,1,0:T(8,128)S(1)} %get-tuple-element.16.power_ref, f32[4,128,128]{2,1,0:T(8,128)S(1)} %get-tuple-element.17.pr_ref, f32[72,128]{1,0:T(8,128)S(1)} %get-tuple-element.18.band_ref, bf16[528,128]{1,0:T(8,128)(2,1)S(1)} %get-tuple-element.19.own_ref, ...), custom_call_target="tpu_custom_call" | custom-call | tf_op jit(solution)/shard_map/search/pallas_call | solution.py:461
  31.4 12.8 %all_to_all.5.recv_ref = f32[8,4,4,128]{3,2,1,0:T(4,128)S(1)} all-to-all(f32[8,4,4,128]{3,2,1,0:T(4,128)S(1)} %search.1), channel_id=1, replica_groups=mesh['group'=2,'dm'=4,'tm'=2,'beam'=2] {'dm','tm'}, dimensions={0} | all-to-all | bytes 131072 | tf_op jit(solution)/shard_map/all_to_all | solution.py:482
  44.2 0.0 copy-done.10
  44.2 1.6 %boxes.1 = bf16[4,4,1,4,8,128]{5,4,3,2,1,0:T(8,128)(2,1)} custom-call(f32[8,4,4,128]{3,2,1,0:T(4,128)S(1)} %all_to_all.5.recv_ref, s32[8]{0:T(128)S(1)} %copy-done.10), custom_call_target="tpu_custom_call" | custom-call | tf_op jit(solution)/shard_map/boxes/pallas_call | solution.py:483
Async XLA Ops:
  0.0 44.2 %copy-start.10 = (s32[8]{0:T(128)S(1)}, s32[8]{0:T(128)}, u32[]{:S(2)}) copy-start(s32[8]{0:T(128)} %widths_ref.1) | copy-start | bytes 100
  0.0 3.4 %copy-start = (bf16[1,2097152]{1,0:T(2,128)(2,1)S(1)}, bf16[1,2097152]{1,0:T(2,128)(2,1)}, u32[]{:S(2)}) copy-start(bf16[1,2097152]{1,0:T(2,128)(2,1)} %raw_ref.1) | copy-start | bytes 12582916
  3.4 0.9 %copy-start.1 = (f32[4,16384]{1,0:T(4,128)S(1)}, f32[4,16384]{1,0:T(4,128)}, u32[]{:S(2)}) copy-start(f32[4,16384]{1,0:T(4,128)} %proto_ref.1) | copy-start | bytes 786436
  4.3 0.9 %copy-start.2 = (bf16[256,256]{1,0:T(8,128)(2,1)S(1)}, bf16[256,256]{1,0:T(8,128)(2,1)}, u32[]{:S(2)}) copy-start(bf16[256,256]{1,0:T(8,128)(2,1)} %constant.14.clone.second_in) | copy-start | bytes 393220
  5.3 0.9 %copy-start.3 = (f32[2,72,128]{2,1,0:T(8,128)S(1)}, f32[2,72,128]{2,1,0:T(8,128)}, u32[]{:S(2)}) copy-start(f32[2,72,128]{2,1,0:T(8,128)} %constant.13.clone.twiddle_in) | copy-start | bytes 221188
  6.1 0.8 %copy-start.4 = (f32[72,128]{1,0:T(8,128)S(1)}, f32[72,128]{1,0:T(8,128)}, u32[]{:S(2)}) copy-start(f32[72,128]{1,0:T(8,128)} %constant.16.clone.weight_in) | copy-start | bytes 110596
  6.9 0.8 %copy-start.5 = (bf16[144,128]{1,0:T(8,128)(2,1)S(1)}, bf16[144,128]{1,0:T(8,128)(2,1)}, u32[]{:S(2)}) copy-start(bf16[144,128]{1,0:T(8,128)(2,1)} %constant.12.clone.first_in) | copy-start | bytes 110596
  7.7 0.8 %copy-start.6 = (bf16[64,256]{1,0:T(8,128)(2,1)S(1)}, bf16[64,256]{1,0:T(8,128)(2,1)}, u32[]{:S(2)}) copy-start(bf16[64,256]{1,0:T(8,128)(2,1)} %constant.17.clone.expand_ref) | copy-start | bytes 98308
  8.4 0.8 %copy-start.7 = (bf16[128,80]{1,0:T(8,128)(2,1)S(1)}, bf16[128,80]{1,0:T(8,128)(2,1)}, u32[]{:S(2)}) copy-start(bf16[128,80]{1,0:T(8,128)(2,1)} %constant.15.clone.masks_in) | copy-start | bytes 61444
  9.2 0.7 %copy-start.8 = (s32[8,4,64]{2,1,0:T(4,128)S(1)}, s32[8,4,64]{2,1,0:T(4,128)}, u32[]{:S(2)}) copy-start(s32[8,4,64]{2,1,0:T(4,128)} %delays_ref.1) | copy-start | bytes 24580
  9.9 0.7 %copy-start.9 = (s32[8,1]{0,1:T(1,128)S(1)}, s32[8,1]{0,1:T(1,128)}, u32[]{:S(2)}) copy-start(s32[8,1]{0,1:T(1,128)} %param.15) | copy-start | bytes 100
  21.3 6.6 %collective-permute-start = (bf16[528,128]{1,0:T(8,128)(2,1)S(1)}, bf16[528,128]{1,0:T(8,128)(2,1)S(1)}, u32[]{:S(2)}, u32[]{:S(2)}) collective-permute-start(bf16[528,128]{1,0:T(8,128)(2,1)S(1)} %get-tuple-element.19.own_ref), channel_id=1, source_target_pairs={{0,2},{2,0},{1,3},{3,1},{4,6},{6,4},{5,7},{7,5},{8,10},{10,8},{9,1... | collective-permute-start | bytes 405512 | tf_op jit(solution)/shard_map/ppermute | solution.py:450

commit v3 on v2

--- a/solution.py
+++ b/solution.py
@@ -128,8 +128,8 @@
     return out
 
 
-def channelize(z, raw_ref, proto_ref, first_in, twiddle_in, second_in, masks_in, weight_in, expand_ref, delays_ref, owners_in,
-               power_ref, pr_ref, band_ref, msg_ref, first_ref, twiddle_ref, second_ref, masks_ref, weight_ref, hits_ref, owners_ref,
+def channelize(z, raw_ref, proto_ref, first_in, twiddle_in, second_in, masks_in, weight_in, expand_ref, delays_ref, owners_in, widths_in,
+               power_ref, pr_ref, band_ref, msg_ref, first_ref, twiddle_ref, second_ref, masks_ref, weight_ref, hits_ref, owners_ref, widths_ref,
                buf, tap_ref, spread_ref, trial_ref, hist_ref, y0_ref, y1_ref, t0_ref, t1_ref, t2_ref, t3_ref, sems, sides):
     chunks = z.spec // CHUNK
     span = CHUNK * z.channels
@@ -142,17 +142,15 @@
     pairs = [
         (proto_ref, tap_ref), (first_in, first_ref), (twiddle_in, twiddle_ref), (second_in, second_ref),
         (delays_ref, trial_ref), (expand_ref, spread_ref), (masks_in, masks_ref), (weight_in, weight_ref),
+        (owners_in, owners_ref), (widths_in, widths_ref),
     ]
     copies = [pltpu.make_async_copy(source, target, sides.at[i]) for i, (source, target) in enumerate(pairs)]
-    copies[0].start()
-    for copy in copies[1:]:
+    for copy in copies:
         copy.start()
     for i in range(1, chunks):
         raw_copy(i).start()
     hist_ref[...] = jnp.zeros_like(hist_ref)
     band_ref[...] = jnp.zeros_like(band_ref)
-    for g in range(z.groups):
-        owners_ref[g] = owners_in[g]
     early = lax.axis_index("tm") > 0
     copies[0].wait()
     for tap in range(z.taps):
@@ -392,12 +390,12 @@
     return pl.BlockSpec(memory_space=pltpu.SMEM)
 
 
-def any_spec():
-    return pl.BlockSpec(memory_space=pl.ANY)
-
-
-def kept(*values):
-    return [pltpu.with_memory_space_constraint(value, pltpu.VMEM) for value in values]
+def hbm_spec():
+    return pl.BlockSpec(memory_space=pltpu.HBM)
+
+
+def kept(*values, space=pltpu.VMEM):
+    return [pltpu.with_memory_space_constraint(value, space) for value in values]
 
 
 def shards(n_dm, n_tm, raw, proto, delays, widths, owners):
@@ -411,7 +409,7 @@
     f32, bf16 = jnp.float32, jnp.bfloat16
     chunks = z.spec // CHUNK
     half = CHUNK // 2 * z.rows16
-    power, pr, band, msg, first, twiddle, second, masks, weight, hits, owner = pl.pallas_call(
+    power, pr, band, msg, first, twiddle, second, masks, weight, hits, owner, width = pl.pallas_call(
         functools.partial(channelize, z),
         out_shape=(
             pltpu.VMEM((z.spec, z.rows, LANES), f32),
@@ -425,9 +423,10 @@
             pltpu.VMEM(weight.shape, f32),
             pltpu.VMEM((groups, (MAXT + 1) * 8, 2 * LANES), bf16),
             pltpu.SMEM((groups,), jnp.int32),
+            pltpu.SMEM(widths.shape, jnp.int32),
         ),
-        in_specs=[any_spec()] * 9 + [smem_spec()],
-        out_specs=[vmem_spec()] * 10 + [smem_spec()],
+        in_specs=[hbm_spec()] * 11,
+        out_specs=[vmem_spec()] * 10 + [smem_spec()] * 2,
         scratch_shapes=[
             pltpu.VMEM((1, z.spec * channels), bf16),
             pltpu.VMEM(proto.shape, f32),
@@ -441,11 +440,16 @@
             pltpu.VMEM((half, 2 * LANES), bf16),
             pltpu.VMEM((half, 2 * LANES), bf16),
             pltpu.SemaphoreType.DMA((chunks,)),
-            pltpu.SemaphoreType.DMA((8,)),
+            pltpu.SemaphoreType.DMA((10,)),
         ],
         compiler_params=params,
         name="channelize",
-    )(raw, proto, first, twiddle, second, masks, weight, expand, delays, owners.reshape(groups))
+    )(
+        *kept(
+            raw, proto, first, twiddle, second, masks, weight, expand, delays, owners.reshape(groups), widths,
+            space=pltpu.HBM,
+        )
+    )
     if n_tm == 2:
         own, other = msg, lax.ppermute(msg, "tm", [(0, 1), (1, 0)])
     else:
@@ -477,7 +481,7 @@
         name="search",
     )(
         *kept(power, pr, band, own, other, first, twiddle, second, masks, weight, hits),
-        pltpu.with_memory_space_constraint(owner, pltpu.SMEM),
+        *kept(owner, space=pltpu.SMEM),
     )
     recv = lax.all_to_all(out, ("dm", "tm"), split_axis=0, concat_axis=0, tiled=True)
     return pl.pallas_call(
@@ -488,7 +492,7 @@
         scratch_shapes=[pltpu.VMEM((WMAX, z.capacity * trials, LANES), f32)],
         compiler_params=params,
         name="boxes",
-    )(*kept(recv), widths)
+    )(*kept(recv), *kept(width, space=pltpu.SMEM))
 
 
 def solution(mesh):

time: 46.4 us -> 35.6 us (0.77)
  local copies, waits for them, and re-layouts: 10.6 us -> 0 us
    unnamed x22 -> x0, local copies, waits for them, and re-layouts: 10.6 us -> none
    pallas_call x1, Pallas kernels: 10.7 us -> 11.6 us  [shards(): pl.pallas_call(functools.partial(channelize, z), out_shape=(pltpu.VMEM((z...]
    pallas_call x1, Pallas kernels: 1.56 us -> 1.01 us  [shards(): pl.pallas_call(functools.partial(boxes, z), out_shape=jax.ShapeDtypeStruc...]
where the time goes in v3:
time: 35.6 us; the launch traced here: 35.4 us
  Pallas kernels  16.1 us (45%)
  blocking collectives  12.7 us (36%)
  waiting for transfers between devices  3.59 us (10%)
  starting transfers between devices  3 us (8%)
    all_to_all x1, blocking collectives, shards(): lax.all_to_all(out, ('dm', 'tm'), split_axis=0, concat_axis=0, tiled=True)  12.7 us
    pallas_call x1, Pallas kernels, shards(): pl.pallas_call(functools.partial(channelize, z), out_shape=(pltpu.VMEM((z...  11.6 us
    ppermute x1, waiting for transfers between devices, shards(): own, other = (msg, lax.ppermute(msg, 'tm', [(0, 1), (1, 0)]))  3.59 us
    pallas_call x1, Pallas kernels, shards(): pl.pallas_call(functools.partial(search, z), out_shape=pltpu.VMEM((n_dm *...  3.47 us
    ppermute x1, starting transfers between devices, shards(): own, other = (msg, lax.ppermute(msg, 'tm', [(0, 1), (1, 0)]))  3 us
    pallas_call x1, Pallas kernels, shards(): pl.pallas_call(functools.partial(boxes, z), out_shape=jax.ShapeDtypeStruc...  1.01 us
  transfers between devices with their start and end apart: 1, of which 1 were waited for; matrix products, arithmetic and copies ran while one was open for 0% of the time, Pallas kernels for 0%

profile of v3, /device:TPU:0, one launch (start us, length us, event | category | flops | bytes accessed | tf_op | source)
XLA Modules:
  0.0 35.4 jit_solution(6956658847999647140)
XLA Ops:
  0.0 11.6 %channelize.1 = (f32[128,72,128]{2,1,0:T(8,128)S(1)}, f32[4,128,128]{2,1,0:T(8,128)S(1)}, f32[72,128]{1,0:T(8,128)S(1)}, bf16[528,128]{1,0:T(8,128)(2,1)S(1)}, b...) custom-call(bf16[1,2097152]{1,0:T(2,128)(2,1)} %raw_ref.1, ...), custom_call_target="tpu_custom_call" | custom-call | tf_op jit(solution)/shard_map/channelize/pallas_call | solution.py:412
  11.6 3.0 %collective-permute-start = (bf16[528,128]{1,0:T(8,128)(2,1)S(1)}, bf16[528,128]{1,0:T(8,128)(2,1)S(1)}, u32[]{:S(2)}, u32[]{:S(2)}) collective-permute-start(bf16[528,128]{1,0:T(8,128)(2,1)S(1)} %get-tuple-element.20.own_ref), channel_id=1, source_target_pairs={{0,2},{2,0},{1,3},{3,1},{4,6},{6,4},{5,7},{7,5},{8,10},{10,8},{9,1... | collective-permute-start | bytes 405512 | tf_op jit(solution)/shard_map/ppermute | solution.py:454
  14.6 3.6 %collective-permute-done.other_ref = bf16[528,128]{1,0:T(8,128)(2,1)S(1)} collective-permute-done((bf16[528,128]{1,0:T(8,128)(2,1)S(1)}, bf16[528,128]{1,0:T(8,128)(2,1)S(1)}, u32[]{:S(2)}, u32[]{:S(2)}) %collective-permute-start) | collective-permute-done | bytes 135200 | tf_op jit(solution)/shard_map/ppermute | solution.py:454
  18.2 3.5 %search.1 = f32[8,4,4,128]{3,2,1,0:T(4,128)S(1)} custom-call(f32[128,72,128]{2,1,0:T(8,128)S(1)} %get-tuple-element.17.power_ref, f32[4,128,128]{2,1,0:T(8,128)S(1)} %get-tuple-element.18.pr_ref, f32[72,128]{1,0:T(8,128)S(1)} %get-tuple-element.19.band_ref, bf16[528,128]{1,0:T(8,128)(2,1)S(1)} %get-tuple-element.20.own_ref, ...), custom_call_target="tpu_custom_call" | custom-call | tf_op jit(solution)/shard_map/search/pallas_call | solution.py:465
  21.7 12.7 %all_to_all.5.recv_ref = f32[8,4,4,128]{3,2,1,0:T(4,128)S(1)} all-to-all(f32[8,4,4,128]{3,2,1,0:T(4,128)S(1)} %search.1), channel_id=1, replica_groups=mesh['group'=2,'dm'=4,'tm'=2,'beam'=2] {'dm','tm'}, dimensions={0} | all-to-all | bytes 131072 | tf_op jit(solution)/shard_map/all_to_all | solution.py:486
  34.4 1.0 %boxes.1 = bf16[4,4,1,4,8,128]{5,4,3,2,1,0:T(8,128)(2,1)} custom-call(f32[8,4,4,128]{3,2,1,0:T(4,128)S(1)} %all_to_all.5.recv_ref, s32[8]{0:T(128)S(4)} %get-tuple-element.28.widths_ref), custom_call_target="tpu_custom_call" | custom-call | tf_op jit(solution)/shard_map/boxes/pallas_call | solution.py:487
Async XLA Ops:
  11.6 6.6 %collective-permute-start = (bf16[528,128]{1,0:T(8,128)(2,1)S(1)}, bf16[528,128]{1,0:T(8,128)(2,1)S(1)}, u32[]{:S(2)}, u32[]{:S(2)}) collective-permute-start(bf16[528,128]{1,0:T(8,128)(2,1)S(1)} %get-tuple-element.20.own_ref), channel_id=1, source_target_pairs={{0,2},{2,0},{1,3},{3,1},{4,6},{6,4},{5,7},{7,5},{8,10},{10,8},{9,1... | collective-permute-start | bytes 405512 | tf_op jit(solution)/shard_map/ppermute | solution.py:454

commit v4 on v3

--- a/solution.py
+++ b/solution.py
@@ -45,50 +45,69 @@
         self.capacity = 2 * (groups // n_dm)
 
 
-def dft_constants(z):
+def constants(z):
     cos_a, sin_a = angle_tables(DFT_A, DFT_A, DFT_A)
     first = np.zeros((2 * z.rows, DFT_A))
     first[: z.half] = cos_a[: z.half]
     first[z.rows : z.rows + z.half] = -sin_a[: z.half]
-    tw_cos, tw_sin = np.zeros((2, z.rows, z.side))
+    tw_cos, tw_sin = np.zeros((2, z.rows16, z.side))
     tw_cos[: z.half], tw_sin[: z.half] = angle_tables(z.half, z.side, z.channels)
     cos_b, sin_b = angle_tables(z.side, z.side, z.side)
-    second = np.block([[cos_b, -sin_b], [sin_b, cos_b]])
-    return (
-        jnp.asarray(first, jnp.bfloat16),
-        jnp.asarray(np.stack([tw_cos, tw_sin]), jnp.float32),
-        jnp.asarray(second, jnp.bfloat16),
-    )
-
-
-def mask_constants(z):
     width = z.channels // NBLK
     fine = np.arange(z.groups)[:, None] * FD * (width - 1 - np.arange(width))[None, :] // (z.groups * (width - 1))
     parities = width // DFT_A
-    masks = np.zeros((2, FD, parities, z.groups, z.rows16))
+    masks = np.zeros((2, FD, parities, z.groups, LANES))
     for step in range(FD):
         for parity in range(parities):
             hit = fine[:, parity * DFT_A : (parity + 1) * DFT_A] == step
             masks[0, step, parity, :, : z.half] = hit[:, : z.half]
             masks[1, step, parity, :, 1 : z.half - 1] = hit[:, : z.half - 1 : -1]
-    weight = np.zeros((z.rows, LANES))
+    weight = np.zeros((z.rows16, LANES))
     weight[: z.half] = 2.0 / z.channels
     weight[0] = weight[z.half - 1] = 1.0 / z.channels
     expand = np.zeros((NBLK, 2 * z.side))
     lane = np.arange(z.side)
     expand[lane // parities, lane] = 1
     expand[(z.side - 1 - lane) // parities, z.side + lane] = 1
-    return (
-        jnp.asarray(masks.reshape(-1, z.rows16), jnp.bfloat16),
-        jnp.asarray(weight, jnp.float32),
-        jnp.asarray(expand, jnp.bfloat16),
-    )
+    tables = {
+        "first": first,
+        "cos": tw_cos,
+        "sin": tw_sin,
+        "second": np.concatenate([cos_b, sin_b]),
+        "second_im": np.concatenate([-sin_b, cos_b]),
+        "masks": masks.reshape(-1, LANES),
+        "weight": weight,
+        "expand": expand[:, : z.side],
+        "expand_im": expand[:, z.side :],
+    }
+    places, row = {}, 0
+    for name, table in tables.items():
+        places[name] = (row, row + table.shape[0])
+        row += table.shape[0]
+    return jnp.asarray(np.concatenate(list(tables.values())), jnp.bfloat16), places
+
+
+def table(z, ref, name):
+    first, last = z.places[name]
+    return ref[first:last]
+
+
+def wide_table(z, ref, name):
+    return jnp.concatenate([table(z, ref, name), table(z, ref, name + "_im")], 1)
 
 
 def fill_frames(z, history, load, pr_ref, y_ref, count, save=None):
     for block in range(DFT_A // 16):
         rows = pl.ds(block * 16, 16)
-        taps = [pr_ref[tap, rows, :] for tap in range(z.taps)]
+        taps = [
+            jnp.concatenate(
+                [
+                    pr_ref[tap, :, (2 * block + part) * 8 * LANES : (2 * block + part + 1) * 8 * LANES].reshape(8, LANES)
+                    for part in range(2)
+                ]
+            )
+            for tap in range(z.taps)
+        ]
         window = [history(k, block) for k in range(z.hist)]
         for k in range(count):
             window.append(load(k, block))
@@ -102,25 +121,24 @@
                 save(k, block, window[k])
 
 
-def transform(z, y_ref, first_ref, twiddle_ref, second_ref, t_refs, count):
+def transform(z, y_ref, tab_ref, t_refs, count):
     pad = jnp.zeros((z.rows16 - z.rows, LANES), jnp.float32)
+    cos, sin = table(z, tab_ref, "cos"), table(z, tab_ref, "sin")
     part = count // len(t_refs)
     out = []
     for index, t_ref in enumerate(t_refs):
         for at in range(0, part, 2):
             pair = min(2, part - at)
             lane = (index * part + at) * LANES
-            a = jnp.dot(first_ref[...], y_ref[:, lane : lane + pair * LANES], preferred_element_type=jnp.float32)
+            a = jnp.dot(table(z, tab_ref, "first"), y_ref[:, lane : lane + pair * LANES], preferred_element_type=jnp.float32)
             for k in range(pair):
-                re = a[: z.rows, k * LANES : (k + 1) * LANES]
-                im = a[z.rows :, k * LANES : (k + 1) * LANES]
-                cos, sin = twiddle_ref[0], twiddle_ref[1]
-                t_re = re * cos + im * sin
-                t_im = im * cos - re * sin
+                lanes = slice(k * LANES, (k + 1) * LANES)
+                re = jnp.concatenate([a[: z.rows, lanes], pad]).astype(jnp.bfloat16)
+                im = jnp.concatenate([a[z.rows :, lanes], pad]).astype(jnp.bfloat16)
                 rows = slice((at + k) * z.rows16, (at + k + 1) * z.rows16)
-                t_ref[rows, :LANES] = jnp.concatenate([t_re, pad]).astype(jnp.bfloat16)
-                t_ref[rows, LANES:] = jnp.concatenate([t_im, pad]).astype(jnp.bfloat16)
-        c = jnp.dot(t_ref[...], second_ref[...], preferred_element_type=jnp.float32)
+                t_ref[rows, :LANES] = re * cos + im * sin
+                t_ref[rows, LANES:] = im * cos - re * sin
+        c = jnp.dot(t_ref[...], wide_table(z, tab_ref, "second"), preferred_element_type=jnp.float32)
         for k in range(part):
             rows = c[k * z.rows16 : k * z.rows16 + z.rows]
             re, im = rows[:, :LANES], rows[:, LANES:]
@@ -128,55 +146,38 @@
     return out
 
 
-def channelize(z, raw_ref, proto_ref, first_in, twiddle_in, second_in, masks_in, weight_in, expand_ref, delays_ref, owners_in, widths_in,
-               power_ref, pr_ref, band_ref, msg_ref, first_ref, twiddle_ref, second_ref, masks_ref, weight_ref, hits_ref, owners_ref, widths_ref,
-               buf, tap_ref, spread_ref, trial_ref, hist_ref, y0_ref, y1_ref, t0_ref, t1_ref, t2_ref, t3_ref, sems, sides):
+def channelize(z, raw_ref, proto_ref, tab_in, delays_ref, owners_in, widths_in,
+               power_ref, pr_ref, band_ref, msg_ref, tab_ref, hits_ref, owners_ref, widths_ref,
+               buf, trial_ref, hist_ref, y0_ref, y1_ref, t0_ref, t1_ref, t2_ref, t3_ref, sems):
     chunks = z.spec // CHUNK
     span = CHUNK * z.channels
 
-    def raw_copy(i):
-        part = pl.ds(i * span, span)
-        return pltpu.make_async_copy(raw_ref.at[:, part], buf.at[:, part], sems.at[i])
-
-    raw_copy(0).start()
-    pairs = [
-        (proto_ref, tap_ref), (first_in, first_ref), (twiddle_in, twiddle_ref), (second_in, second_ref),
-        (delays_ref, trial_ref), (expand_ref, spread_ref), (masks_in, masks_ref), (weight_in, weight_ref),
-        (owners_in, owners_ref), (widths_in, widths_ref),
-    ]
-    copies = [pltpu.make_async_copy(source, target, sides.at[i]) for i, (source, target) in enumerate(pairs)]
-    for copy in copies:
-        copy.start()
-    for i in range(1, chunks):
-        raw_copy(i).start()
+    def raw_copy(i, side):
+        part = pl.ds(pl.multiple_of(i * span, span), span)
+        return pltpu.make_async_copy(raw_ref.at[:, part], buf.at[:, part], sems.at[side])
+
+    tab_copy = pltpu.make_async_copy(tab_in, tab_ref, sems.at[2])
+    delays_copy = pltpu.make_async_copy(delays_ref, trial_ref, sems.at[2])
+    owners_copy = pltpu.make_async_copy(owners_in, owners_ref, sems.at[3])
+    widths_copy = pltpu.make_async_copy(widths_in, widths_ref, sems.at[3])
+    raw_copy(0, 0).start()
+    for tap in range(z.taps):
+        pltpu.make_async_copy(proto_ref.at[tap : tap + 1], pr_ref.at[tap], sems.at[3]).start()
+    tab_copy.start()
+    raw_copy(1, 1).start()
     hist_ref[...] = jnp.zeros_like(hist_ref)
     band_ref[...] = jnp.zeros_like(band_ref)
     early = lax.axis_index("tm") > 0
-    copies[0].wait()
-    for tap in range(z.taps):
-        pr_ref[tap] = tap_ref[tap : tap + 1, :].reshape(DFT_A, LANES)
-    for copy in copies[1:]:
-        copy.wait()
-    unit = 1.0 / (math.sqrt(z.channels // NBLK) * math.sqrt(NBLK))
-    trials = trial_ref.shape[1]
-    tall = jnp.concatenate(
-        [
-            jnp.concatenate([trial_ref[g].astype(jnp.float32), jnp.zeros((8 - trials, NBLK), jnp.float32)])
-            for g in range(z.groups)
-        ]
-    )
-    spread = jnp.dot(tall.astype(jnp.bfloat16), spread_ref[...], preferred_element_type=jnp.float32)
-    for g in range(z.groups):
-        mine = spread[g * 8 : g * 8 + 8]
-        hits = jnp.concatenate([jnp.where(mine == value, unit, 0.0) for value in range(MAXT + 1)])
-        hits_ref[g] = hits.astype(jnp.bfloat16)
 
     def frames(i, y_ref):
         base = i * span
 
         def load(k, block):
-            start = pl.multiple_of(base + k * z.channels + block * 16 * LANES, 16 * LANES)
-            return buf[:, pl.ds(start, 16 * LANES)].astype(jnp.float32).reshape(16, LANES)
+            parts = []
+            for part in range(2):
+                start = pl.multiple_of(base + k * z.channels + (2 * block + part) * 8 * LANES, 8 * LANES)
+                parts.append(buf[:, pl.ds(start, 8 * LANES)].astype(jnp.float32).reshape(8, LANES))
+            return jnp.concatenate(parts)
 
         def history(k, block):
             return hist_ref[k, block * 16 : block * 16 + 16, :]
@@ -187,7 +188,7 @@
         fill_frames(z, history, load, pr_ref, y_ref, CHUNK, save)
 
     def powers(i, y_ref, t_refs):
-        power = transform(z, y_ref, first_ref, twiddle_ref, second_ref, t_refs, CHUNK)
+        power = transform(z, y_ref, tab_ref, t_refs, CHUNK)
         late = power[z.hist]
         for k in range(z.hist + 1, CHUNK):
             late = late + power[k]
@@ -199,16 +200,24 @@
         for k in range(CHUNK):
             power_ref[i * CHUNK + k] = power[k]
 
-    def arrived(i):
-        raw_copy(i).wait()
-
-    arrived(0)
+    pltpu.make_async_copy(pr_ref, pr_ref, sems.at[3]).wait()
+    owners_copy.start()
+    raw_copy(0, 0).wait()
+    raw_copy(2, 0).start()
     frames(0, y0_ref)
+    tab_copy.wait()
+    delays_copy.start()
 
     def step(j, carry):
         i = 2 * j
-        arrived(i + 1)
-        arrived(i + 2)
+        raw_copy(i + 1, 1).wait()
+        raw_copy(i + 2, 0).wait()
+        raw_copy(i + 3, 1).start()
+
+        @pl.when(i + 4 < chunks)
+        def _():
+            raw_copy(i + 4, 0).start()
+
         frames(i + 1, y1_ref)
         powers(i, y0_ref, [t0_ref, t1_ref])
         frames(i + 2, y0_ref)
@@ -216,10 +225,28 @@
         return carry
 
     lax.fori_loop(0, chunks // 2 - 1, step, 0)
-    arrived(chunks - 1)
+    raw_copy(chunks - 1, 1).wait()
+    owners_copy.wait()
+    widths_copy.start()
+    delays_copy.wait()
     frames(chunks - 1, y1_ref)
     powers(chunks - 2, y0_ref, [t0_ref, t1_ref])
     powers(chunks - 1, y1_ref, [t2_ref, t3_ref])
+    unit = 1.0 / (math.sqrt(z.channels // NBLK) * math.sqrt(NBLK))
+    trials = trial_ref.shape[1]
+    tall = jnp.concatenate(
+        [
+            jnp.concatenate([trial_ref[g].astype(jnp.float32), jnp.zeros((8 - trials, NBLK), jnp.float32)])
+            for g in range(z.groups)
+        ]
+    )
+    spread = jnp.dot(
+        tall.astype(jnp.bfloat16), wide_table(z, tab_ref, "expand"), preferred_element_type=jnp.float32
+    )
+    for g in range(z.groups):
+        mine = spread[g * 8 : g * 8 + 8]
+        hits = jnp.concatenate([jnp.where(mine == value, unit, 0.0) for value in range(MAXT + 1)])
+        hits_ref[g] = hits.astype(jnp.bfloat16)
 
     def spectrum(start):
         start = pl.multiple_of(start, z.channels)
@@ -235,10 +262,10 @@
     high = band_ref[...].astype(jnp.bfloat16)
     msg_ref[row : row + z.rows] = high
     msg_ref[row + z.rows : row + 2 * z.rows] = (band_ref[...] - high.astype(jnp.float32)).astype(jnp.bfloat16)
-
-
-def search(z, power_ref, pr_ref, band_ref, own_ref, other_ref, first_ref, twiddle_ref, second_ref,
-           masks_ref, weight_ref, hits_ref, owners_ref,
+    widths_copy.wait()
+
+
+def search(z, power_ref, pr_ref, band_ref, own_ref, other_ref, tab_ref, hits_ref, owners_ref,
            out_ref, y_ref, t_ref, bound_ref, inv_ref, weighted_ref, sums_ref, mean_ref, sub_ref):
     me = lax.axis_index("tm")
     groups, spec = z.groups, z.spec
@@ -261,13 +288,13 @@
         fill_frames(
             z, lambda k, block: take(k, block, True), lambda k, block: take(k, block, False), pr_ref, y_ref, z.hist
         )
-        power = transform(z, y_ref, first_ref, twiddle_ref, second_ref, [t_ref], z.hist)
+        power = transform(z, y_ref, tab_ref, [t_ref], z.hist)
         for k in range(z.hist):
             total = total + power[k]
             bound_ref[b * z.hist + k] = power[k]
     scale = float(z.taps * z.channels)
     inv_ref[...] = 1.0 / (total * (1.0 / (z.spec * z.n_tm)) + 1e-6 * scale)
-    weighted_ref[...] = weight_ref[...] * inv_ref[...]
+    weighted_ref[...] = table(z, tab_ref, "weight").astype(jnp.float32)[: z.rows] * inv_ref[...]
     mine = jnp.maximum(me - 1, 0) * z.hist
 
     def power_of(i, k):
@@ -306,7 +333,8 @@
             flats.append(jnp.concatenate([flat, pad]).astype(jnp.bfloat16))
             if k % 2 == 0:
                 continue
-            found = jnp.dot(masks_ref[...], jnp.concatenate(flats[-2:], 1), preferred_element_type=jnp.float32)
+            masks = table(z, tab_ref, "masks")[:, : z.rows16]
+            found = jnp.dot(masks, jnp.concatenate(flats[-2:], 1), preferred_element_type=jnp.float32)
             for half in range(2):
                 value = found[:, half * LANES : (half + 1) * LANES]
                 at = pl.multiple_of((i * CHUNK + k - 1 + half) * groups, 8)
@@ -402,35 +430,27 @@
     taps, channels = proto.shape
     groups, trials, _ = delays.shape
     z = Sizes(taps, channels, raw.shape[1] // channels, groups, n_dm, n_tm)
-    first, twiddle, second = dft_constants(z)
-    masks, weight, expand = mask_constants(z)
+    tables, z.places = constants(z)
     params = pltpu.CompilerParams(vmem_limit_bytes=LIMIT)
     own_rows = z.raw_rows * (1 if n_tm == 2 else 2) + 2 * z.rows
     f32, bf16 = jnp.float32, jnp.bfloat16
-    chunks = z.spec // CHUNK
     half = CHUNK // 2 * z.rows16
-    power, pr, band, msg, first, twiddle, second, masks, weight, hits, owner, width = pl.pallas_call(
+    power, pr, band, msg, tables, hits, owner, width = pl.pallas_call(
         functools.partial(channelize, z),
         out_shape=(
             pltpu.VMEM((z.spec, z.rows, LANES), f32),
-            pltpu.VMEM((taps, DFT_A, LANES), f32),
+            pltpu.VMEM((taps, 1, channels), f32),
             pltpu.VMEM((z.rows, LANES), f32),
             pltpu.VMEM((own_rows, LANES), bf16),
-            pltpu.VMEM(first.shape, bf16),
-            pltpu.VMEM(twiddle.shape, f32),
-            pltpu.VMEM(second.shape, bf16),
-            pltpu.VMEM(masks.shape, bf16),
-            pltpu.VMEM(weight.shape, f32),
+            pltpu.VMEM(tables.shape, bf16),
             pltpu.VMEM((groups, (MAXT + 1) * 8, 2 * LANES), bf16),
             pltpu.SMEM((groups,), jnp.int32),
             pltpu.SMEM(widths.shape, jnp.int32),
         ),
-        in_specs=[hbm_spec()] * 11,
-        out_specs=[vmem_spec()] * 10 + [smem_spec()] * 2,
+        in_specs=[hbm_spec()] * 6,
+        out_specs=[vmem_spec()] * 6 + [smem_spec()] * 2,
         scratch_shapes=[
             pltpu.VMEM((1, z.spec * channels), bf16),
-            pltpu.VMEM(proto.shape, f32),
-            pltpu.VMEM(expand.shape, bf16),
             pltpu.VMEM(delays.shape, jnp.int32),
             pltpu.VMEM((z.hist, DFT_A, LANES), f32),
             pltpu.VMEM((DFT_A, CHUNK * LANES), bf16),
@@ -439,16 +459,12 @@
             pltpu.VMEM((half, 2 * LANES), bf16),
             pltpu.VMEM((half, 2 * LANES), bf16),
             pltpu.VMEM((half, 2 * LANES), bf16),
-            pltpu.SemaphoreType.DMA((chunks,)),
-            pltpu.SemaphoreType.DMA((10,)),
+            pltpu.SemaphoreType.DMA((4,)),
         ],
         compiler_params=params,
         name="channelize",
     )(
-        *kept(
-            raw, proto, first, twiddle, second, masks, weight, expand, delays, owners.reshape(groups), widths,
-            space=pltpu.HBM,
-        )
+        *kept(raw, proto, tables, delays, owners.reshape(groups), widths, space=pltpu.HBM)
     )
     if n_tm == 2:
         own, other = msg, lax.ppermute(msg, "tm", [(0, 1), (1, 0)])
@@ -465,7 +481,7 @@
     out = pl.pallas_call(
         functools.partial(search, z),
         out_shape=pltpu.VMEM((n_dm * n_tm, z.capacity, trials, LANES), f32),
-        in_specs=[vmem_spec()] * 11 + [smem_spec()],
+        in_specs=[vmem_spec()] * 7 + [smem_spec()],
         out_specs=vmem_spec(),
         scratch_shapes=[
             pltpu.VMEM((DFT_A, (z.hist + 1) * LANES), bf16),
@@ -480,7 +496,7 @@
         compiler_params=params,
         name="search",
     )(
-        *kept(power, pr, band, own, other, first, twiddle, second, masks, weight, hits),
+        *kept(power, pr, band, own, other, tables, hits),
         *kept(owner, space=pltpu.SMEM),
     )
     recv = lax.all_to_all(out, ("dm", "tm"), split_axis=0, concat_axis=0, tiled=True)

time: 35.6 us -> 33.7 us (0.947)
  Pallas kernels: 16.1 us -> 14.2 us
    pallas_call x1, Pallas kernels: 11.6 us -> 9.69 us  [shards(): pl.pallas_call(functools.partial(channelize, z), out_shape=(pltpu.VMEM((z...]
where the time goes in v4:
time: 33.7 us; the launch traced here: 33.5 us
  Pallas kernels  14.2 us (42%)
  blocking collectives  12.7 us (38%)
  waiting for transfers between devices  3.59 us (11%)
  starting transfers between devices  3 us (9%)
    all_to_all x1, blocking collectives, shards(): lax.all_to_all(out, ('dm', 'tm'), split_axis=0, concat_axis=0, tiled=True)  12.7 us
    pallas_call x1, Pallas kernels, shards(): pl.pallas_call(functools.partial(channelize, z), out_shape=(pltpu.VMEM((z...  9.69 us
    ppermute x1, waiting for transfers between devices, shards(): own, other = (msg, lax.ppermute(msg, 'tm', [(0, 1), (1, 0)]))  3.59 us
    pallas_call x1, Pallas kernels, shards(): pl.pallas_call(functools.partial(search, z), out_shape=pltpu.VMEM((n_dm *...  3.48 us
    ppermute x1, starting transfers between devices, shards(): own, other = (msg, lax.ppermute(msg, 'tm', [(0, 1), (1, 0)]))  3 us
    pallas_call x1, Pallas kernels, shards(): pl.pallas_call(functools.partial(boxes, z), out_shape=jax.ShapeDtypeStruc...  1.01 us
  transfers between devices with their start and end apart: 1, of which 1 were waited for; matrix products, arithmetic and copies ran while one was open for 0% of the time, Pallas kernels for 0%

profile of v4, /device:TPU:0, one launch (start us, length us, event | category | flops | bytes accessed | tf_op | source)
XLA Modules:
  0.0 33.5 jit_solution(8287555918962493964)
XLA Ops:
  0.0 9.7 %channelize.1 = (f32[128,72,128]{2,1,0:T(8,128)S(1)}, f32[4,1,16384]{2,1,0:T(1,128)S(1)}, f32[72,128]{1,0:T(8,128)S(1)}, bf16[528,128]{1,0:T(8,128)(2,1)S(1)}, b...) custom-call(bf16[1,2097152]{1,0:T(2,128)(2,1)} %raw_ref.1, ...), custom_call_target="tpu_custom_call" | custom-call | tf_op jit(solution)/shard_map/channelize/pallas_call | solution.py:438
  9.7 3.0 %collective-permute-start = (bf16[528,128]{1,0:T(8,128)(2,1)S(1)}, bf16[528,128]{1,0:T(8,128)(2,1)S(1)}, u32[]{:S(2)}, u32[]{:S(2)}) collective-permute-start(bf16[528,128]{1,0:T(8,128)(2,1)S(1)} %get-tuple-element.16.own_ref), channel_id=1, source_target_pairs={{0,2},{2,0},{1,3},{3,1},{4,6},{6,4},{5,7},{7,5},{8,10},{10,8},{9,1... | collective-permute-start | bytes 405512 | tf_op jit(solution)/shard_map/ppermute | solution.py:470
  12.7 3.6 %collective-permute-done.other_ref = bf16[528,128]{1,0:T(8,128)(2,1)S(1)} collective-permute-done((bf16[528,128]{1,0:T(8,128)(2,1)S(1)}, bf16[528,128]{1,0:T(8,128)(2,1)S(1)}, u32[]{:S(2)}, u32[]{:S(2)}) %collective-permute-start) | collective-permute-done | bytes 135200 | tf_op jit(solution)/shard_map/ppermute | solution.py:470
  16.3 3.5 %search.1 = f32[8,4,4,128]{3,2,1,0:T(4,128)S(1)} custom-call(f32[128,72,128]{2,1,0:T(8,128)S(1)} %get-tuple-element.13.power_ref, f32[4,1,16384]{2,1,0:T(1,128)S(1)} %get-tuple-element.14.pr_ref, f32[72,128]{1,0:T(8,128)S(1)} %get-tuple-element.15.band_ref, bf16[528,128]{1,0:T(8,128)(2,1)S(1)} %get-tuple-element.16.own_ref, ...), custom_call_target="tpu_custom_call" | custom-call | tf_op jit(solution)/shard_map/search/pallas_call | solution.py:481
  19.8 12.7 %all_to_all.5.recv_ref = f32[8,4,4,128]{3,2,1,0:T(4,128)S(1)} all-to-all(f32[8,4,4,128]{3,2,1,0:T(4,128)S(1)} %search.1), channel_id=1, replica_groups=mesh['group'=2,'dm'=4,'tm'=2,'beam'=2] {'dm','tm'}, dimensions={0} | all-to-all | bytes 131072 | tf_op jit(solution)/shard_map/all_to_all | solution.py:502
  32.5 1.0 %boxes.1 = bf16[4,4,1,4,8,128]{5,4,3,2,1,0:T(8,128)(2,1)} custom-call(f32[8,4,4,128]{3,2,1,0:T(4,128)S(1)} %all_to_all.5.recv_ref, s32[8]{0:T(128)S(4)} %get-tuple-element.20.widths_ref), custom_call_target="tpu_custom_call" | custom-call | tf_op jit(solution)/shard_map/boxes/pallas_call | solution.py:503
Async XLA Ops:
  9.7 6.6 %collective-permute-start = (bf16[528,128]{1,0:T(8,128)(2,1)S(1)}, bf16[528,128]{1,0:T(8,128)(2,1)S(1)}, u32[]{:S(2)}, u32[]{:S(2)}) collective-permute-start(bf16[528,128]{1,0:T(8,128)(2,1)S(1)} %get-tuple-element.16.own_ref), channel_id=1, source_target_pairs={{0,2},{2,0},{1,3},{3,1},{4,6},{6,4},{5,7},{7,5},{8,10},{10,8},{9,1... | collective-permute-start | bytes 405512 | tf_op jit(solution)/shard_map/ppermute | solution.py:470

commit v5 on v4

--- a/solution.py
+++ b/solution.py
@@ -41,8 +41,10 @@
         self.hist = taps - 1
         self.raw_rows = self.hist * DFT_A
         self.bounds = n_tm - 1
-        self.msg_rows = self.bounds * self.raw_rows + 2 * self.rows
+        self.msg_rows = self.bounds * self.raw_rows + self.rows
         self.capacity = 2 * (groups // n_dm)
+        self.low_chunks = (spec - (WMAX - 1) - MAXT * TT - (FD - 1)) // CHUNK
+        self.high_rows = ceil_to(spec + FD - 1 - self.low_chunks * CHUNK, 16)
 
 
 def constants(z):
@@ -265,11 +267,8 @@
     widths_copy.wait()
 
 
-def search(z, power_ref, pr_ref, band_ref, own_ref, other_ref, tab_ref, hits_ref, owners_ref,
-           out_ref, y_ref, t_ref, bound_ref, inv_ref, weighted_ref, sums_ref, mean_ref, sub_ref):
+def boundary(z, power_ref, pr_ref, band_ref, own_ref, other_ref, tab_ref, y_ref, t_ref, bound_ref, inv_ref):
     me = lax.axis_index("tm")
-    groups, spec = z.groups, z.spec
-    chunks = spec // CHUNK
     total = band_ref[...]
     lo = z.bounds * z.raw_rows
     total = total + (
@@ -294,12 +293,17 @@
             bound_ref[b * z.hist + k] = power[k]
     scale = float(z.taps * z.channels)
     inv_ref[...] = 1.0 / (total * (1.0 / (z.spec * z.n_tm)) + 1e-6 * scale)
+
+
+def subbands(z, first, last, power_ref, bound_ref, inv_ref, tab_ref, weighted_ref, sums_ref, mean_ref, sub_ref):
+    me = lax.axis_index("tm")
+    groups = z.groups
     weighted_ref[...] = table(z, tab_ref, "weight").astype(jnp.float32)[: z.rows] * inv_ref[...]
     mine = jnp.maximum(me - 1, 0) * z.hist
 
     def power_of(i, k):
         value = power_ref[i * CHUNK + k]
-        if k < z.hist:
+        if first == 0 and k < z.hist:
             value = jnp.where(jnp.logical_and(me > 0, i == 0), bound_ref[mine + k], value)
         return value
 
@@ -337,7 +341,7 @@
             found = jnp.dot(masks, jnp.concatenate(flats[-2:], 1), preferred_element_type=jnp.float32)
             for half in range(2):
                 value = found[:, half * LANES : (half + 1) * LANES]
-                at = pl.multiple_of((i * CHUNK + k - 1 + half) * groups, 8)
+                at = pl.multiple_of(((i - first) * CHUNK + k - 1 + half) * groups, 8)
                 for m in range(2):
                     parts = [picked(m, step, value) for step in range(FD)]
                     sub_ref[m, pl.ds(at, groups)] = open_sums[m][0] + parts[0]
@@ -346,41 +350,98 @@
                         parts[step + 1] if later[step] is None else later[step] + parts[step + 1]
                         for step in range(FD - 1)
                     ]
-        means(jnp.minimum(i + 1, chunks - 1))
+        means(jnp.minimum(i + 1, last - 1))
         return tuple(tuple(value) for value in open_sums)
 
-    means(0)
+    means(first)
     empty = jnp.zeros((groups, LANES), jnp.float32)
-    carry = lax.fori_loop(0, chunks, flat_step, ((empty,) * (FD - 1),) * 2)
-    length = spec + FD - 1
-    stop = ceil_to(length, 16)
+    return lax.fori_loop(first, last, flat_step, ((empty,) * (FD - 1),) * 2)
+
+
+def delayed(z, hits, series):
+    lane = lax.broadcasted_iota(jnp.int32, (8, LANES), 1)
+    found = lax.dot_general(hits, series, (((1,), (1,)), ((), ())), preferred_element_type=jnp.float32)
+    total = found[:8]
+    for value in range(1, MAXT + 1):
+        moved = pltpu.roll(found[value * 8 : value * 8 + 8], value * TT, 1)
+        total = total + jnp.where(lane >= value * TT, moved, 0.0)
+    return total
+
+
+def tails(z, power_ref, pr_ref, band_ref, own_ref, other_ref, tab_ref, hits_ref,
+          prev_ref, high_ref, bound_ref, inv_ref, y_ref, t_ref, late_ref, weighted_ref, sums_ref, mean_ref):
+    groups = z.groups
+    boundary(z, power_ref, pr_ref, band_ref, own_ref, other_ref, tab_ref, y_ref, t_ref, bound_ref, inv_ref)
+    carry = subbands(
+        z, z.low_chunks, z.spec // CHUNK, power_ref, bound_ref, inv_ref, tab_ref, weighted_ref, sums_ref, mean_ref, high_ref
+    )
+    count = z.high_rows
+    done = z.spec - z.low_chunks * CHUNK
     for m in range(2):
         for step in range(FD - 1):
-            sub_ref[m, (spec + step) * groups : (spec + step + 1) * groups] = carry[m][step]
-    sub_ref[:, length * groups :] = jnp.zeros((2, (stop - length) * groups, LANES), jnp.float32)
-    trials = out_ref.shape[2]
-    out_ref[...] = jnp.zeros_like(out_ref)
-    wide = 2 * LANES
-    blank = jnp.zeros((wide - stop, wide), jnp.bfloat16)
+            high_ref[m, (done + step) * groups : (done + step + 1) * groups] = carry[m][step]
+    high_ref[:, (done + FD - 1) * groups :] = jnp.zeros((2, (count - done - FD + 1) * groups, LANES), jnp.float32)
+    blank = jnp.zeros((LANES - count, 2 * LANES), jnp.bfloat16)
+    trials = late_ref.shape[1]
+    lane = lax.broadcasted_iota(jnp.int32, (8, LANES), 1)
+    start = done - (WMAX - 1)
     for g in range(groups):
-        both = [sub_ref[m, pl.ds(g, stop, stride=groups)].astype(jnp.bfloat16) for m in range(2)]
-        series = jnp.concatenate([jnp.concatenate(both, 1), blank])
-        found = lax.dot_general(hits_ref[g], series, (((1,), (1,)), ((), ())), preferred_element_type=jnp.float32)
-        dd = found[:8]
-        for value in range(1, MAXT + 1):
-            dd = dd + pltpu.roll(found[value * 8 : value * 8 + 8], value * TT, 1)
+        both = [high_ref[m, pl.ds(g, count, stride=groups)].astype(jnp.bfloat16) for m in range(2)]
+        dd = delayed(z, hits_ref[g], jnp.concatenate([jnp.concatenate(both, 1), blank]))
+        late = pltpu.roll(dd, LANES - start, 1)
+        late_ref[g] = jnp.where(lane < WMAX - 1 + MAXT * TT + FD - 1, late, 0.0)[:trials]
+    prev_ref[...] = late_ref[...].reshape(groups * trials, LANES).astype(jnp.bfloat16)
+
+
+def bulk(z, power_ref, bound_ref, inv_ref, tab_ref, hits_ref, high_ref,
+         main_ref, weighted_ref, sums_ref, mean_ref, low_ref, join_ref):
+    groups = z.groups
+    carry = subbands(z, 0, z.low_chunks, power_ref, bound_ref, inv_ref, tab_ref, weighted_ref, sums_ref, mean_ref, low_ref)
+    join_ref[...] = jnp.zeros_like(join_ref)
+    for m in range(2):
+        for step in range(FD - 1):
+            join_ref[m, step * groups : (step + 1) * groups] = carry[m][step]
+    low = z.low_chunks * CHUNK
+    trials = main_ref.shape[1]
+    for g in range(groups):
+        both = []
+        for m in range(2):
+            edge = high_ref[m, pl.ds(g, 8, stride=groups)] + join_ref[m, pl.ds(g, 8, stride=groups)]
+            rest = high_ref[m, pl.ds(8 * groups + g, z.spec - low - 8, stride=groups)]
+            both.append(jnp.concatenate([low_ref[m, pl.ds(g, low, stride=groups)], edge, rest]).astype(jnp.bfloat16))
+        main_ref[g] = delayed(z, hits_ref[g], jnp.concatenate(both, 1))[:trials]
+
+
+def parcels(z, main_ref, prev_ref, owners_ref, stay_ref, leave_ref, late_ref, all_ref):
+    me = lax.axis_index("dm")
+    all_ref[...] = jnp.zeros_like(all_ref)
+    late_ref[...] = prev_ref[...].astype(jnp.float32).reshape(late_ref.shape)
+    for g in range(z.groups):
         owner = owners_ref[g]
         rank = jnp.int32(0)
         for earlier in range(g):
             rank = rank + jnp.where(owners_ref[earlier] == owner, 1, 0)
-        late = pltpu.roll(dd, wide - (spec - WMAX + 1), 1)
-        out_ref[owner * z.n_tm + jnp.minimum(me + 1, z.n_tm - 1), rank] = late[:trials, :LANES]
-        out_ref[owner * z.n_tm + me, rank] = dd[:trials, :LANES]
-
-
-def boxes(z, recv_ref, widths_ref, out_ref, d_ref):
-    me = lax.axis_index("tm")
-    trials = recv_ref.shape[2]
+        all_ref[owner ^ me, 0, rank] = main_ref[g]
+        all_ref[owner ^ me, 1, rank] = late_ref[g]
+    for r in range(z.n_dm):
+        value = all_ref[r].reshape(stay_ref.shape[2:]).astype(jnp.bfloat16)
+        (leave_ref if r % 2 else stay_ref)[r // 2, 0] = value
+
+
+def relay(held_ref, got_ref, stay_ref, leave_ref):
+    count = held_ref.shape[1]
+    for r in range(held_ref.shape[0]):
+        target = leave_ref if r % 2 else stay_ref
+        target[r // 2, :count] = held_ref[r]
+        target[r // 2, count:] = got_ref[r]
+
+
+def boxes(z, widths_ref, *refs):
+    held_ref, got_ref, out_ref, d_ref = refs
+    early = lax.axis_index("tm") == 0
+    me = lax.axis_index("dm")
+    trials = out_ref.shape[3]
+    near = held_ref.shape[1]
     rank = lax.broadcasted_iota(jnp.int32, (8, LANES), 0)
     count = widths_ref.shape[0]
     width = jnp.zeros((8, LANES), jnp.int32)
@@ -389,25 +450,23 @@
     norm = 1.0 / jnp.sqrt(width.astype(jnp.float32))
     weights = [jnp.where(width > lag, norm, 0.0) for lag in range(WMAX)]
     prior = WMAX - 1
-    zero = jnp.zeros((8, LANES), jnp.float32)
-    before = jnp.maximum(me - 1, 0)
     rows = z.capacity * trials
-    for d in range(z.n_dm):
-        own = recv_ref[d * z.n_tm + me].reshape(rows, LANES)
-        past = recv_ref[d * z.n_tm + before].reshape(rows, LANES)
-        past = jnp.where(me > 0, past, 0.0)
+    for r in range(z.n_dm):
+        ref, at = (held_ref, r) if r < near else (got_ref, r - near)
+        own = ref[0, at, :rows].astype(jnp.float32)
+        past = jnp.where(early, 0.0, ref[0, at, rows:].astype(jnp.float32))
         wide = jnp.concatenate([own, jnp.zeros_like(own)], 1)
         wide = pltpu.roll(wide, prior, 1) + jnp.concatenate([past, jnp.zeros_like(past)], 1)
         for lag in range(WMAX):
             shift = prior - lag
-            d_ref[lag] = (pltpu.roll(wide, 2 * LANES - shift, 1) if shift else wide)[:, :LANES]
+            d_ref[r, lag] = (pltpu.roll(wide, 2 * LANES - shift, 1) if shift else wide)[:, :LANES]
         for s in range(z.capacity):
             for j in range(trials):
                 acc = None
                 for lag in range(WMAX):
-                    part = d_ref[lag, s * trials + j : s * trials + j + 1, :] * weights[lag]
+                    part = d_ref[r, lag, s * trials + j : s * trials + j + 1, :] * weights[lag]
                     acc = part if acc is None else acc + part
-                out_ref[s, d, 0, j] = acc[:count].astype(jnp.bfloat16)
+                out_ref[s, me ^ r, 0, j] = acc[:count].astype(jnp.bfloat16)
 
 
 def vmem_spec():
@@ -477,38 +536,79 @@
         high = rest.astype(bf16)
         pair = jnp.concatenate([high, (rest - high.astype(f32)).astype(bf16)])
         own, other = jnp.concatenate([lasts, pair]), jnp.concatenate([firsts, pair])
-    length = ceil_to(z.spec + FD - 1, 16)
-    out = pl.pallas_call(
-        functools.partial(search, z),
-        out_shape=pltpu.VMEM((n_dm * n_tm, z.capacity, trials, LANES), f32),
-        in_specs=[vmem_spec()] * 7 + [smem_spec()],
-        out_specs=vmem_spec(),
+    work = [
+        pltpu.VMEM((z.rows, LANES), f32),
+        pltpu.VMEM((CHUNK * 8, LANES), f32),
+        pltpu.VMEM((z.spec, LANES), f32),
+    ]
+    prev, high, bound, inv = pl.pallas_call(
+        functools.partial(tails, z),
+        out_shape=(
+            pltpu.VMEM((groups * trials, LANES), bf16),
+            pltpu.VMEM((2, z.high_rows * groups, LANES), f32),
+            pltpu.VMEM((z.bounds * z.hist, z.rows, LANES), f32),
+            pltpu.VMEM((z.rows, LANES), f32),
+        ),
+        in_specs=[vmem_spec()] * 7,
+        out_specs=[vmem_spec()] * 4,
         scratch_shapes=[
             pltpu.VMEM((DFT_A, (z.hist + 1) * LANES), bf16),
             pltpu.VMEM((z.hist * z.rows16, 2 * LANES), bf16),
-            pltpu.VMEM((z.bounds * z.hist, z.rows, LANES), f32),
-            pltpu.VMEM((z.rows, LANES), f32),
-            pltpu.VMEM((z.rows, LANES), f32),
-            pltpu.VMEM((CHUNK * 8, LANES), f32),
-            pltpu.VMEM((z.spec, LANES), f32),
-            pltpu.VMEM((2, length * groups, LANES), f32),
+            pltpu.VMEM((groups, trials, LANES), f32),
+        ]
+        + work,
+        compiler_params=params,
+        name="tails",
+    )(*kept(power, pr, band, own, other, tables, hits))
+    before = lax.ppermute(prev, "tm", [(i, (i + 1) % n_tm) for i in range(n_tm)])
+    main = pl.pallas_call(
+        functools.partial(bulk, z),
+        out_shape=pltpu.VMEM((groups, trials, LANES), f32),
+        in_specs=[vmem_spec()] * 6,
+        out_specs=vmem_spec(),
+        scratch_shapes=work
+        + [
+            pltpu.VMEM((2, z.low_chunks * CHUNK * groups, LANES), f32),
+            pltpu.VMEM((2, 8 * groups, LANES), f32),
         ],
         compiler_params=params,
-        name="search",
-    )(
-        *kept(power, pr, band, own, other, tables, hits),
-        *kept(owner, space=pltpu.SMEM),
-    )
-    recv = lax.all_to_all(out, ("dm", "tm"), split_axis=0, concat_axis=0, tiled=True)
+        cost_estimate=pl.CostEstimate(flops=10**9, bytes_accessed=8 * 10**6, transcendentals=0),
+        name="bulk",
+    )(*kept(power, bound, inv, tables, hits, high))
+    slots = (2, z.capacity, trials, LANES)
+    parcel = (2 * z.capacity * trials, LANES)
+    held, leaving = pl.pallas_call(
+        functools.partial(parcels, z),
+        out_shape=(pltpu.VMEM((n_dm // 2, 1, *parcel), bf16),) * 2,
+        in_specs=[vmem_spec()] * 2 + [smem_spec()],
+        out_specs=[vmem_spec()] * 2,
+        scratch_shapes=[pltpu.VMEM((groups, trials, LANES), f32), pltpu.VMEM((n_dm, *slots), f32)],
+        compiler_params=params,
+        name="parcels",
+    )(*kept(main, before), *kept(owner, space=pltpu.SMEM))
+    bit = 1
+    while True:
+        got = lax.ppermute(leaving, "dm", [(i, i ^ bit) for i in range(n_dm)])
+        bit *= 2
+        if bit == n_dm:
+            break
+        held, leaving = pl.pallas_call(
+            relay,
+            out_shape=(pltpu.VMEM((n_dm // 2 // bit, bit, *parcel), bf16),) * 2,
+            in_specs=[vmem_spec()] * 2,
+            out_specs=[vmem_spec()] * 2,
+            compiler_params=params,
+            name="relay",
+        )(*kept(held, got))
     return pl.pallas_call(
         functools.partial(boxes, z),
         out_shape=jax.ShapeDtypeStruct((z.capacity, n_dm, 1, trials, widths.shape[0], z.spec), bf16),
-        in_specs=[vmem_spec(), smem_spec()],
+        in_specs=[smem_spec()] + [vmem_spec()] * 2,
         out_specs=vmem_spec(),
-        scratch_shapes=[pltpu.VMEM((WMAX, z.capacity * trials, LANES), f32)],
+        scratch_shapes=[pltpu.VMEM((n_dm, WMAX, z.capacity * trials, LANES), f32)],
         compiler_params=params,
         name="boxes",
-    )(*kept(recv), *kept(width, space=pltpu.SMEM))
+    )(*kept(width, space=pltpu.SMEM), *kept(held, got))
 
 
 def solution(mesh):

time: 33.7 us -> 31.6 us (0.938)
  blocking collectives: 12.7 us -> 0 us
  starting transfers between devices: 3 us -> 9.12 us
  waiting for transfers between devices: 3.59 us -> 7.7 us
  Pallas kernels: 14.2 us -> 14.6 us
    all_to_all x1 -> x0, blocking collectives: 12.7 us -> none  [shards(): lax.all_to_all(out, ('dm', 'tm'), split_axis=0, concat_axis=0, tiled=True)]
    ppermute x0 -> x3, starting transfers between devices: none -> 6.12 us  [the longest x2 4.34 us: shards(): got = lax.ppermute(leaving, 'dm', [(i, i ^ bit) for i in range(n_dm)])]
    ppermute x0 -> x3, waiting for transfers between devices: none -> 4.11 us  [the longest x2 4.1 us: shards(): got = lax.ppermute(leaving, 'dm', [(i, i ^ bit) for i in range(n_dm)])]
    pallas_call x1 -> x4, Pallas kernels: 3.48 us -> 4 us  [the longest x1 2.09 us: shards(): pl.pallas_call(functools.partial(bulk, z), out_shape=pltpu.VMEM((groups,...]
  transfers between devices with their start and end apart: 1 -> 4, of which waited for: 1 -> 3; matrix products, arithmetic and copies ran while one was open for 0% -> 0% of each run, Pallas kernels for 0% -> 7%
where the time goes in v5:
time: 31.6 us; the launch traced here: 31.4 us
  Pallas kernels  14.6 us (46%)
  starting transfers between devices  9.12 us (29%)
  waiting for transfers between devices  7.7 us (24%)
    pallas_call x1, Pallas kernels, shards(): pl.pallas_call(functools.partial(channelize, z), out_shape=(pltpu.VMEM((z...  9.6 us
    ppermute x2, starting transfers between devices, shards(): got = lax.ppermute(leaving, 'dm', [(i, i ^ bit) for i in range(n_dm)])  4.34 us
    ppermute x2, waiting for transfers between devices, shards(): got = lax.ppermute(leaving, 'dm', [(i, i ^ bit) for i in range(n_dm)])  4.1 us
    ppermute x1, waiting for transfers between devices, shards(): own, other = (msg, lax.ppermute(msg, 'tm', [(0, 1), (1, 0)]))  3.6 us
    ppermute x1, starting transfers between devices, shards(): own, other = (msg, lax.ppermute(msg, 'tm', [(0, 1), (1, 0)]))  3 us
    pallas_call x1, Pallas kernels, shards(): pl.pallas_call(functools.partial(bulk, z), out_shape=pltpu.VMEM((groups,...  2.09 us
    pallas_call x1, Pallas kernels, shards(): pl.pallas_call(functools.partial(tails, z), out_shape=(pltpu.VMEM((groups...  1.84 us
    ppermute x1, starting transfers between devices, shards(): lax.ppermute(prev, 'tm', [(i, (i + 1) % n_tm) for i in range(n_tm)])  1.78 us
  transfers between devices with their start and end apart: 4, of which 3 were waited for; matrix products, arithmetic and copies ran while one was open for 0% of the time, Pallas kernels for 7%

profile of v5, /device:TPU:0, one launch (start us, length us, event | category | flops | bytes accessed | tf_op | source)
XLA Modules:
  0.0 31.4 jit_solution(8367860821293906345)
XLA Ops:
  0.0 9.6 %channelize.1 = (f32[128,72,128]{2,1,0:T(8,128)S(1)}, f32[4,1,16384]{2,1,0:T(1,128)S(1)}, f32[72,128]{1,0:T(8,128)S(1)}, bf16[528,128]{1,0:T(8,128)(2,1)S(1)}, b...) custom-call(bf16[1,2097152]{1,0:T(2,128)(2,1)} %raw_ref.1, ...), custom_call_target="tpu_custom_call" | custom-call | tf_op jit(solution)/shard_map/channelize/pallas_call | solution.py:497
  9.6 3.0 %collective-permute-start = (bf16[528,128]{1,0:T(8,128)(2,1)S(1)}, bf16[528,128]{1,0:T(8,128)(2,1)S(1)}, u32[]{:S(2)}, u32[]{:S(2)}) collective-permute-start(bf16[528,128]{1,0:T(8,128)(2,1)S(1)} %get-tuple-element.25.own_ref), channel_id=1, source_target_pairs={{0,2},{2,0},{1,3},{3,1},{4,6},{6,4},{5,7},{7,5},{8,10},{10,8},{9,1... | collective-permute-start | bytes 405512 | tf_op jit(solution)/shard_map/ppermute | solution.py:529
  12.6 3.6 %collective-permute-done.other_ref = bf16[528,128]{1,0:T(8,128)(2,1)S(1)} collective-permute-done((bf16[528,128]{1,0:T(8,128)(2,1)S(1)}, bf16[528,128]{1,0:T(8,128)(2,1)S(1)}, u32[]{:S(2)}, u32[]{:S(2)}) %collective-permute-start) | collective-permute-done | bytes 135200 | tf_op jit(solution)/shard_map/ppermute | solution.py:529
  16.2 1.8 %tails.1 = (bf16[32,128]{1,0:T(8,128)(2,1)S(1)}, f32[2,512,128]{2,1,0:T(8,128)S(1)}, f32[3,72,128]{2,1,0:T(8,128)S(1)}, f32[72,128]{1,0:T(8,128)S(1)}) custom-call(f32[128,72,128]{2,1,0:T(8,128)S(1)} %get-tuple-element.22.power_ref, f32[4,1,16384]{2,1,0:T(1,128)S(1)} %get-tuple-element.23.pr_ref, f32[72,128]{1,0:T(8,128)S(1)} %get-tuple-element.24.band_ref, ...), custom_call_target="tpu_custom_call" | custom-call | tf_op jit(solution)/shard_map/tails/pallas_call | solution.py:544
  18.0 1.8 %collective-permute-start.1 = (bf16[32,128]{1,0:T(8,128)(2,1)S(1)}, bf16[32,128]{1,0:T(8,128)(2,1)S(1)}, u32[]{:S(2)}, u32[]{:S(2)}) collective-permute-start(bf16[32,128]{1,0:T(8,128)(2,1)S(1)} %get-tuple-element.31), channel_id=1, source_target_pairs={{0,2},{2,0},{1,3},{3,1},{4,6},{6,4},{5,7},{7,5},{8,10},{10,8},{9,1... | collective-permute-start | bytes 24584 | tf_op jit(solution)/shard_map/ppermute | solution.py:563
  19.8 2.1 %bulk.1.main_ref = f32[8,4,128]{2,1,0:T(4,128)S(1)} custom-call(f32[128,72,128]{2,1,0:T(8,128)S(1)} %get-tuple-element.22.power_ref, f32[3,72,128]{2,1,0:T(8,128)S(1)} %get-tuple-element.28.bound_ref, f32[72,128]{1,0:T(8,128)S(1)} %get-tuple-element.29.inv_ref, bf16[1152,128]{1,0:T(8,128)(2,1)S(1)} %get-tuple-element.26.tab_ref, ...), custom_call_target="tpu_custom_call" | custom-call | flops 1000000000 | bytes 8000000 | tf_op jit(solution)/shard_map/bulk/pallas_call | solution.py:564
  21.9 0.0 collective-permute-done.1.prev_ref
  21.9 0.1 parcels.1
  22.0 1.7 %collective-permute-start.2 = (bf16[2,1,32,128]{3,2,1,0:T(8,128)(2,1)S(1)}, bf16[2,1,32,128]{3,2,1,0:T(8,128)(2,1)S(1)}, u32[]{:S(2)}, u32[]{:S(2)}) collective-permute-start(bf16[2,1,32,128]{3,2,1,0:T(8,128)(2,1)S(1)} %get-tuple-element.34), channel_id=1, source_target_pairs={{0,4},{4,0},{8,12},{12,8},{1,5},{5,1},{9,13},{13,9},{2,6},{6,2},{1... | collective-permute-start | bytes 49160 | tf_op jit(solution)/shard_map/ppermute | solution.py:591
  23.7 2.1 %collective-permute-done.2.got_ref = bf16[2,1,32,128]{3,2,1,0:T(8,128)(2,1)S(1)} collective-permute-done((bf16[2,1,32,128]{3,2,1,0:T(8,128)(2,1)S(1)}, bf16[2,1,32,128]{3,2,1,0:T(8,128)(2,1)S(1)}, u32[]{:S(2)}, u32[]{:S(2)}) %collective-permute-start.2) | collective-permute-done | bytes 16416 | tf_op jit(solution)/shard_map/ppermute | solution.py:591
  25.8 2.7 %collective-permute-start.3 = (bf16[1,2,32,128]{3,2,1,0:T(8,128)(2,1)S(1)}, bf16[1,2,32,128]{3,2,1,0:T(8,128)(2,1)S(1)}, u32[]{:S(2)}, u32[]{:S(2)}) collective-permute-start(bf16[1,2,32,128]{3,2,1,0:T(8,128)(2,1)S(1)} %get-tuple-element.36), channel_id=1, source_target_pairs={{0,8},{4,12},{8,0},{12,4},{1,9},{5,13},{9,1},{13,5},{2,10},{6,14},... | collective-permute-start | bytes 49160 | tf_op jit(solution)/shard_map/ppermute | solution.py:591
  28.5 2.0 %collective-permute-done.3.refs_1_ = bf16[1,2,32,128]{3,2,1,0:T(8,128)(2,1)S(1)} collective-permute-done((bf16[1,2,32,128]{3,2,1,0:T(8,128)(2,1)S(1)}, bf16[1,2,32,128]{3,2,1,0:T(8,128)(2,1)S(1)}, u32[]{:S(2)}, u32[]{:S(2)}) %collective-permute-start.3) | collective-permute-done | bytes 16416 | tf_op jit(solution)/shard_map/ppermute | solution.py:591
  30.5 1.0 %boxes.1 = bf16[4,4,1,4,8,128]{5,4,3,2,1,0:T(8,128)(2,1)} custom-call(s32[8]{0:T(128)S(4)} %get-tuple-element.21.widths_ref, bf16[1,2,32,128]{3,2,1,0:T(8,128)(2,1)S(1)} %get-tuple-element.35.refs_0_, bf16[1,2,32,128]{3,2,1,0:T(8,128)(2,1)S(1)} %collective-permute-done.3.refs_1_), custom_call_target="tpu_custom_call" | custom-call | tf_op jit(solution)/shard_map/boxes/pallas_call | solution.py:603
  (1 shorter events, 0.0 us)
Async XLA Ops:
  9.6 6.6 %collective-permute-start = (bf16[528,128]{1,0:T(8,128)(2,1)S(1)}, bf16[528,128]{1,0:T(8,128)(2,1)S(1)}, u32[]{:S(2)}, u32[]{:S(2)}) collective-permute-start(bf16[528,128]{1,0:T(8,128)(2,1)S(1)} %get-tuple-element.25.own_ref), channel_id=1, source_target_pairs={{0,2},{2,0},{1,3},{3,1},{4,6},{6,4},{5,7},{7,5},{8,10},{10,8},{9,1... | collective-permute-start | bytes 405512 | tf_op jit(solution)/shard_map/ppermute | solution.py:529
  18.0 3.9 %collective-permute-start.1 = (bf16[32,128]{1,0:T(8,128)(2,1)S(1)}, bf16[32,128]{1,0:T(8,128)(2,1)S(1)}, u32[]{:S(2)}, u32[]{:S(2)}) collective-permute-start(bf16[32,128]{1,0:T(8,128)(2,1)S(1)} %get-tuple-element.31), channel_id=1, source_target_pairs={{0,2},{2,0},{1,3},{3,1},{4,6},{6,4},{5,7},{7,5},{8,10},{10,8},{9,1... | collective-permute-start | bytes 24584 | tf_op jit(solution)/shard_map/ppermute | solution.py:563
  22.0 3.8 %collective-permute-start.2 = (bf16[2,1,32,128]{3,2,1,0:T(8,128)(2,1)S(1)}, bf16[2,1,32,128]{3,2,1,0:T(8,128)(2,1)S(1)}, u32[]{:S(2)}, u32[]{:S(2)}) collective-permute-start(bf16[2,1,32,128]{3,2,1,0:T(8,128)(2,1)S(1)} %get-tuple-element.34), channel_id=1, source_target_pairs={{0,4},{4,0},{8,12},{12,8},{1,5},{5,1},{9,13},{13,9},{2,6},{6,2},{1... | collective-permute-start | bytes 49160 | tf_op jit(solution)/shard_map/ppermute | solution.py:591
  25.8 4.6 %collective-permute-start.3 = (bf16[1,2,32,128]{3,2,1,0:T(8,128)(2,1)S(1)}, bf16[1,2,32,128]{3,2,1,0:T(8,128)(2,1)S(1)}, u32[]{:S(2)}, u32[]{:S(2)}) collective-permute-start(bf16[1,2,32,128]{3,2,1,0:T(8,128)(2,1)S(1)} %get-tuple-element.36), channel_id=1, source_target_pairs={{0,8},{4,12},{8,0},{12,4},{1,9},{5,13},{9,1},{13,5},{2,10},{6,14},... | collective-permute-start | bytes 49160 | tf_op jit(solution)/shard_map/ppermute | solution.py:591

commit v6 on v5

--- a/solution.py
+++ b/solution.py
@@ -35,13 +35,12 @@
         self.taps, self.channels, self.spec, self.groups = taps, channels, spec, groups
         self.n_dm, self.n_tm = n_dm, n_tm
         self.side = channels // DFT_A
-        self.half = DFT_A // 2 + 1
-        self.rows = ceil_to(self.half, 8)
-        self.rows16 = ceil_to(self.half, 16)
+        self.rows = DFT_A // 2
+        self.deep = self.rows + 16
+        self.band_rows = self.rows + 8
         self.hist = taps - 1
         self.raw_rows = self.hist * DFT_A
         self.bounds = n_tm - 1
-        self.msg_rows = self.bounds * self.raw_rows + self.rows
         self.capacity = 2 * (groups // n_dm)
         self.low_chunks = (spec - (WMAX - 1) - MAXT * TT - (FD - 1)) // CHUNK
         self.high_rows = ceil_to(spec + FD - 1 - self.low_chunks * CHUNK, 16)
@@ -49,11 +48,14 @@
 
 def constants(z):
     cos_a, sin_a = angle_tables(DFT_A, DFT_A, DFT_A)
-    first = np.zeros((2 * z.rows, DFT_A))
-    first[: z.half] = cos_a[: z.half]
-    first[z.rows : z.rows + z.half] = -sin_a[: z.half]
-    tw_cos, tw_sin = np.zeros((2, z.rows16, z.side))
-    tw_cos[: z.half], tw_sin[: z.half] = angle_tables(z.half, z.side, z.channels)
+    first = np.concatenate([cos_a[: z.rows], -sin_a[: z.rows]])
+    first[z.rows] = cos_a[z.rows]
+    tw_cos, tw_sin = angle_tables(z.rows + 1, z.side, z.channels)
+    edge = np.zeros((16, z.side))
+    edge[0], edge[1] = tw_cos[z.rows], -tw_sin[z.rows]
+    tw_cos, tw_sin = tw_cos[: z.rows], tw_sin[: z.rows]
+    hidden = tw_cos.copy()
+    hidden[0] = 0
     cos_b, sin_b = angle_tables(z.side, z.side, z.side)
     width = z.channels // NBLK
     fine = np.arange(z.groups)[:, None] * FD * (width - 1 - np.arange(width))[None, :] // (z.groups * (width - 1))
@@ -62,11 +64,11 @@
     for step in range(FD):
         for parity in range(parities):
             hit = fine[:, parity * DFT_A : (parity + 1) * DFT_A] == step
-            masks[0, step, parity, :, : z.half] = hit[:, : z.half]
-            masks[1, step, parity, :, 1 : z.half - 1] = hit[:, : z.half - 1 : -1]
-    weight = np.zeros((z.rows16, LANES))
-    weight[: z.half] = 2.0 / z.channels
-    weight[0] = weight[z.half - 1] = 1.0 / z.channels
+            masks[0, step, parity, :, : z.rows] = hit[:, : z.rows]
+            masks[0, step, parity, :, z.rows : z.deep] = hit[:, z.rows, None]
+            masks[1, step, parity, :, 1 : z.rows] = hit[:, : z.rows : -1]
+    weight = np.full((z.deep, LANES), 2.0 / z.channels)
+    weight[0] = weight[z.rows] = 1.0 / z.channels
     expand = np.zeros((NBLK, 2 * z.side))
     lane = np.arange(z.side)
     expand[lane // parities, lane] = 1
@@ -74,6 +76,8 @@
     tables = {
         "first": first,
         "cos": tw_cos,
+        "hidden": hidden,
+        "edge": edge,
         "sin": tw_sin,
         "second": np.concatenate([cos_b, sin_b]),
         "second_im": np.concatenate([-sin_b, cos_b]),
@@ -123,53 +127,67 @@
                 save(k, block, window[k])
 
 
-def transform(z, y_ref, tab_ref, t_refs, count):
-    pad = jnp.zeros((z.rows16 - z.rows, LANES), jnp.float32)
-    cos, sin = table(z, tab_ref, "cos"), table(z, tab_ref, "sin")
+def transform(z, y_ref, tab_ref, t_refs, edge_ref, count):
+    cos, hidden, sin = (table(z, tab_ref, name) for name in ("cos", "hidden", "sin"))
     part = count // len(t_refs)
     out = []
     for index, t_ref in enumerate(t_refs):
         for at in range(0, part, 2):
             pair = min(2, part - at)
             lane = (index * part + at) * LANES
-            a = jnp.dot(table(z, tab_ref, "first"), y_ref[:, lane : lane + pair * LANES], preferred_element_type=jnp.float32)
+            a = jnp.dot(
+                table(z, tab_ref, "first"), y_ref[:, lane : lane + pair * LANES], preferred_element_type=jnp.float32
+            )
             for k in range(pair):
                 lanes = slice(k * LANES, (k + 1) * LANES)
-                re = jnp.concatenate([a[: z.rows, lanes], pad]).astype(jnp.bfloat16)
-                im = jnp.concatenate([a[z.rows :, lanes], pad]).astype(jnp.bfloat16)
-                rows = slice((at + k) * z.rows16, (at + k + 1) * z.rows16)
+                edge_ref[index * part + at + k : index * part + at + k + 1] = a[z.rows : z.rows + 1, lanes]
+                re, im = a[: z.rows, lanes].astype(jnp.bfloat16), a[z.rows :, lanes].astype(jnp.bfloat16)
+                rows = slice((at + k) * z.rows, (at + k + 1) * z.rows)
                 t_ref[rows, :LANES] = re * cos + im * sin
-                t_ref[rows, LANES:] = im * cos - re * sin
-        c = jnp.dot(t_ref[...], wide_table(z, tab_ref, "second"), preferred_element_type=jnp.float32)
+                t_ref[rows, LANES:] = im * hidden - re * sin
+        last = index + 1 == len(t_refs)
+        if last:
+            turn = table(z, tab_ref, "edge").astype(jnp.float32)
+            rows = slice(part * z.rows, part * z.rows + 16)
+            t_ref[rows, :LANES] = (edge_ref[...] * turn[0:1]).astype(jnp.bfloat16)
+            t_ref[rows, LANES:] = (edge_ref[...] * turn[1:2]).astype(jnp.bfloat16)
+        c = jnp.dot(
+            t_ref[: part * z.rows + (16 if last else 0)], wide_table(z, tab_ref, "second"),
+            preferred_element_type=jnp.float32,
+        )
         for k in range(part):
-            rows = c[k * z.rows16 : k * z.rows16 + z.rows]
+            rows = c[k * z.rows : (k + 1) * z.rows]
             re, im = rows[:, :LANES], rows[:, LANES:]
             out.append(re * re + im * im)
-    return out
+    re, im = c[part * z.rows :, :LANES], c[part * z.rows :, LANES:]
+    return out, re * re + im * im
 
 
 def channelize(z, raw_ref, proto_ref, tab_in, delays_ref, owners_in, widths_in,
-               power_ref, pr_ref, band_ref, msg_ref, tab_ref, hits_ref, owners_ref, widths_ref,
-               buf, trial_ref, hist_ref, y0_ref, y1_ref, t0_ref, t1_ref, t2_ref, t3_ref, sems):
+               power_ref, edges_ref, pr_ref, band_ref, msg_ref, tab_ref, trial_ref, owners_ref, widths_ref,
+               buf, hist_ref, y0_ref, y1_ref, t0_ref, t1_ref, t2_ref, t3_ref, e0_ref, e1_ref, sum_ref, sems):
     chunks = z.spec // CHUNK
     span = CHUNK * z.channels
 
-    def raw_copy(i, side):
-        part = pl.ds(pl.multiple_of(i * span, span), span)
+    def raw_copy(first, last, side):
+        part = pl.ds(first * span, (last - first) * span)
         return pltpu.make_async_copy(raw_ref.at[:, part], buf.at[:, part], sems.at[side])
 
     tab_copy = pltpu.make_async_copy(tab_in, tab_ref, sems.at[2])
     delays_copy = pltpu.make_async_copy(delays_ref, trial_ref, sems.at[2])
     owners_copy = pltpu.make_async_copy(owners_in, owners_ref, sems.at[3])
     widths_copy = pltpu.make_async_copy(widths_in, widths_ref, sems.at[3])
-    raw_copy(0, 0).start()
+    early_copies = [raw_copy(0, 1, 0), raw_copy(1, 3, 1), raw_copy(3, 5, 4), raw_copy(5, chunks, 0)]
+    early_copies[0].start()
     for tap in range(z.taps):
         pltpu.make_async_copy(proto_ref.at[tap : tap + 1], pr_ref.at[tap], sems.at[3]).start()
     tab_copy.start()
-    raw_copy(1, 1).start()
+    early_copies[1].start()
     hist_ref[...] = jnp.zeros_like(hist_ref)
     band_ref[...] = jnp.zeros_like(band_ref)
+    sum_ref[...] = jnp.zeros_like(sum_ref)
     early = lax.axis_index("tm") > 0
+    place = lax.broadcasted_iota(jnp.int32, (16, LANES), 0)
 
     def frames(i, y_ref):
         base = i * span
@@ -189,8 +207,8 @@
 
         fill_frames(z, history, load, pr_ref, y_ref, CHUNK, save)
 
-    def powers(i, y_ref, t_refs):
-        power = transform(z, y_ref, tab_ref, t_refs, CHUNK)
+    def powers(i, y_ref, t_refs, e_ref):
+        power, edges = transform(z, y_ref, tab_ref, t_refs, e_ref, CHUNK)
         late = power[z.hist]
         for k in range(z.hist + 1, CHUNK):
             late = late + power[k]
@@ -198,42 +216,61 @@
         for k in range(1, z.hist):
             head = head + power[k]
         skip = jnp.logical_and(i == 0, early)
-        band_ref[...] = band_ref[...] + late + jnp.where(skip, 0.0, head)
+        band_ref[: z.rows] = band_ref[: z.rows] + late + jnp.where(skip, 0.0, head)
+        sum_ref[...] = sum_ref[...] + jnp.where(jnp.logical_and(skip, place < z.hist), 0.0, edges)
+        edges_ref[pl.ds(pl.multiple_of(i * CHUNK, CHUNK), CHUNK)] = edges
         for k in range(CHUNK):
             power_ref[i * CHUNK + k] = power[k]
 
     pltpu.make_async_copy(pr_ref, pr_ref, sems.at[3]).wait()
     owners_copy.start()
-    raw_copy(0, 0).wait()
-    raw_copy(2, 0).start()
+    early_copies[0].wait()
+    early_copies[2].start()
     frames(0, y0_ref)
+    early_copies[3].start()
     tab_copy.wait()
     delays_copy.start()
 
     def step(j, carry):
         i = 2 * j
-        raw_copy(i + 1, 1).wait()
-        raw_copy(i + 2, 0).wait()
-        raw_copy(i + 3, 1).start()
-
-        @pl.when(i + 4 < chunks)
-        def _():
-            raw_copy(i + 4, 0).start()
+        for turn in range(3):
+
+            @pl.when(j == turn)
+            def _(turn=turn):
+                early_copies[turn + 1].wait()
 
         frames(i + 1, y1_ref)
-        powers(i, y0_ref, [t0_ref, t1_ref])
+        powers(i, y0_ref, [t0_ref, t1_ref], e0_ref)
         frames(i + 2, y0_ref)
-        powers(i + 1, y1_ref, [t2_ref, t3_ref])
+        powers(i + 1, y1_ref, [t2_ref, t3_ref], e1_ref)
         return carry
 
     lax.fori_loop(0, chunks // 2 - 1, step, 0)
-    raw_copy(chunks - 1, 1).wait()
     owners_copy.wait()
     widths_copy.start()
     delays_copy.wait()
     frames(chunks - 1, y1_ref)
-    powers(chunks - 2, y0_ref, [t0_ref, t1_ref])
-    powers(chunks - 1, y1_ref, [t2_ref, t3_ref])
+    powers(chunks - 2, y0_ref, [t0_ref, t1_ref], e0_ref)
+    powers(chunks - 1, y1_ref, [t2_ref, t3_ref], e1_ref)
+    def spectrum(start):
+        start = pl.multiple_of(start, z.channels)
+        return buf[:, pl.ds(start, z.channels)].astype(jnp.float32).reshape(DFT_A, LANES).astype(jnp.bfloat16)
+
+    row = 0
+    tail = (z.spec - z.hist) * z.channels
+    starts = [jnp.where(early, 0, tail)] if z.n_tm == 2 else [tail, 0]
+    for start in starts:
+        for k in range(z.hist):
+            msg_ref[row : row + DFT_A] = spectrum(start + k * z.channels)
+            row += DFT_A
+    total = jnp.sum(sum_ref[...], 0, keepdims=True)
+    rest = jnp.concatenate([total, jnp.zeros((15, LANES), jnp.float32)])
+    band_ref[z.rows :] = rest[: z.band_rows - z.rows]
+    msg_ref[row : row + z.deep] = jnp.concatenate([band_ref[: z.rows], rest]).astype(jnp.bfloat16)
+    widths_copy.wait()
+
+
+def coarse(z, tab_ref, trial_ref, hits_ref):
     unit = 1.0 / (math.sqrt(z.channels // NBLK) * math.sqrt(NBLK))
     trials = trial_ref.shape[1]
     tall = jnp.concatenate(
@@ -250,30 +287,14 @@
         hits = jnp.concatenate([jnp.where(mine == value, unit, 0.0) for value in range(MAXT + 1)])
         hits_ref[g] = hits.astype(jnp.bfloat16)
 
-    def spectrum(start):
-        start = pl.multiple_of(start, z.channels)
-        return buf[:, pl.ds(start, z.channels)].astype(jnp.float32).reshape(DFT_A, LANES).astype(jnp.bfloat16)
-
-    row = 0
-    tail = (z.spec - z.hist) * z.channels
-    starts = [jnp.where(early, 0, tail)] if z.n_tm == 2 else [tail, 0]
-    for start in starts:
-        for k in range(z.hist):
-            msg_ref[row : row + DFT_A] = spectrum(start + k * z.channels)
-            row += DFT_A
-    high = band_ref[...].astype(jnp.bfloat16)
-    msg_ref[row : row + z.rows] = high
-    msg_ref[row + z.rows : row + 2 * z.rows] = (band_ref[...] - high.astype(jnp.float32)).astype(jnp.bfloat16)
-    widths_copy.wait()
-
-
-def boundary(z, power_ref, pr_ref, band_ref, own_ref, other_ref, tab_ref, y_ref, t_ref, bound_ref, inv_ref):
+
+def boundary(z, pr_ref, band_ref, own_ref, other_ref, tab_ref, y_ref, t_ref, e_ref, bound_ref, sides_ref, inv_ref):
     me = lax.axis_index("tm")
-    total = band_ref[...]
     lo = z.bounds * z.raw_rows
-    total = total + (
-        other_ref[lo : lo + z.rows].astype(jnp.float32) + other_ref[lo + z.rows : lo + 2 * z.rows].astype(jnp.float32)
-    )
+    rest = other_ref[lo : lo + z.deep].astype(jnp.float32)
+    total = band_ref[: z.rows] + rest[: z.rows]
+    edge = band_ref[z.rows :] + rest[z.rows : z.band_rows]
+    e_ref[...] = jnp.zeros_like(e_ref)
     swap = jnp.logical_and(me > 0, z.n_tm == 2)
     y_ref[:, z.hist * LANES :] = jnp.zeros((DFT_A, LANES), jnp.bfloat16)
     for b in range(z.bounds):
@@ -287,19 +308,33 @@
         fill_frames(
             z, lambda k, block: take(k, block, True), lambda k, block: take(k, block, False), pr_ref, y_ref, z.hist
         )
-        power = transform(z, y_ref, tab_ref, [t_ref], z.hist)
+        power, edges = transform(z, y_ref, tab_ref, [t_ref], e_ref, z.hist)
+        sides_ref[b] = edges
+        edge = edge + jnp.sum(edges, 0, keepdims=True)
         for k in range(z.hist):
             total = total + power[k]
             bound_ref[b * z.hist + k] = power[k]
     scale = float(z.taps * z.channels)
+    total = jnp.concatenate([total, edge])
     inv_ref[...] = 1.0 / (total * (1.0 / (z.spec * z.n_tm)) + 1e-6 * scale)
 
 
-def subbands(z, first, last, power_ref, bound_ref, inv_ref, tab_ref, weighted_ref, sums_ref, mean_ref, sub_ref):
+def subbands(
+    z, first, last, power_ref, edges_ref, bound_ref, sides_ref, inv_ref, tab_ref, weighted_ref, sums_ref, mean_ref, sub_ref
+):
     me = lax.axis_index("tm")
     groups = z.groups
-    weighted_ref[...] = table(z, tab_ref, "weight").astype(jnp.float32)[: z.rows] * inv_ref[...]
-    mine = jnp.maximum(me - 1, 0) * z.hist
+    weighted_ref[...] = table(z, tab_ref, "weight").astype(jnp.float32)[: z.band_rows] * inv_ref[...]
+    before = jnp.maximum(me - 1, 0)
+    mine = before * z.hist
+    place = lax.broadcasted_iota(jnp.int32, (CHUNK, LANES), 0)
+
+    def edges_of(i):
+        value = edges_ref[pl.ds(pl.multiple_of(i * CHUNK, CHUNK), CHUNK)]
+        if first == 0:
+            inside = jnp.logical_and(jnp.logical_and(me > 0, i == 0), place < z.hist)
+            value = jnp.where(inside, sides_ref[before], value)
+        return value
 
     def power_of(i, k):
         value = power_ref[i * CHUNK + k]
@@ -309,17 +344,16 @@
 
     def means(i):
         for k in range(CHUNK):
-            value = power_of(i, k) * weighted_ref[...]
+            value = power_of(i, k) * weighted_ref[: z.rows]
             sums_ref[k * 8 : k * 8 + 8] = jnp.sum(value.reshape(z.rows // 8, 8, LANES), 0)
-        acc = sums_ref[pl.ds(0, CHUNK, stride=8)]
-        for j in range(1, 8):
+        acc = edges_of(i) * weighted_ref[z.rows : z.rows + 1]
+        for j in range(8):
             acc = acc + sums_ref[pl.ds(j, CHUNK, stride=8)]
         at = pl.multiple_of(i * CHUNK, CHUNK)
         mean_ref[pl.ds(at, CHUNK)] = jnp.broadcast_to(jnp.sum(acc, 1, keepdims=True), (CHUNK, LANES))
 
     parities = z.channels // NBLK // DFT_A
     lane = lax.broadcasted_iota(jnp.int32, (groups, LANES), 1)
-    pad = jnp.zeros((z.rows16 - z.rows, LANES), jnp.float32)
 
     def picked(m, step, value):
         row = (m * FD + step) * parities * groups
@@ -331,13 +365,16 @@
 
     def flat_step(i, carry):
         flats = []
+        at = pl.multiple_of(i * CHUNK, CHUNK)
+        edges = edges_of(i) * inv_ref[z.rows : z.rows + 1] - mean_ref[pl.ds(at, CHUNK)]
         open_sums = [list(carry[m]) for m in range(2)]
         for k in range(CHUNK):
-            flat = power_of(i, k) * inv_ref[...] - mean_ref[pl.ds(i * CHUNK + k, 1)]
-            flats.append(jnp.concatenate([flat, pad]).astype(jnp.bfloat16))
+            flat = power_of(i, k) * inv_ref[: z.rows] - mean_ref[pl.ds(i * CHUNK + k, 1)]
+            edge = jnp.where(place == k, edges, 0.0)
+            flats.append(jnp.concatenate([flat, edge]).astype(jnp.bfloat16))
             if k % 2 == 0:
                 continue
-            masks = table(z, tab_ref, "masks")[:, : z.rows16]
+            masks = table(z, tab_ref, "masks")[:, : z.deep]
             found = jnp.dot(masks, jnp.concatenate(flats[-2:], 1), preferred_element_type=jnp.float32)
             for half in range(2):
                 value = found[:, half * LANES : (half + 1) * LANES]
@@ -368,12 +405,13 @@
     return total
 
 
-def tails(z, power_ref, pr_ref, band_ref, own_ref, other_ref, tab_ref, hits_ref,
-          prev_ref, high_ref, bound_ref, inv_ref, y_ref, t_ref, late_ref, weighted_ref, sums_ref, mean_ref):
+def tails(z, power_ref, edges_ref, pr_ref, band_ref, own_ref, other_ref, tab_ref, hits_ref,
+          prev_ref, high_ref, bound_ref, sides_ref, inv_ref, y_ref, t_ref, e_ref, late_ref, weighted_ref, sums_ref, mean_ref):
     groups = z.groups
-    boundary(z, power_ref, pr_ref, band_ref, own_ref, other_ref, tab_ref, y_ref, t_ref, bound_ref, inv_ref)
+    boundary(z, pr_ref, band_ref, own_ref, other_ref, tab_ref, y_ref, t_ref, e_ref, bound_ref, sides_ref, inv_ref)
     carry = subbands(
-        z, z.low_chunks, z.spec // CHUNK, power_ref, bound_ref, inv_ref, tab_ref, weighted_ref, sums_ref, mean_ref, high_ref
+        z, z.low_chunks, z.spec // CHUNK, power_ref, edges_ref, bound_ref, sides_ref, inv_ref, tab_ref,
+        weighted_ref, sums_ref, mean_ref, high_ref,
     )
     count = z.high_rows
     done = z.spec - z.low_chunks * CHUNK
@@ -393,10 +431,13 @@
     prev_ref[...] = late_ref[...].reshape(groups * trials, LANES).astype(jnp.bfloat16)
 
 
-def bulk(z, power_ref, bound_ref, inv_ref, tab_ref, hits_ref, high_ref,
+def bulk(z, power_ref, edges_ref, bound_ref, sides_ref, inv_ref, tab_ref, hits_ref, high_ref,
          main_ref, weighted_ref, sums_ref, mean_ref, low_ref, join_ref):
     groups = z.groups
-    carry = subbands(z, 0, z.low_chunks, power_ref, bound_ref, inv_ref, tab_ref, weighted_ref, sums_ref, mean_ref, low_ref)
+    carry = subbands(
+        z, 0, z.low_chunks, power_ref, edges_ref, bound_ref, sides_ref, inv_ref, tab_ref,
+        weighted_ref, sums_ref, mean_ref, low_ref,
+    )
     join_ref[...] = jnp.zeros_like(join_ref)
     for m in range(2):
         for step in range(FD - 1):
@@ -491,34 +532,37 @@
     z = Sizes(taps, channels, raw.shape[1] // channels, groups, n_dm, n_tm)
     tables, z.places = constants(z)
     params = pltpu.CompilerParams(vmem_limit_bytes=LIMIT)
-    own_rows = z.raw_rows * (1 if n_tm == 2 else 2) + 2 * z.rows
+    own_rows = z.raw_rows * (1 if n_tm == 2 else 2) + z.deep
     f32, bf16 = jnp.float32, jnp.bfloat16
-    half = CHUNK // 2 * z.rows16
-    power, pr, band, msg, tables, hits, owner, width = pl.pallas_call(
+    half = CHUNK // 2 * z.rows
+    power, edges, pr, band, msg, tables, trial, owner, width = pl.pallas_call(
         functools.partial(channelize, z),
         out_shape=(
             pltpu.VMEM((z.spec, z.rows, LANES), f32),
+            pltpu.VMEM((z.spec, LANES), f32),
             pltpu.VMEM((taps, 1, channels), f32),
-            pltpu.VMEM((z.rows, LANES), f32),
+            pltpu.VMEM((z.band_rows, LANES), f32),
             pltpu.VMEM((own_rows, LANES), bf16),
             pltpu.VMEM(tables.shape, bf16),
-            pltpu.VMEM((groups, (MAXT + 1) * 8, 2 * LANES), bf16),
+            pltpu.VMEM(delays.shape, jnp.int32),
             pltpu.SMEM((groups,), jnp.int32),
             pltpu.SMEM(widths.shape, jnp.int32),
         ),
         in_specs=[hbm_spec()] * 6,
-        out_specs=[vmem_spec()] * 6 + [smem_spec()] * 2,
+        out_specs=[vmem_spec()] * 7 + [smem_spec()] * 2,
         scratch_shapes=[
             pltpu.VMEM((1, z.spec * channels), bf16),
-            pltpu.VMEM(delays.shape, jnp.int32),
             pltpu.VMEM((z.hist, DFT_A, LANES), f32),
             pltpu.VMEM((DFT_A, CHUNK * LANES), bf16),
             pltpu.VMEM((DFT_A, CHUNK * LANES), bf16),
             pltpu.VMEM((half, 2 * LANES), bf16),
+            pltpu.VMEM((half + 16, 2 * LANES), bf16),
             pltpu.VMEM((half, 2 * LANES), bf16),
-            pltpu.VMEM((half, 2 * LANES), bf16),
-            pltpu.VMEM((half, 2 * LANES), bf16),
-            pltpu.SemaphoreType.DMA((4,)),
+            pltpu.VMEM((half + 16, 2 * LANES), bf16),
+            pltpu.VMEM((16, LANES), f32),
+            pltpu.VMEM((16, LANES), f32),
+            pltpu.VMEM((16, LANES), f32),
+            pltpu.SemaphoreType.DMA((5,)),
         ],
         compiler_params=params,
         name="channelize",
@@ -531,40 +575,48 @@
         every = lax.all_gather(msg, "tm")
         lasts = every[:-1, : z.raw_rows].reshape(-1, LANES)
         firsts = every[1:, z.raw_rows : 2 * z.raw_rows].reshape(-1, LANES)
-        parts = every[:, 2 * z.raw_rows :].astype(f32).reshape(n_tm, 2, z.rows, LANES)
-        rest = jnp.sum(parts, (0, 1)) - band
-        high = rest.astype(bf16)
-        pair = jnp.concatenate([high, (rest - high.astype(f32)).astype(bf16)])
-        own, other = jnp.concatenate([lasts, pair]), jnp.concatenate([firsts, pair])
+        rest = lax.psum(band, "tm") - band
+        rest = jnp.concatenate([rest, jnp.zeros((z.deep - z.band_rows, LANES), f32)]).astype(bf16)
+        own, other = jnp.concatenate([lasts, rest]), jnp.concatenate([firsts, rest])
+    hits = pl.pallas_call(
+        functools.partial(coarse, z),
+        out_shape=pltpu.VMEM((groups, (MAXT + 1) * 8, 2 * LANES), bf16),
+        in_specs=[vmem_spec()] * 2,
+        out_specs=vmem_spec(),
+        compiler_params=params,
+        name="coarse",
+    )(*kept(tables, trial))
     work = [
-        pltpu.VMEM((z.rows, LANES), f32),
+        pltpu.VMEM((z.band_rows, LANES), f32),
         pltpu.VMEM((CHUNK * 8, LANES), f32),
         pltpu.VMEM((z.spec, LANES), f32),
     ]
-    prev, high, bound, inv = pl.pallas_call(
+    prev, high, bound, sides, inv = pl.pallas_call(
         functools.partial(tails, z),
         out_shape=(
             pltpu.VMEM((groups * trials, LANES), bf16),
             pltpu.VMEM((2, z.high_rows * groups, LANES), f32),
             pltpu.VMEM((z.bounds * z.hist, z.rows, LANES), f32),
-            pltpu.VMEM((z.rows, LANES), f32),
+            pltpu.VMEM((z.bounds, 16, LANES), f32),
+            pltpu.VMEM((z.band_rows, LANES), f32),
         ),
-        in_specs=[vmem_spec()] * 7,
-        out_specs=[vmem_spec()] * 4,
+        in_specs=[vmem_spec()] * 8,
+        out_specs=[vmem_spec()] * 5,
         scratch_shapes=[
             pltpu.VMEM((DFT_A, (z.hist + 1) * LANES), bf16),
-            pltpu.VMEM((z.hist * z.rows16, 2 * LANES), bf16),
+            pltpu.VMEM((z.hist * z.rows + 16, 2 * LANES), bf16),
+            pltpu.VMEM((16, LANES), f32),
             pltpu.VMEM((groups, trials, LANES), f32),
         ]
         + work,
         compiler_params=params,
         name="tails",
-    )(*kept(power, pr, band, own, other, tables, hits))
+    )(*kept(power, edges, pr, band, own, other, tables, hits))
     before = lax.ppermute(prev, "tm", [(i, (i + 1) % n_tm) for i in range(n_tm)])
     main = pl.pallas_call(
         functools.partial(bulk, z),
         out_shape=pltpu.VMEM((groups, trials, LANES), f32),
-        in_specs=[vmem_spec()] * 6,
+        in_specs=[vmem_spec()] * 8,
         out_specs=vmem_spec(),
         scratch_shapes=work
         + [
@@ -574,7 +626,7 @@
         compiler_params=params,
         cost_estimate=pl.CostEstimate(flops=10**9, bytes_accessed=8 * 10**6, transcendentals=0),
         name="bulk",
-    )(*kept(power, bound, inv, tables, hits, high))
+    )(*kept(power, edges, bound, sides, inv, tables, hits, high))
     slots = (2, z.capacity, trials, LANES)
     parcel = (2 * z.capacity * trials, LANES)
     held, leaving = pl.pallas_call(

time: 31.6 us -> 30.9 us (0.978)
  waiting for transfers between devices: 7.7 us -> 7.14 us
    ppermute x1, waiting for transfers between devices: 3.6 us -> 3.08 us  [shards(): own, other = (msg, lax.ppermute(msg, 'tm', [(0, 1), (1, 0)]))]
where the time goes in v6:
time: 30.9 us; the launch traced here: 30.8 us
  Pallas kernels  14.4 us (47%)
  starting transfers between devices  9.17 us (30%)
  waiting for transfers between devices  7.14 us (23%)
    pallas_call x1, Pallas kernels, shards(): pl.pallas_call(functools.partial(channelize, z), out_shape=(pltpu.VMEM((z...  9.34 us
    ppermute x2, starting transfers between devices, shards(): got = lax.ppermute(leaving, 'dm', [(i, i ^ bit) for i in range(n_dm)])  4.39 us
    ppermute x2, waiting for transfers between devices, shards(): got = lax.ppermute(leaving, 'dm', [(i, i ^ bit) for i in range(n_dm)])  4.05 us
    ppermute x1, waiting for transfers between devices, shards(): own, other = (msg, lax.ppermute(msg, 'tm', [(0, 1), (1, 0)]))  3.08 us
    ppermute x1, starting transfers between devices, shards(): own, other = (msg, lax.ppermute(msg, 'tm', [(0, 1), (1, 0)]))  3 us
    pallas_call x1, Pallas kernels, shards(): pl.pallas_call(functools.partial(bulk, z), out_shape=pltpu.VMEM((groups,...  2.08 us
    pallas_call x1, Pallas kernels, shards(): pl.pallas_call(functools.partial(tails, z), out_shape=(pltpu.VMEM((groups...  1.81 us
    ppermute x1, starting transfers between devices, shards(): lax.ppermute(prev, 'tm', [(i, (i + 1) % n_tm) for i in range(n_tm)])  1.78 us
  transfers between devices with their start and end apart: 4, of which 3 were waited for; matrix products, arithmetic and copies ran while one was open for 0% of the time, Pallas kernels for 7%

profile of v6, /device:TPU:0, one launch (start us, length us, event | category | flops | bytes accessed | tf_op | source)
XLA Modules:
  0.0 30.8 jit_solution(16851190779058199255)
XLA Ops:
  0.0 9.3 %channelize.1 = (f32[128,64,128]{2,1,0:T(8,128)S(1)}, f32[128,128]{1,0:T(8,128)S(1)}, f32[4,1,16384]{2,1,0:T(1,128)S(1)}, f32[72,128]{1,0:T(8,128)S(1)}, bf16[46...) custom-call(bf16[1,2097152]{1,0:T(2,128)(2,1)} %raw_ref.1, ...), custom_call_target="tpu_custom_call" | custom-call | tf_op jit(solution)/shard_map/channelize/pallas_call | solution.py:538
  9.4 3.0 %collective-permute-start = (bf16[464,128]{1,0:T(8,128)(2,1)S(1)}, bf16[464,128]{1,0:T(8,128)(2,1)S(1)}, u32[]{:S(2)}, u32[]{:S(2)}) collective-permute-start(bf16[464,128]{1,0:T(8,128)(2,1)S(1)} %get-tuple-element.28.own_ref), channel_id=1, source_target_pairs={{0,2},{2,0},{1,3},{3,1},{4,6},{6,4},{5,7},{7,5},{8,10},{10,8},{9,1... | collective-permute-start | bytes 356360 | tf_op jit(solution)/shard_map/ppermute | solution.py:573
  12.4 0.1 coarse.1.hits_ref
  12.5 3.1 %collective-permute-done.other_ref = bf16[464,128]{1,0:T(8,128)(2,1)S(1)} collective-permute-done((bf16[464,128]{1,0:T(8,128)(2,1)S(1)}, bf16[464,128]{1,0:T(8,128)(2,1)S(1)}, u32[]{:S(2)}, u32[]{:S(2)}) %collective-permute-start) | collective-permute-done | bytes 118816 | tf_op jit(solution)/shard_map/ppermute | solution.py:573
  15.6 1.8 %tails.1 = (bf16[32,128]{1,0:T(8,128)(2,1)S(1)}, f32[2,512,128]{2,1,0:T(8,128)S(1)}, f32[3,64,128]{2,1,0:T(8,128)S(1)}, f32[1,16,128]{2,1,0:T(8,128)S(1)}, f32[72,128]{1,0:T(8,128)S(1)}) custom-call(f32[128,64,128]{2,1,0:T(8,128)S(1)} %get-tuple-element.24.power_ref, f32[128,128]{1,0:T(8,128)S(1)} %get-tuple-element.25.edges_ref, ...), custom_call_target="tpu_custom_call" | custom-call | tf_op jit(solution)/shard_map/tails/pallas_call | solution.py:594
  17.4 1.8 %collective-permute-start.1 = (bf16[32,128]{1,0:T(8,128)(2,1)S(1)}, bf16[32,128]{1,0:T(8,128)(2,1)S(1)}, u32[]{:S(2)}, u32[]{:S(2)}) collective-permute-start(bf16[32,128]{1,0:T(8,128)(2,1)S(1)} %get-tuple-element.35), channel_id=1, source_target_pairs={{0,2},{2,0},{1,3},{3,1},{4,6},{6,4},{5,7},{7,5},{8,10},{10,8},{9,1... | collective-permute-start | bytes 24584 | tf_op jit(solution)/shard_map/ppermute | solution.py:615
  19.2 2.1 %bulk.1.main_ref = f32[8,4,128]{2,1,0:T(4,128)S(1)} custom-call(f32[128,64,128]{2,1,0:T(8,128)S(1)} %get-tuple-element.24.power_ref, f32[128,128]{1,0:T(8,128)S(1)} %get-tuple-element.25.edges_ref, f32[3,64,128]{2,1,0:T(8,128)S(1)} %get-tuple-element.31.bound_ref, f32[1,16,128]{2,1,0:T(8,128)S(1)} %get-tuple-element.32.sides_ref, ...), custom_call_target="tpu_custom_call" | custom-call | flops 1000000000 | bytes 8000000 | tf_op jit(solution)/shard_map/bulk/pallas_call | solution.py:616
  21.3 0.0 collective-permute-done.1.prev_ref
  21.3 0.1 parcels.1
  21.3 1.7 %collective-permute-start.2 = (bf16[2,1,32,128]{3,2,1,0:T(8,128)(2,1)S(1)}, bf16[2,1,32,128]{3,2,1,0:T(8,128)(2,1)S(1)}, u32[]{:S(2)}, u32[]{:S(2)}) collective-permute-start(bf16[2,1,32,128]{3,2,1,0:T(8,128)(2,1)S(1)} %get-tuple-element.38), channel_id=1, source_target_pairs={{0,4},{4,0},{8,12},{12,8},{1,5},{5,1},{9,13},{13,9},{2,6},{6,2},{1... | collective-permute-start | bytes 49160 | tf_op jit(solution)/shard_map/ppermute | solution.py:643
  23.0 2.1 %collective-permute-done.2.got_ref = bf16[2,1,32,128]{3,2,1,0:T(8,128)(2,1)S(1)} collective-permute-done((bf16[2,1,32,128]{3,2,1,0:T(8,128)(2,1)S(1)}, bf16[2,1,32,128]{3,2,1,0:T(8,128)(2,1)S(1)}, u32[]{:S(2)}, u32[]{:S(2)}) %collective-permute-start.2) | collective-permute-done | bytes 16416 | tf_op jit(solution)/shard_map/ppermute | solution.py:643
  25.1 2.7 %collective-permute-start.3 = (bf16[1,2,32,128]{3,2,1,0:T(8,128)(2,1)S(1)}, bf16[1,2,32,128]{3,2,1,0:T(8,128)(2,1)S(1)}, u32[]{:S(2)}, u32[]{:S(2)}) collective-permute-start(bf16[1,2,32,128]{3,2,1,0:T(8,128)(2,1)S(1)} %get-tuple-element.40), channel_id=1, source_target_pairs={{0,8},{4,12},{8,0},{12,4},{1,9},{5,13},{9,1},{13,5},{2,10},{6,14},... | collective-permute-start | bytes 49160 | tf_op jit(solution)/shard_map/ppermute | solution.py:643
  27.8 2.0 %collective-permute-done.3.refs_1_ = bf16[1,2,32,128]{3,2,1,0:T(8,128)(2,1)S(1)} collective-permute-done((bf16[1,2,32,128]{3,2,1,0:T(8,128)(2,1)S(1)}, bf16[1,2,32,128]{3,2,1,0:T(8,128)(2,1)S(1)}, u32[]{:S(2)}, u32[]{:S(2)}) %collective-permute-start.3) | collective-permute-done | bytes 16416 | tf_op jit(solution)/shard_map/ppermute | solution.py:643
  29.8 1.0 %boxes.1 = bf16[4,4,1,4,8,128]{5,4,3,2,1,0:T(8,128)(2,1)} custom-call(s32[8]{0:T(128)S(4)} %get-tuple-element.23.widths_ref, bf16[1,2,32,128]{3,2,1,0:T(8,128)(2,1)S(1)} %get-tuple-element.39.refs_0_, bf16[1,2,32,128]{3,2,1,0:T(8,128)(2,1)S(1)} %collective-permute-done.3.refs_1_), custom_call_target="tpu_custom_call" | custom-call | tf_op jit(solution)/shard_map/boxes/pallas_call | solution.py:655
  (1 shorter events, 0.0 us)
Async XLA Ops:
  9.4 6.2 %collective-permute-start = (bf16[464,128]{1,0:T(8,128)(2,1)S(1)}, bf16[464,128]{1,0:T(8,128)(2,1)S(1)}, u32[]{:S(2)}, u32[]{:S(2)}) collective-permute-start(bf16[464,128]{1,0:T(8,128)(2,1)S(1)} %get-tuple-element.28.own_ref), channel_id=1, source_target_pairs={{0,2},{2,0},{1,3},{3,1},{4,6},{6,4},{5,7},{7,5},{8,10},{10,8},{9,1... | collective-permute-start | bytes 356360 | tf_op jit(solution)/shard_map/ppermute | solution.py:573
  17.4 3.9 %collective-permute-start.1 = (bf16[32,128]{1,0:T(8,128)(2,1)S(1)}, bf16[32,128]{1,0:T(8,128)(2,1)S(1)}, u32[]{:S(2)}, u32[]{:S(2)}) collective-permute-start(bf16[32,128]{1,0:T(8,128)(2,1)S(1)} %get-tuple-element.35), channel_id=1, source_target_pairs={{0,2},{2,0},{1,3},{3,1},{4,6},{6,4},{5,7},{7,5},{8,10},{10,8},{9,1... | collective-permute-start | bytes 24584 | tf_op jit(solution)/shard_map/ppermute | solution.py:615
  21.3 3.8 %collective-permute-start.2 = (bf16[2,1,32,128]{3,2,1,0:T(8,128)(2,1)S(1)}, bf16[2,1,32,128]{3,2,1,0:T(8,128)(2,1)S(1)}, u32[]{:S(2)}, u32[]{:S(2)}) collective-permute-start(bf16[2,1,32,128]{3,2,1,0:T(8,128)(2,1)S(1)} %get-tuple-element.38), channel_id=1, source_target_pairs={{0,4},{4,0},{8,12},{12,8},{1,5},{5,1},{9,13},{13,9},{2,6},{6,2},{1... | collective-permute-start | bytes 49160 | tf_op jit(solution)/shard_map/ppermute | solution.py:643
  25.1 4.6 %collective-permute-start.3 = (bf16[1,2,32,128]{3,2,1,0:T(8,128)(2,1)S(1)}, bf16[1,2,32,128]{3,2,1,0:T(8,128)(2,1)S(1)}, u32[]{:S(2)}, u32[]{:S(2)}) collective-permute-start(bf16[1,2,32,128]{3,2,1,0:T(8,128)(2,1)S(1)} %get-tuple-element.40), channel_id=1, source_target_pairs={{0,8},{4,12},{8,0},{12,4},{1,9},{5,13},{9,1},{13,5},{2,10},{6,14},... | collective-permute-start | bytes 49160 | tf_op jit(solution)/shard_map/ppermute | solution.py:643

commit v7 on v6

--- a/solution.py
+++ b/solution.py
@@ -81,11 +81,17 @@
         "sin": tw_sin,
         "second": np.concatenate([cos_b, sin_b]),
         "second_im": np.concatenate([-sin_b, cos_b]),
-        "masks": masks.reshape(-1, LANES),
+        "masks": masks,
         "weight": weight,
         "expand": expand[:, : z.side],
         "expand_im": expand[:, z.side :],
     }
+    kept_masks, z.mask_rows = [], {}
+    for key in np.ndindex(masks.shape[:3]):
+        if masks[key].any():
+            z.mask_rows[key] = len(kept_masks) * z.groups
+            kept_masks.append(masks[key])
+    tables["masks"] = np.concatenate(kept_masks)
     places, row = {}, 0
     for name, table in tables.items():
         places[name] = (row, row + table.shape[0])
@@ -174,10 +180,10 @@
         return pltpu.make_async_copy(raw_ref.at[:, part], buf.at[:, part], sems.at[side])
 
     tab_copy = pltpu.make_async_copy(tab_in, tab_ref, sems.at[2])
-    delays_copy = pltpu.make_async_copy(delays_ref, trial_ref, sems.at[2])
+    delays_copy = pltpu.make_async_copy(delays_ref, trial_ref, sems.at[1])
     owners_copy = pltpu.make_async_copy(owners_in, owners_ref, sems.at[3])
-    widths_copy = pltpu.make_async_copy(widths_in, widths_ref, sems.at[3])
-    early_copies = [raw_copy(0, 1, 0), raw_copy(1, 3, 1), raw_copy(3, 5, 4), raw_copy(5, chunks, 0)]
+    widths_copy = pltpu.make_async_copy(widths_in, widths_ref, sems.at[2])
+    early_copies = [raw_copy(0, 1, 0), raw_copy(1, 3, 1), raw_copy(3, 5, 2), raw_copy(5, chunks, 0)]
     early_copies[0].start()
     for tap in range(z.taps):
         pltpu.make_async_copy(proto_ref.at[tap : tap + 1], pr_ref.at[tap], sems.at[3]).start()
@@ -225,11 +231,10 @@
     pltpu.make_async_copy(pr_ref, pr_ref, sems.at[3]).wait()
     owners_copy.start()
     early_copies[0].wait()
+    tab_copy.wait()
     early_copies[2].start()
     frames(0, y0_ref)
     early_copies[3].start()
-    tab_copy.wait()
-    delays_copy.start()
 
     def step(j, carry):
         i = 2 * j
@@ -238,6 +243,8 @@
             @pl.when(j == turn)
             def _(turn=turn):
                 early_copies[turn + 1].wait()
+                if turn < 2:
+                    (delays_copy, widths_copy)[turn].start()
 
         frames(i + 1, y1_ref)
         powers(i, y0_ref, [t0_ref, t1_ref], e0_ref)
@@ -247,7 +254,6 @@
 
     lax.fori_loop(0, chunks // 2 - 1, step, 0)
     owners_copy.wait()
-    widths_copy.start()
     delays_copy.wait()
     frames(chunks - 1, y1_ref)
     powers(chunks - 2, y0_ref, [t0_ref, t1_ref], e0_ref)
@@ -336,6 +342,8 @@
             value = jnp.where(inside, sides_ref[before], value)
         return value
 
+    empty = jnp.zeros((groups, LANES), jnp.float32)
+
     def power_of(i, k):
         value = power_ref[i * CHUNK + k]
         if first == 0 and k < z.hist:
@@ -356,12 +364,16 @@
     lane = lax.broadcasted_iota(jnp.int32, (groups, LANES), 1)
 
     def picked(m, step, value):
-        row = (m * FD + step) * parities * groups
-        part = value[row : row + groups]
-        for parity in range(1, parities):
-            hit = (lane if m == 0 else LANES - 1 - lane) % parities == parity
-            part = jnp.where(hit, value[row + parity * groups : row + (parity + 1) * groups], part)
+        rows = [z.mask_rows.get((m, step, parity)) for parity in range(parities)]
+        part = None if None in rows else value[rows[0] : rows[0] + groups]
+        for parity, row in enumerate(rows):
+            if row is not None and (part is None or parity > 0):
+                hit = (lane if m == 0 else LANES - 1 - lane) % parities == parity
+                part = jnp.where(hit, value[row : row + groups], 0.0 if part is None else part)
         return part
+
+    def plus(left, right):
+        return left if right is None else right if left is None else left + right
 
     def flat_step(i, carry):
         flats = []
@@ -381,17 +393,13 @@
                 at = pl.multiple_of(((i - first) * CHUNK + k - 1 + half) * groups, 8)
                 for m in range(2):
                     parts = [picked(m, step, value) for step in range(FD)]
-                    sub_ref[m, pl.ds(at, groups)] = open_sums[m][0] + parts[0]
+                    sub_ref[m, pl.ds(at, groups)] = plus(open_sums[m][0], parts[0])
                     later = open_sums[m][1:] + [None]
-                    open_sums[m] = [
-                        parts[step + 1] if later[step] is None else later[step] + parts[step + 1]
-                        for step in range(FD - 1)
-                    ]
+                    open_sums[m] = [plus(later[step], parts[step + 1]) for step in range(FD - 1)]
         means(jnp.minimum(i + 1, last - 1))
-        return tuple(tuple(value) for value in open_sums)
+        return tuple(tuple(empty if part is None else part for part in value) for value in open_sums)
 
     means(first)
-    empty = jnp.zeros((groups, LANES), jnp.float32)
     return lax.fori_loop(first, last, flat_step, ((empty,) * (FD - 1),) * 2)
 
 
@@ -418,7 +426,7 @@
     for m in range(2):
         for step in range(FD - 1):
             high_ref[m, (done + step) * groups : (done + step + 1) * groups] = carry[m][step]
-    high_ref[:, (done + FD - 1) * groups :] = jnp.zeros((2, (count - done - FD + 1) * groups, LANES), jnp.float32)
+    high_ref[:, (done + FD - 1) * groups :] = jnp.zeros((2, (count + 1 - done - FD + 1) * groups, LANES), jnp.float32)
     blank = jnp.zeros((LANES - count, 2 * LANES), jnp.bfloat16)
     trials = late_ref.shape[1]
     lane = lax.broadcasted_iota(jnp.int32, (8, LANES), 1)
@@ -562,7 +570,7 @@
             pltpu.VMEM((16, LANES), f32),
             pltpu.VMEM((16, LANES), f32),
             pltpu.VMEM((16, LANES), f32),
-            pltpu.SemaphoreType.DMA((5,)),
+            pltpu.SemaphoreType.DMA((4,)),
         ],
         compiler_params=params,
         name="channelize",
@@ -588,14 +596,14 @@
     )(*kept(tables, trial))
     work = [
         pltpu.VMEM((z.band_rows, LANES), f32),
-        pltpu.VMEM((CHUNK * 8, LANES), f32),
+        pltpu.VMEM((CHUNK * 8 + 8, LANES), f32),
         pltpu.VMEM((z.spec, LANES), f32),
     ]
     prev, high, bound, sides, inv = pl.pallas_call(
         functools.partial(tails, z),
         out_shape=(
             pltpu.VMEM((groups * trials, LANES), bf16),
-            pltpu.VMEM((2, z.high_rows * groups, LANES), f32),
+            pltpu.VMEM((2, (z.high_rows + 1) * groups, LANES), f32),
             pltpu.VMEM((z.bounds * z.hist, z.rows, LANES), f32),
             pltpu.VMEM((z.bounds, 16, LANES), f32),
             pltpu.VMEM((z.band_rows, LANES), f32),
@@ -620,8 +628,8 @@
         out_specs=vmem_spec(),
         scratch_shapes=work
         + [
-            pltpu.VMEM((2, z.low_chunks * CHUNK * groups, LANES), f32),
-            pltpu.VMEM((2, 8 * groups, LANES), f32),
+            pltpu.VMEM((2, (z.low_chunks * CHUNK + 1) * groups, LANES), f32),
+            pltpu.VMEM((2, 9 * groups, LANES), f32),
         ],
         compiler_params=params,
         cost_estimate=pl.CostEstimate(flops=10**9, bytes_accessed=8 * 10**6, transcendentals=0),

time: 30.9 us -> 30.6 us (level)
  starting transfers between devices: 9.17 us -> 9.58 us
  Pallas kernels: 14.4 us -> 14 us
  waiting for transfers between devices: 7.14 us -> 6.82 us
    ppermute x2, starting transfers between devices: 4.39 us -> 4.79 us  [shards(): got = lax.ppermute(leaving, 'dm', [(i, i ^ bit) for i in range(n_dm)])]
    ppermute x2, waiting for transfers between devices: 4.05 us -> 3.65 us  [shards(): got = lax.ppermute(leaving, 'dm', [(i, i ^ bit) for i in range(n_dm)])]
  transfers between devices with their start and end apart: 4 -> 4, of which waited for: 3 -> 4; matrix products, arithmetic and copies ran while one was open for 0% -> 0% of each run, Pallas kernels for 7% -> 6%
where the time goes in v7:
time: 30.6 us; the launch traced here: 30.5 us
  Pallas kernels  14 us (46%)
  starting transfers between devices  9.58 us (31%)
  waiting for transfers between devices  6.82 us (22%)
    pallas_call x1, Pallas kernels, shards(): pl.pallas_call(functools.partial(channelize, z), out_shape=(pltpu.VMEM((z...  9.33 us
    ppermute x2, starting transfers between devices, shards(): got = lax.ppermute(leaving, 'dm', [(i, i ^ bit) for i in range(n_dm)])  4.79 us
    ppermute x2, waiting for transfers between devices, shards(): got = lax.ppermute(leaving, 'dm', [(i, i ^ bit) for i in range(n_dm)])  3.65 us
    ppermute x1, waiting for transfers between devices, shards(): own, other = (msg, lax.ppermute(msg, 'tm', [(0, 1), (1, 0)]))  3.08 us
    ppermute x1, starting transfers between devices, shards(): own, other = (msg, lax.ppermute(msg, 'tm', [(0, 1), (1, 0)]))  3 us
    pallas_call x1, Pallas kernels, shards(): pl.pallas_call(functools.partial(bulk, z), out_shape=pltpu.VMEM((groups,...  1.82 us
    ppermute x1, starting transfers between devices, shards(): lax.ppermute(prev, 'tm', [(i, (i + 1) % n_tm) for i in range(n_tm)])  1.79 us
    pallas_call x1, Pallas kernels, shards(): pl.pallas_call(functools.partial(tails, z), out_shape=(pltpu.VMEM((groups...  1.68 us
  transfers between devices with their start and end apart: 4, of which 4 were waited for; matrix products, arithmetic and copies ran while one was open for 0% of the time, Pallas kernels for 6%

profile of v7, /device:TPU:0, one launch (start us, length us, event | category | flops | bytes accessed | tf_op | source)
XLA Modules:
  0.0 30.5 jit_solution(780362704440191211)
XLA Ops:
  0.0 9.3 %channelize.1 = (f32[128,64,128]{2,1,0:T(8,128)S(1)}, f32[128,128]{1,0:T(8,128)S(1)}, f32[4,1,16384]{2,1,0:T(1,128)S(1)}, f32[72,128]{1,0:T(8,128)S(1)}, bf16[46...) custom-call(bf16[1,2097152]{1,0:T(2,128)(2,1)} %raw_ref.1, ...), custom_call_target="tpu_custom_call" | custom-call | tf_op jit(solution)/shard_map/channelize/pallas_call | solution.py:546
  9.3 3.0 %collective-permute-start = (bf16[464,128]{1,0:T(8,128)(2,1)S(1)}, bf16[464,128]{1,0:T(8,128)(2,1)S(1)}, u32[]{:S(2)}, u32[]{:S(2)}) collective-permute-start(bf16[464,128]{1,0:T(8,128)(2,1)S(1)} %get-tuple-element.28.own_ref), channel_id=1, source_target_pairs={{0,2},{2,0},{1,3},{3,1},{4,6},{6,4},{5,7},{7,5},{8,10},{10,8},{9,1... | collective-permute-start | bytes 356360 | tf_op jit(solution)/shard_map/ppermute | solution.py:581
  12.3 0.1 coarse.1.hits_ref
  12.5 3.1 %collective-permute-done.other_ref = bf16[464,128]{1,0:T(8,128)(2,1)S(1)} collective-permute-done((bf16[464,128]{1,0:T(8,128)(2,1)S(1)}, bf16[464,128]{1,0:T(8,128)(2,1)S(1)}, u32[]{:S(2)}, u32[]{:S(2)}) %collective-permute-start) | collective-permute-done | bytes 118816 | tf_op jit(solution)/shard_map/ppermute | solution.py:581
  15.6 1.7 %tails.1 = (bf16[32,128]{1,0:T(8,128)(2,1)S(1)}, f32[2,520,128]{2,1,0:T(8,128)S(1)}, f32[3,64,128]{2,1,0:T(8,128)S(1)}, f32[1,16,128]{2,1,0:T(8,128)S(1)}, f32[72,128]{1,0:T(8,128)S(1)}) custom-call(f32[128,64,128]{2,1,0:T(8,128)S(1)} %get-tuple-element.24.power_ref, f32[128,128]{1,0:T(8,128)S(1)} %get-tuple-element.25.edges_ref, ...), custom_call_target="tpu_custom_call" | custom-call | tf_op jit(solution)/shard_map/tails/pallas_call | solution.py:602
  17.3 1.8 %collective-permute-start.1 = (bf16[32,128]{1,0:T(8,128)(2,1)S(1)}, bf16[32,128]{1,0:T(8,128)(2,1)S(1)}, u32[]{:S(2)}, u32[]{:S(2)}) collective-permute-start(bf16[32,128]{1,0:T(8,128)(2,1)S(1)} %get-tuple-element.35), channel_id=1, source_target_pairs={{0,2},{2,0},{1,3},{3,1},{4,6},{6,4},{5,7},{7,5},{8,10},{10,8},{9,1... | collective-permute-start | bytes 24584 | tf_op jit(solution)/shard_map/ppermute | solution.py:623
  19.0 1.8 %bulk.1.main_ref = f32[8,4,128]{2,1,0:T(4,128)S(1)} custom-call(f32[128,64,128]{2,1,0:T(8,128)S(1)} %get-tuple-element.24.power_ref, f32[128,128]{1,0:T(8,128)S(1)} %get-tuple-element.25.edges_ref, f32[3,64,128]{2,1,0:T(8,128)S(1)} %get-tuple-element.31.bound_ref, f32[1,16,128]{2,1,0:T(8,128)S(1)} %get-tuple-element.32.sides_ref, ...), custom_call_target="tpu_custom_call" | custom-call | flops 1000000000 | bytes 8000000 | tf_op jit(solution)/shard_map/bulk/pallas_call | solution.py:624
  20.9 0.1 collective-permute-done.1.prev_ref
  21.0 0.1 parcels.1
  21.0 1.9 %collective-permute-start.2 = (bf16[2,1,32,128]{3,2,1,0:T(8,128)(2,1)S(1)}, bf16[2,1,32,128]{3,2,1,0:T(8,128)(2,1)S(1)}, u32[]{:S(2)}, u32[]{:S(2)}) collective-permute-start(bf16[2,1,32,128]{3,2,1,0:T(8,128)(2,1)S(1)} %get-tuple-element.38), channel_id=1, source_target_pairs={{0,4},{4,0},{8,12},{12,8},{1,5},{5,1},{9,13},{13,9},{2,6},{6,2},{1... | collective-permute-start | bytes 49160 | tf_op jit(solution)/shard_map/ppermute | solution.py:651
  22.9 1.9 %collective-permute-done.2.got_ref = bf16[2,1,32,128]{3,2,1,0:T(8,128)(2,1)S(1)} collective-permute-done((bf16[2,1,32,128]{3,2,1,0:T(8,128)(2,1)S(1)}, bf16[2,1,32,128]{3,2,1,0:T(8,128)(2,1)S(1)}, u32[]{:S(2)}, u32[]{:S(2)}) %collective-permute-start.2) | collective-permute-done | bytes 16416 | tf_op jit(solution)/shard_map/ppermute | solution.py:651
  24.8 2.9 %collective-permute-start.3 = (bf16[1,2,32,128]{3,2,1,0:T(8,128)(2,1)S(1)}, bf16[1,2,32,128]{3,2,1,0:T(8,128)(2,1)S(1)}, u32[]{:S(2)}, u32[]{:S(2)}) collective-permute-start(bf16[1,2,32,128]{3,2,1,0:T(8,128)(2,1)S(1)} %get-tuple-element.40), channel_id=1, source_target_pairs={{0,8},{4,12},{8,0},{12,4},{1,9},{5,13},{9,1},{13,5},{2,10},{6,14},... | collective-permute-start | bytes 49160 | tf_op jit(solution)/shard_map/ppermute | solution.py:651
  27.7 1.7 %collective-permute-done.3.refs_1_ = bf16[1,2,32,128]{3,2,1,0:T(8,128)(2,1)S(1)} collective-permute-done((bf16[1,2,32,128]{3,2,1,0:T(8,128)(2,1)S(1)}, bf16[1,2,32,128]{3,2,1,0:T(8,128)(2,1)S(1)}, u32[]{:S(2)}, u32[]{:S(2)}) %collective-permute-start.3) | collective-permute-done | bytes 16416 | tf_op jit(solution)/shard_map/ppermute | solution.py:651
  29.5 1.0 %boxes.1 = bf16[4,4,1,4,8,128]{5,4,3,2,1,0:T(8,128)(2,1)} custom-call(s32[8]{0:T(128)S(4)} %get-tuple-element.23.widths_ref, bf16[1,2,32,128]{3,2,1,0:T(8,128)(2,1)S(1)} %get-tuple-element.39.refs_0_, bf16[1,2,32,128]{3,2,1,0:T(8,128)(2,1)S(1)} %collective-permute-done.3.refs_1_), custom_call_target="tpu_custom_call" | custom-call | tf_op jit(solution)/shard_map/boxes/pallas_call | solution.py:663
  (1 shorter events, 0.0 us)
Async XLA Ops:
  9.3 6.2 %collective-permute-start = (bf16[464,128]{1,0:T(8,128)(2,1)S(1)}, bf16[464,128]{1,0:T(8,128)(2,1)S(1)}, u32[]{:S(2)}, u32[]{:S(2)}) collective-permute-start(bf16[464,128]{1,0:T(8,128)(2,1)S(1)} %get-tuple-element.28.own_ref), channel_id=1, source_target_pairs={{0,2},{2,0},{1,3},{3,1},{4,6},{6,4},{5,7},{7,5},{8,10},{10,8},{9,1... | collective-permute-start | bytes 356360 | tf_op jit(solution)/shard_map/ppermute | solution.py:581
  17.3 3.7 %collective-permute-start.1 = (bf16[32,128]{1,0:T(8,128)(2,1)S(1)}, bf16[32,128]{1,0:T(8,128)(2,1)S(1)}, u32[]{:S(2)}, u32[]{:S(2)}) collective-permute-start(bf16[32,128]{1,0:T(8,128)(2,1)S(1)} %get-tuple-element.35), channel_id=1, source_target_pairs={{0,2},{2,0},{1,3},{3,1},{4,6},{6,4},{5,7},{7,5},{8,10},{10,8},{9,1... | collective-permute-start | bytes 24584 | tf_op jit(solution)/shard_map/ppermute | solution.py:623
  21.0 3.8 %collective-permute-start.2 = (bf16[2,1,32,128]{3,2,1,0:T(8,128)(2,1)S(1)}, bf16[2,1,32,128]{3,2,1,0:T(8,128)(2,1)S(1)}, u32[]{:S(2)}, u32[]{:S(2)}) collective-permute-start(bf16[2,1,32,128]{3,2,1,0:T(8,128)(2,1)S(1)} %get-tuple-element.38), channel_id=1, source_target_pairs={{0,4},{4,0},{8,12},{12,8},{1,5},{5,1},{9,13},{13,9},{2,6},{6,2},{1... | collective-permute-start | bytes 49160 | tf_op jit(solution)/shard_map/ppermute | solution.py:651
  24.8 4.6 %collective-permute-start.3 = (bf16[1,2,32,128]{3,2,1,0:T(8,128)(2,1)S(1)}, bf16[1,2,32,128]{3,2,1,0:T(8,128)(2,1)S(1)}, u32[]{:S(2)}, u32[]{:S(2)}) collective-permute-start(bf16[1,2,32,128]{3,2,1,0:T(8,128)(2,1)S(1)} %get-tuple-element.40), channel_id=1, source_target_pairs={{0,8},{4,12},{8,0},{12,4},{1,9},{5,13},{9,1},{13,5},{2,10},{6,14},... | collective-permute-start | bytes 49160 | tf_op jit(solution)/shard_map/ppermute | solution.py:651

commit v8 on v7

--- a/solution.py
+++ b/solution.py
@@ -171,7 +171,7 @@
 
 def channelize(z, raw_ref, proto_ref, tab_in, delays_ref, owners_in, widths_in,
                power_ref, edges_ref, pr_ref, band_ref, msg_ref, tab_ref, trial_ref, owners_ref, widths_ref,
-               buf, hist_ref, y0_ref, y1_ref, t0_ref, t1_ref, t2_ref, t3_ref, e0_ref, e1_ref, sum_ref, sems):
+               buf, hist_ref, y0_ref, y1_ref, t0_ref, t1_ref, e0_ref, e1_ref, sum_ref, sems):
     chunks = z.spec // CHUNK
     span = CHUNK * z.channels
 
@@ -247,17 +247,17 @@
                     (delays_copy, widths_copy)[turn].start()
 
         frames(i + 1, y1_ref)
-        powers(i, y0_ref, [t0_ref, t1_ref], e0_ref)
+        powers(i, y0_ref, [t0_ref], e0_ref)
         frames(i + 2, y0_ref)
-        powers(i + 1, y1_ref, [t2_ref, t3_ref], e1_ref)
+        powers(i + 1, y1_ref, [t1_ref], e1_ref)
         return carry
 
     lax.fori_loop(0, chunks // 2 - 1, step, 0)
     owners_copy.wait()
     delays_copy.wait()
     frames(chunks - 1, y1_ref)
-    powers(chunks - 2, y0_ref, [t0_ref, t1_ref], e0_ref)
-    powers(chunks - 1, y1_ref, [t2_ref, t3_ref], e1_ref)
+    powers(chunks - 2, y0_ref, [t0_ref], e0_ref)
+    powers(chunks - 1, y1_ref, [t1_ref], e1_ref)
     def spectrum(start):
         start = pl.multiple_of(start, z.channels)
         return buf[:, pl.ds(start, z.channels)].astype(jnp.float32).reshape(DFT_A, LANES).astype(jnp.bfloat16)
@@ -472,17 +472,19 @@
             rank = rank + jnp.where(owners_ref[earlier] == owner, 1, 0)
         all_ref[owner ^ me, 0, rank] = main_ref[g]
         all_ref[owner ^ me, 1, rank] = late_ref[g]
+    half = z.n_dm // 2
     for r in range(z.n_dm):
         value = all_ref[r].reshape(stay_ref.shape[2:]).astype(jnp.bfloat16)
-        (leave_ref if r % 2 else stay_ref)[r // 2, 0] = value
+        (stay_ref if r < half else leave_ref)[r % half, 0] = value
 
 
 def relay(held_ref, got_ref, stay_ref, leave_ref):
     count = held_ref.shape[1]
-    for r in range(held_ref.shape[0]):
-        target = leave_ref if r % 2 else stay_ref
-        target[r // 2, :count] = held_ref[r]
-        target[r // 2, count:] = got_ref[r]
+    half = held_ref.shape[0] // 2
+    for r in range(2 * half):
+        target = stay_ref if r < half else leave_ref
+        target[r % half, :count] = held_ref[r]
+        target[r % half, count:] = got_ref[r]
 
 
 def boxes(z, widths_ref, *refs):
@@ -500,8 +502,11 @@
     weights = [jnp.where(width > lag, norm, 0.0) for lag in range(WMAX)]
     prior = WMAX - 1
     rows = z.capacity * trials
-    for r in range(z.n_dm):
-        ref, at = (held_ref, r) if r < near else (got_ref, r - near)
+    order, bit = [0], z.n_dm // 2
+    while bit:
+        order, bit = order + [r + bit for r in order], bit // 2
+    for place, r in enumerate(order):
+        ref, at = (held_ref, place) if place < near else (got_ref, place - near)
         own = ref[0, at, :rows].astype(jnp.float32)
         past = jnp.where(early, 0.0, ref[0, at, rows:].astype(jnp.float32))
         wide = jnp.concatenate([own, jnp.zeros_like(own)], 1)
@@ -563,10 +568,8 @@
             pltpu.VMEM((z.hist, DFT_A, LANES), f32),
             pltpu.VMEM((DFT_A, CHUNK * LANES), bf16),
             pltpu.VMEM((DFT_A, CHUNK * LANES), bf16),
-            pltpu.VMEM((half, 2 * LANES), bf16),
-            pltpu.VMEM((half + 16, 2 * LANES), bf16),
-            pltpu.VMEM((half, 2 * LANES), bf16),
-            pltpu.VMEM((half + 16, 2 * LANES), bf16),
+            pltpu.VMEM((2 * half + 16, 2 * LANES), bf16),
+            pltpu.VMEM((2 * half + 16, 2 * LANES), bf16),
             pltpu.VMEM((16, LANES), f32),
             pltpu.VMEM((16, LANES), f32),
             pltpu.VMEM((16, LANES), f32),
@@ -646,15 +649,15 @@
         compiler_params=params,
         name="parcels",
     )(*kept(main, before), *kept(owner, space=pltpu.SMEM))
-    bit = 1
+    bit = n_dm // 2
     while True:
         got = lax.ppermute(leaving, "dm", [(i, i ^ bit) for i in range(n_dm)])
-        bit *= 2
-        if bit == n_dm:
+        bit //= 2
+        if bit == 0:
             break
         held, leaving = pl.pallas_call(
             relay,
-            out_shape=(pltpu.VMEM((n_dm // 2 // bit, bit, *parcel), bf16),) * 2,
+            out_shape=(pltpu.VMEM((bit, n_dm // 2 // bit, *parcel), bf16),) * 2,
             in_specs=[vmem_spec()] * 2,
             out_specs=[vmem_spec()] * 2,
             compiler_params=params,

time: 30.6 us -> 30.1 us (0.984)
  Pallas kernels: 14 us -> 13.5 us
    pallas_call x1, Pallas kernels: 9.33 us -> 8.82 us  [shards(): pl.pallas_call(functools.partial(channelize, z), out_shape=(pltpu.VMEM((z...]
  transfers between devices with their start and end apart: 4 -> 4, of which waited for: 4 -> 4; matrix products, arithmetic and copies ran while one was open for 0% -> 0% of each run, Pallas kernels for 6% -> 7%
where the time goes in v8:
time: 30.1 us; the launch traced here: 29.9 us
  Pallas kernels  13.5 us (45%)
  starting transfers between devices  9.52 us (32%)
  waiting for transfers between devices  6.88 us (23%)
    pallas_call x1, Pallas kernels, shards(): pl.pallas_call(functools.partial(channelize, z), out_shape=(pltpu.VMEM((z...  8.82 us
    ppermute x2, starting transfers between devices, shards(): got = lax.ppermute(leaving, 'dm', [(i, i ^ bit) for i in range(n_dm)])  4.73 us
    ppermute x2, waiting for transfers between devices, shards(): got = lax.ppermute(leaving, 'dm', [(i, i ^ bit) for i in range(n_dm)])  3.71 us
    ppermute x1, waiting for transfers between devices, shards(): own, other = (msg, lax.ppermute(msg, 'tm', [(0, 1), (1, 0)]))  3.09 us
    ppermute x1, starting transfers between devices, shards(): own, other = (msg, lax.ppermute(msg, 'tm', [(0, 1), (1, 0)]))  3 us
    pallas_call x1, Pallas kernels, shards(): pl.pallas_call(functools.partial(bulk, z), out_shape=pltpu.VMEM((groups,...  1.82 us
    ppermute x1, starting transfers between devices, shards(): lax.ppermute(prev, 'tm', [(i, (i + 1) % n_tm) for i in range(n_tm)])  1.79 us
    pallas_call x1, Pallas kernels, shards(): pl.pallas_call(functools.partial(tails, z), out_shape=(pltpu.VMEM((groups...  1.68 us
  transfers between devices with their start and end apart: 4, of which 4 were waited for; matrix products, arithmetic and copies ran while one was open for 0% of the time, Pallas kernels for 7%

profile of v8, /device:TPU:0, one launch (start us, length us, event | category | flops | bytes accessed | tf_op | source)
XLA Modules:
  0.0 29.9 jit_solution(11050238179167358834)
XLA Ops:
  0.0 8.8 %channelize.1 = (f32[128,64,128]{2,1,0:T(8,128)S(1)}, f32[128,128]{1,0:T(8,128)S(1)}, f32[4,1,16384]{2,1,0:T(1,128)S(1)}, f32[72,128]{1,0:T(8,128)S(1)}, bf16[46...) custom-call(bf16[1,2097152]{1,0:T(2,128)(2,1)} %raw_ref.1, ...), custom_call_target="tpu_custom_call" | custom-call | tf_op jit(solution)/shard_map/channelize/pallas_call | solution.py:551
  8.8 3.0 %collective-permute-start = (bf16[464,128]{1,0:T(8,128)(2,1)S(1)}, bf16[464,128]{1,0:T(8,128)(2,1)S(1)}, u32[]{:S(2)}, u32[]{:S(2)}) collective-permute-start(bf16[464,128]{1,0:T(8,128)(2,1)S(1)} %get-tuple-element.28.own_ref), channel_id=1, source_target_pairs={{0,2},{2,0},{1,3},{3,1},{4,6},{6,4},{5,7},{7,5},{8,10},{10,8},{9,1... | collective-permute-start | bytes 356360 | tf_op jit(solution)/shard_map/ppermute | solution.py:584
  11.8 0.1 coarse.1.hits_ref
  12.0 3.1 %collective-permute-done.other_ref = bf16[464,128]{1,0:T(8,128)(2,1)S(1)} collective-permute-done((bf16[464,128]{1,0:T(8,128)(2,1)S(1)}, bf16[464,128]{1,0:T(8,128)(2,1)S(1)}, u32[]{:S(2)}, u32[]{:S(2)}) %collective-permute-start) | collective-permute-done | bytes 118816 | tf_op jit(solution)/shard_map/ppermute | solution.py:584
  15.1 1.7 %tails.1 = (bf16[32,128]{1,0:T(8,128)(2,1)S(1)}, f32[2,520,128]{2,1,0:T(8,128)S(1)}, f32[3,64,128]{2,1,0:T(8,128)S(1)}, f32[1,16,128]{2,1,0:T(8,128)S(1)}, f32[72,128]{1,0:T(8,128)S(1)}) custom-call(f32[128,64,128]{2,1,0:T(8,128)S(1)} %get-tuple-element.24.power_ref, f32[128,128]{1,0:T(8,128)S(1)} %get-tuple-element.25.edges_ref, ...), custom_call_target="tpu_custom_call" | custom-call | tf_op jit(solution)/shard_map/tails/pallas_call | solution.py:605
  16.7 1.8 %collective-permute-start.1 = (bf16[32,128]{1,0:T(8,128)(2,1)S(1)}, bf16[32,128]{1,0:T(8,128)(2,1)S(1)}, u32[]{:S(2)}, u32[]{:S(2)}) collective-permute-start(bf16[32,128]{1,0:T(8,128)(2,1)S(1)} %get-tuple-element.35), channel_id=1, source_target_pairs={{0,2},{2,0},{1,3},{3,1},{4,6},{6,4},{5,7},{7,5},{8,10},{10,8},{9,1... | collective-permute-start | bytes 24584 | tf_op jit(solution)/shard_map/ppermute | solution.py:626
  18.5 1.8 %bulk.1.main_ref = f32[8,4,128]{2,1,0:T(4,128)S(1)} custom-call(f32[128,64,128]{2,1,0:T(8,128)S(1)} %get-tuple-element.24.power_ref, f32[128,128]{1,0:T(8,128)S(1)} %get-tuple-element.25.edges_ref, f32[3,64,128]{2,1,0:T(8,128)S(1)} %get-tuple-element.31.bound_ref, f32[1,16,128]{2,1,0:T(8,128)S(1)} %get-tuple-element.32.sides_ref, ...), custom_call_target="tpu_custom_call" | custom-call | flops 1000000000 | bytes 8000000 | tf_op jit(solution)/shard_map/bulk/pallas_call | solution.py:627
  20.4 0.1 collective-permute-done.1.prev_ref
  20.4 0.1 parcels.1
  20.5 2.9 %collective-permute-start.2 = (bf16[2,1,32,128]{3,2,1,0:T(8,128)(2,1)S(1)}, bf16[2,1,32,128]{3,2,1,0:T(8,128)(2,1)S(1)}, u32[]{:S(2)}, u32[]{:S(2)}) collective-permute-start(bf16[2,1,32,128]{3,2,1,0:T(8,128)(2,1)S(1)} %get-tuple-element.38), channel_id=1, source_target_pairs={{0,8},{4,12},{8,0},{12,4},{1,9},{5,13},{9,1},{13,5},{2,10},{6,14},... | collective-permute-start | bytes 49160 | tf_op jit(solution)/shard_map/ppermute | solution.py:654
  23.4 1.8 %collective-permute-done.2.got_ref = bf16[2,1,32,128]{3,2,1,0:T(8,128)(2,1)S(1)} collective-permute-done((bf16[2,1,32,128]{3,2,1,0:T(8,128)(2,1)S(1)}, bf16[2,1,32,128]{3,2,1,0:T(8,128)(2,1)S(1)}, u32[]{:S(2)}, u32[]{:S(2)}) %collective-permute-start.2) | collective-permute-done | bytes 16416 | tf_op jit(solution)/shard_map/ppermute | solution.py:654
  25.2 1.8 %collective-permute-start.3 = (bf16[1,2,32,128]{3,2,1,0:T(8,128)(2,1)S(1)}, bf16[1,2,32,128]{3,2,1,0:T(8,128)(2,1)S(1)}, u32[]{:S(2)}, u32[]{:S(2)}) collective-permute-start(bf16[1,2,32,128]{3,2,1,0:T(8,128)(2,1)S(1)} %get-tuple-element.40), channel_id=1, source_target_pairs={{0,4},{4,0},{8,12},{12,8},{1,5},{5,1},{9,13},{13,9},{2,6},{6,2},{1... | collective-permute-start | bytes 49160 | tf_op jit(solution)/shard_map/ppermute | solution.py:654
  27.0 1.9 %collective-permute-done.3.refs_1_ = bf16[1,2,32,128]{3,2,1,0:T(8,128)(2,1)S(1)} collective-permute-done((bf16[1,2,32,128]{3,2,1,0:T(8,128)(2,1)S(1)}, bf16[1,2,32,128]{3,2,1,0:T(8,128)(2,1)S(1)}, u32[]{:S(2)}, u32[]{:S(2)}) %collective-permute-start.3) | collective-permute-done | bytes 16416 | tf_op jit(solution)/shard_map/ppermute | solution.py:654
  29.0 1.0 %boxes.1 = bf16[4,4,1,4,8,128]{5,4,3,2,1,0:T(8,128)(2,1)} custom-call(s32[8]{0:T(128)S(4)} %get-tuple-element.23.widths_ref, bf16[1,2,32,128]{3,2,1,0:T(8,128)(2,1)S(1)} %get-tuple-element.39.refs_0_, bf16[1,2,32,128]{3,2,1,0:T(8,128)(2,1)S(1)} %collective-permute-done.3.refs_1_), custom_call_target="tpu_custom_call" | custom-call | tf_op jit(solution)/shard_map/boxes/pallas_call | solution.py:666
  (1 shorter events, 0.0 us)
Async XLA Ops:
  8.8 6.2 %collective-permute-start = (bf16[464,128]{1,0:T(8,128)(2,1)S(1)}, bf16[464,128]{1,0:T(8,128)(2,1)S(1)}, u32[]{:S(2)}, u32[]{:S(2)}) collective-permute-start(bf16[464,128]{1,0:T(8,128)(2,1)S(1)} %get-tuple-element.28.own_ref), channel_id=1, source_target_pairs={{0,2},{2,0},{1,3},{3,1},{4,6},{6,4},{5,7},{7,5},{8,10},{10,8},{9,1... | collective-permute-start | bytes 356360 | tf_op jit(solution)/shard_map/ppermute | solution.py:584
  16.7 3.7 %collective-permute-start.1 = (bf16[32,128]{1,0:T(8,128)(2,1)S(1)}, bf16[32,128]{1,0:T(8,128)(2,1)S(1)}, u32[]{:S(2)}, u32[]{:S(2)}) collective-permute-start(bf16[32,128]{1,0:T(8,128)(2,1)S(1)} %get-tuple-element.35), channel_id=1, source_target_pairs={{0,2},{2,0},{1,3},{3,1},{4,6},{6,4},{5,7},{7,5},{8,10},{10,8},{9,1... | collective-permute-start | bytes 24584 | tf_op jit(solution)/shard_map/ppermute | solution.py:626
  20.5 4.7 %collective-permute-start.2 = (bf16[2,1,32,128]{3,2,1,0:T(8,128)(2,1)S(1)}, bf16[2,1,32,128]{3,2,1,0:T(8,128)(2,1)S(1)}, u32[]{:S(2)}, u32[]{:S(2)}) collective-permute-start(bf16[2,1,32,128]{3,2,1,0:T(8,128)(2,1)S(1)} %get-tuple-element.38), channel_id=1, source_target_pairs={{0,8},{4,12},{8,0},{12,4},{1,9},{5,13},{9,1},{13,5},{2,10},{6,14},... | collective-permute-start | bytes 49160 | tf_op jit(solution)/shard_map/ppermute | solution.py:654
  25.2 3.7 %collective-permute-start.3 = (bf16[1,2,32,128]{3,2,1,0:T(8,128)(2,1)S(1)}, bf16[1,2,32,128]{3,2,1,0:T(8,128)(2,1)S(1)}, u32[]{:S(2)}, u32[]{:S(2)}) collective-permute-start(bf16[1,2,32,128]{3,2,1,0:T(8,128)(2,1)S(1)} %get-tuple-element.40), channel_id=1, source_target_pairs={{0,4},{4,0},{8,12},{12,8},{1,5},{5,1},{9,13},{13,9},{2,6},{6,2},{1... | collective-permute-start | bytes 49160 | tf_op jit(solution)/shard_map/ppermute | solution.py:654

commit v9 on v8

--- a/solution.py
+++ b/solution.py
@@ -17,6 +17,7 @@
 WMAX = 8
 LANES = 128
 CHUNK = 16
+SIDE = 4
 LIMIT = 32 * 1024 * 1024
 
 
@@ -138,8 +139,8 @@
     part = count // len(t_refs)
     out = []
     for index, t_ref in enumerate(t_refs):
-        for at in range(0, part, 2):
-            pair = min(2, part - at)
+        for at in range(0, part, SIDE):
+            pair = min(SIDE, part - at)
             lane = (index * part + at) * LANES
             a = jnp.dot(
                 table(z, tab_ref, "first"), y_ref[:, lane : lane + pair * LANES], preferred_element_type=jnp.float32
@@ -384,13 +385,13 @@
             flat = power_of(i, k) * inv_ref[: z.rows] - mean_ref[pl.ds(i * CHUNK + k, 1)]
             edge = jnp.where(place == k, edges, 0.0)
             flats.append(jnp.concatenate([flat, edge]).astype(jnp.bfloat16))
-            if k % 2 == 0:
+            if (k + 1) % SIDE:
                 continue
             masks = table(z, tab_ref, "masks")[:, : z.deep]
-            found = jnp.dot(masks, jnp.concatenate(flats[-2:], 1), preferred_element_type=jnp.float32)
-            for half in range(2):
+            found = jnp.dot(masks, jnp.concatenate(flats[-SIDE:], 1), preferred_element_type=jnp.float32)
+            for half in range(SIDE):
                 value = found[:, half * LANES : (half + 1) * LANES]
-                at = pl.multiple_of(((i - first) * CHUNK + k - 1 + half) * groups, 8)
+                at = pl.multiple_of(((i - first) * CHUNK + k + 1 - SIDE + half) * groups, 8)
                 for m in range(2):
                     parts = [picked(m, step, value) for step in range(FD)]
                     sub_ref[m, pl.ds(at, groups)] = plus(open_sums[m][0], parts[0])

time: 30.1 us -> 30.1 us (level)
  no operation moved by 1% of the time
where the time goes in v9:
time: 30.1 us; the launch traced here: 30 us
  Pallas kernels  13.5 us (45%)
  starting transfers between devices  9.51 us (32%)
  waiting for transfers between devices  6.9 us (23%)
    pallas_call x1, Pallas kernels, shards(): pl.pallas_call(functools.partial(channelize, z), out_shape=(pltpu.VMEM((z...  8.84 us
    ppermute x2, starting transfers between devices, shards(): got = lax.ppermute(leaving, 'dm', [(i, i ^ bit) for i in range(n_dm)])  4.72 us
    ppermute x2, waiting for transfers between devices, shards(): got = lax.ppermute(leaving, 'dm', [(i, i ^ bit) for i in range(n_dm)])  3.72 us
    ppermute x1, waiting for transfers between devices, shards(): own, other = (msg, lax.ppermute(msg, 'tm', [(0, 1), (1, 0)]))  3.09 us
    ppermute x1, starting transfers between devices, shards(): own, other = (msg, lax.ppermute(msg, 'tm', [(0, 1), (1, 0)]))  3 us
    pallas_call x1, Pallas kernels, shards(): pl.pallas_call(functools.partial(bulk, z), out_shape=pltpu.VMEM((groups,...  1.82 us
    ppermute x1, starting transfers between devices, shards(): lax.ppermute(prev, 'tm', [(i, (i + 1) % n_tm) for i in range(n_tm)])  1.79 us
    pallas_call x1, Pallas kernels, shards(): pl.pallas_call(functools.partial(tails, z), out_shape=(pltpu.VMEM((groups...  1.67 us
  transfers between devices with their start and end apart: 4, of which 4 were waited for; matrix products, arithmetic and copies ran while one was open for 0% of the time, Pallas kernels for 7%

profile of v9, /device:TPU:0, one launch (start us, length us, event | category | flops | bytes accessed | tf_op | source)
XLA Modules:
  0.0 30.0 jit_solution(6226390213141168952)
XLA Ops:
  0.0 8.8 %channelize.1 = (f32[128,64,128]{2,1,0:T(8,128)S(1)}, f32[128,128]{1,0:T(8,128)S(1)}, f32[4,1,16384]{2,1,0:T(1,128)S(1)}, f32[72,128]{1,0:T(8,128)S(1)}, bf16[46...) custom-call(bf16[1,2097152]{1,0:T(2,128)(2,1)} %raw_ref.1, ...), custom_call_target="tpu_custom_call" | custom-call | tf_op jit(solution)/shard_map/channelize/pallas_call | solution.py:552
  8.8 3.0 %collective-permute-start = (bf16[464,128]{1,0:T(8,128)(2,1)S(1)}, bf16[464,128]{1,0:T(8,128)(2,1)S(1)}, u32[]{:S(2)}, u32[]{:S(2)}) collective-permute-start(bf16[464,128]{1,0:T(8,128)(2,1)S(1)} %get-tuple-element.28.own_ref), channel_id=1, source_target_pairs={{0,2},{2,0},{1,3},{3,1},{4,6},{6,4},{5,7},{7,5},{8,10},{10,8},{9,1... | collective-permute-start | bytes 356360 | tf_op jit(solution)/shard_map/ppermute | solution.py:585
  11.8 0.1 coarse.1.hits_ref
  12.0 3.1 %collective-permute-done.other_ref = bf16[464,128]{1,0:T(8,128)(2,1)S(1)} collective-permute-done((bf16[464,128]{1,0:T(8,128)(2,1)S(1)}, bf16[464,128]{1,0:T(8,128)(2,1)S(1)}, u32[]{:S(2)}, u32[]{:S(2)}) %collective-permute-start) | collective-permute-done | bytes 118816 | tf_op jit(solution)/shard_map/ppermute | solution.py:585
  15.1 1.7 %tails.1 = (bf16[32,128]{1,0:T(8,128)(2,1)S(1)}, f32[2,520,128]{2,1,0:T(8,128)S(1)}, f32[3,64,128]{2,1,0:T(8,128)S(1)}, f32[1,16,128]{2,1,0:T(8,128)S(1)}, f32[72,128]{1,0:T(8,128)S(1)}) custom-call(f32[128,64,128]{2,1,0:T(8,128)S(1)} %get-tuple-element.24.power_ref, f32[128,128]{1,0:T(8,128)S(1)} %get-tuple-element.25.edges_ref, ...), custom_call_target="tpu_custom_call" | custom-call | tf_op jit(solution)/shard_map/tails/pallas_call | solution.py:606
  16.8 1.8 %collective-permute-start.1 = (bf16[32,128]{1,0:T(8,128)(2,1)S(1)}, bf16[32,128]{1,0:T(8,128)(2,1)S(1)}, u32[]{:S(2)}, u32[]{:S(2)}) collective-permute-start(bf16[32,128]{1,0:T(8,128)(2,1)S(1)} %get-tuple-element.35), channel_id=1, source_target_pairs={{0,2},{2,0},{1,3},{3,1},{4,6},{6,4},{5,7},{7,5},{8,10},{10,8},{9,1... | collective-permute-start | bytes 24584 | tf_op jit(solution)/shard_map/ppermute | solution.py:627
  18.5 1.8 %bulk.1.main_ref = f32[8,4,128]{2,1,0:T(4,128)S(1)} custom-call(f32[128,64,128]{2,1,0:T(8,128)S(1)} %get-tuple-element.24.power_ref, f32[128,128]{1,0:T(8,128)S(1)} %get-tuple-element.25.edges_ref, f32[3,64,128]{2,1,0:T(8,128)S(1)} %get-tuple-element.31.bound_ref, f32[1,16,128]{2,1,0:T(8,128)S(1)} %get-tuple-element.32.sides_ref, ...), custom_call_target="tpu_custom_call" | custom-call | flops 1000000000 | bytes 8000000 | tf_op jit(solution)/shard_map/bulk/pallas_call | solution.py:628
  20.4 0.1 collective-permute-done.1.prev_ref
  20.5 0.1 parcels.1
  20.5 2.9 %collective-permute-start.2 = (bf16[2,1,32,128]{3,2,1,0:T(8,128)(2,1)S(1)}, bf16[2,1,32,128]{3,2,1,0:T(8,128)(2,1)S(1)}, u32[]{:S(2)}, u32[]{:S(2)}) collective-permute-start(bf16[2,1,32,128]{3,2,1,0:T(8,128)(2,1)S(1)} %get-tuple-element.38), channel_id=1, source_target_pairs={{0,8},{4,12},{8,0},{12,4},{1,9},{5,13},{9,1},{13,5},{2,10},{6,14},... | collective-permute-start | bytes 49160 | tf_op jit(solution)/shard_map/ppermute | solution.py:655
  23.4 1.8 %collective-permute-done.2.got_ref = bf16[2,1,32,128]{3,2,1,0:T(8,128)(2,1)S(1)} collective-permute-done((bf16[2,1,32,128]{3,2,1,0:T(8,128)(2,1)S(1)}, bf16[2,1,32,128]{3,2,1,0:T(8,128)(2,1)S(1)}, u32[]{:S(2)}, u32[]{:S(2)}) %collective-permute-start.2) | collective-permute-done | bytes 16416 | tf_op jit(solution)/shard_map/ppermute | solution.py:655
  25.2 1.8 %collective-permute-start.3 = (bf16[1,2,32,128]{3,2,1,0:T(8,128)(2,1)S(1)}, bf16[1,2,32,128]{3,2,1,0:T(8,128)(2,1)S(1)}, u32[]{:S(2)}, u32[]{:S(2)}) collective-permute-start(bf16[1,2,32,128]{3,2,1,0:T(8,128)(2,1)S(1)} %get-tuple-element.40), channel_id=1, source_target_pairs={{0,4},{4,0},{8,12},{12,8},{1,5},{5,1},{9,13},{13,9},{2,6},{6,2},{1... | collective-permute-start | bytes 49160 | tf_op jit(solution)/shard_map/ppermute | solution.py:655
  27.0 1.9 %collective-permute-done.3.refs_1_ = bf16[1,2,32,128]{3,2,1,0:T(8,128)(2,1)S(1)} collective-permute-done((bf16[1,2,32,128]{3,2,1,0:T(8,128)(2,1)S(1)}, bf16[1,2,32,128]{3,2,1,0:T(8,128)(2,1)S(1)}, u32[]{:S(2)}, u32[]{:S(2)}) %collective-permute-start.3) | collective-permute-done | bytes 16416 | tf_op jit(solution)/shard_map/ppermute | solution.py:655
  29.0 1.0 %boxes.1 = bf16[4,4,1,4,8,128]{5,4,3,2,1,0:T(8,128)(2,1)} custom-call(s32[8]{0:T(128)S(4)} %get-tuple-element.23.widths_ref, bf16[1,2,32,128]{3,2,1,0:T(8,128)(2,1)S(1)} %get-tuple-element.39.refs_0_, bf16[1,2,32,128]{3,2,1,0:T(8,128)(2,1)S(1)} %collective-permute-done.3.refs_1_), custom_call_target="tpu_custom_call" | custom-call | tf_op jit(solution)/shard_map/boxes/pallas_call | solution.py:667
  (1 shorter events, 0.0 us)
Async XLA Ops:
  8.8 6.2 %collective-permute-start = (bf16[464,128]{1,0:T(8,128)(2,1)S(1)}, bf16[464,128]{1,0:T(8,128)(2,1)S(1)}, u32[]{:S(2)}, u32[]{:S(2)}) collective-permute-start(bf16[464,128]{1,0:T(8,128)(2,1)S(1)} %get-tuple-element.28.own_ref), channel_id=1, source_target_pairs={{0,2},{2,0},{1,3},{3,1},{4,6},{6,4},{5,7},{7,5},{8,10},{10,8},{9,1... | collective-permute-start | bytes 356360 | tf_op jit(solution)/shard_map/ppermute | solution.py:585
  16.8 3.7 %collective-permute-start.1 = (bf16[32,128]{1,0:T(8,128)(2,1)S(1)}, bf16[32,128]{1,0:T(8,128)(2,1)S(1)}, u32[]{:S(2)}, u32[]{:S(2)}) collective-permute-start(bf16[32,128]{1,0:T(8,128)(2,1)S(1)} %get-tuple-element.35), channel_id=1, source_target_pairs={{0,2},{2,0},{1,3},{3,1},{4,6},{6,4},{5,7},{7,5},{8,10},{10,8},{9,1... | collective-permute-start | bytes 24584 | tf_op jit(solution)/shard_map/ppermute | solution.py:627
  20.5 4.7 %collective-permute-start.2 = (bf16[2,1,32,128]{3,2,1,0:T(8,128)(2,1)S(1)}, bf16[2,1,32,128]{3,2,1,0:T(8,128)(2,1)S(1)}, u32[]{:S(2)}, u32[]{:S(2)}) collective-permute-start(bf16[2,1,32,128]{3,2,1,0:T(8,128)(2,1)S(1)} %get-tuple-element.38), channel_id=1, source_target_pairs={{0,8},{4,12},{8,0},{12,4},{1,9},{5,13},{9,1},{13,5},{2,10},{6,14},... | collective-permute-start | bytes 49160 | tf_op jit(solution)/shard_map/ppermute | solution.py:655
  25.2 3.7 %collective-permute-start.3 = (bf16[1,2,32,128]{3,2,1,0:T(8,128)(2,1)S(1)}, bf16[1,2,32,128]{3,2,1,0:T(8,128)(2,1)S(1)}, u32[]{:S(2)}, u32[]{:S(2)}) collective-permute-start(bf16[1,2,32,128]{3,2,1,0:T(8,128)(2,1)S(1)} %get-tuple-element.40), channel_id=1, source_target_pairs={{0,4},{4,0},{8,12},{12,8},{1,5},{5,1},{9,13},{13,9},{2,6},{6,2},{1... | collective-permute-start | bytes 49160 | tf_op jit(solution)/shard_map/ppermute | solution.py:655
